TPU v7x, 32 devices: a whole 2x2x4 slice. The times are simulated.
32 devices in a mesh: dp: 8 (over y, x, core), tensor: 4 (over z).
Axes of the slice: x: 2, y: 2, z: 4, core: 2. Of those that a mesh axis runs over, the one named last changes fastest.
Arguments:
- inputs: bfloat16 [8192, 1536], P(('dp', 'tensor')), may hold values from -6 to 6
- first_gain: bfloat16 [1536], P('dp'), may hold values from 0.5 to 1.5
- query_weight: bfloat16 [1536, 1536], P('dp', 'tensor'), may hold values from -0.15625 to 0.15625
- key_matrix: bfloat16 [1536, 768], P('dp', 'tensor'), may hold values from -0.15625 to 0.15625
- value_matrix: bfloat16 [1536, 768], P('dp', 'tensor'), may hold values from -0.15625 to 0.15625
- output_weight: bfloat16 [1536, 1536], P('tensor', 'dp'), may hold values from -1 to 1
- second_gain: bfloat16 [1536], P('dp'), may hold values from 0.5 to 1.5
- gate_weight: bfloat16 [1536, 4096], P('dp', 'tensor'), may hold values from -0.15625 to 0.15625
- up_weight: bfloat16 [1536, 4096], P('dp', 'tensor'), may hold values from -0.15625 to 0.15625
- down_weight: bfloat16 [4096, 1536], P('tensor', 'dp'), may hold values from -0.09375 to 0.09375
- seq_lengths: int32 [3], replicated, may hold values from 1 to 4096, as said below
- piece_starts: int32 [7], replicated, may hold values from 896 to 7424, as said below
- out_cotangent: bfloat16 [8192, 1536], P(('dp', 'tensor')), may hold values from -6 to 6
Outputs:
- layer_out: bfloat16 [8192, 1536], P(('dp', 'tensor'))
- input_grad: bfloat16 [8192, 1536], P(('dp', 'tensor'))
- first_gain_grad: float32 [1536], P('dp')
- query_grad: float32 [1536, 1536], P('dp', 'tensor')
- key_grad: float32 [1536, 768], P('dp', 'tensor')
- value_grad: float32 [1536, 768], P('dp', 'tensor')
- output_grad: float32 [1536, 1536], P('tensor', 'dp')
- second_gain_grad: float32 [1536], P('dp')
- gate_grad: float32 [1536, 4096], P('dp', 'tensor')
- up_grad: float32 [1536, 4096], P('dp', 'tensor')
- down_grad: float32 [4096, 1536], P('tensor', 'dp')
Inputs may be any that keep to these rules, and one draw needn't show every extreme that they name: `seq_lengths`: the sequences fill all 8192 tokens; the first has exactly 4096 tokens and the last 2048. `piece_starts`: piece p starts at p * 1024 + 1024 // 2 plus an offset of 0 to 768; the first and the last piece take the offset 1024 // 2 - 256 // 2; pieces never intersect and end within the tokens, and may cross ends of sequences.
All inputs are finite; a program needn't handle non-finite values.
Results may differ from a plain program's by a relative error of at most 0.02.
Values may be sent and summed in bfloat16 or wider, within the bound.
No kernel may reach another device: no remote copies, remote signals or barrier semaphores. Data moves between devices by JAX's collectives and lax.ppermute only.
A program may use at most 192 MiB of HBM per device.

v0:
```python
import math

import jax
import jax.numpy as jnp
from jax import lax
from jax.sharding import PartitionSpec as P

HEAD_WIDTH = 96
PIECE = 256
REACH = 4


epsilon = 1e-05
rope_base = 100000.0
negative = -1e30


def shifted(value, axis, steps):
    count = lax.axis_size(axis)
    leading, last = (max(0, -steps), min(count, count - steps))
    return lax.ppermute(value, axis, [(source, source + steps) for source in range(leading, last)])


def shortened(value):

    def short(part):
        return part.astype(jnp.bfloat16) if part.dtype == jnp.float32 else part

    return jax.tree.map(short, value)


def dot_plain(left_side, right_side):
    return jnp.dot(left_side, right_side, preferred_element_type=jnp.float32)


def dot_tail(left_side, right_side):
    return lax.dot_general(
        left_side, right_side, (((1,), (1,)), ((), ())), preferred_element_type=jnp.float32
    )


def dot_head(left_side, right_side):
    return lax.dot_general(
        left_side, right_side, (((0,), (0,)), ((), ())), preferred_element_type=jnp.float32
    )


def token_tables(token_index, seq_lengths, piece_starts):
    ends = jnp.cumsum(seq_lengths)
    after = (token_index[:, None] >= ends[None, :]).astype(jnp.int32)
    segment = jnp.sum(after, axis=1)
    position = token_index - jnp.sum(after * seq_lengths[None, :], axis=1)
    inside = (token_index[:, None] >= piece_starts[None, :]) & (
        token_index[:, None] < piece_starts[None, :] + PIECE
    )
    labels = jnp.arange(piece_starts.shape[0], dtype=jnp.int32)[None, :] + 1
    piece_id = jnp.sum(jnp.where(inside, labels, 0), axis=1) - 1
    return (segment, token_index, piece_id, position)


def rope_tables(position, head_size):
    half_width = head_size // 2
    frequency = rope_base ** (-(2.0 / head_size) * jnp.arange(half_width, dtype=jnp.float32))
    angles = position.astype(jnp.float32)[:, None] * frequency[None, :]
    return (jnp.cos(angles)[:, None, :], jnp.sin(angles)[:, None, :])


def rotate(values, position):
    half_width = values.shape[-1] // 2
    cosine, sine_part = rope_tables(position, values.shape[-1])
    front_half = values[..., :half_width]
    back_half = values[..., half_width:]
    return jnp.concatenate(
        [front_half * cosine - back_half * sine_part, back_half * cosine + front_half * sine_part],
        axis=-1,
    )


def unrotate(gradients, position):
    half_width = gradients.shape[-1] // 2
    cosine, sine_part = rope_tables(position, gradients.shape[-1])
    front_half = gradients[..., :half_width]
    back_half = gradients[..., half_width:]
    return jnp.concatenate(
        [front_half * cosine + back_half * sine_part, back_half * cosine - front_half * sine_part],
        axis=-1,
    )


def rms_forward(row_block, gain):
    scaling = lax.rsqrt(jnp.mean(row_block * row_block, axis=-1, keepdims=True) + epsilon)
    return (row_block * scaling * gain, scaling)


def rms_backward(row_block, scaling, gain, upstream):
    weighted = upstream * gain
    gain_part = jnp.sum(upstream * row_block * scaling, axis=0)
    inner = jnp.mean(weighted * row_block, axis=-1, keepdims=True)
    return (scaling * weighted - row_block * (scaling * scaling * scaling) * inner, gain_part)


def permitted(query_info, key_info):
    same_seq = query_info[0][:, None] == key_info[0][None, :]
    causal = key_info[1][None, :] <= query_info[1][:, None]
    picture = (query_info[2][:, None] == key_info[2][None, :]) & (query_info[2][:, None] >= 0)
    return same_seq & (causal | picture)


def body(
    inputs,
    first_gain,
    query_weight,
    key_matrix,
    value_matrix,
    output_weight,
    second_gain,
    gate_weight,
    up_weight,
    down_weight,
    seq_lengths,
    piece_starts,
    out_cotangent,
):
    data_count = lax.axis_size("dp")
    data_index = lax.axis_index("dp")
    local_rows = inputs.shape[0]
    span = local_rows * lax.axis_size("tensor")
    heads_local = query_weight.shape[1] // HEAD_WIDTH
    kv_local = key_matrix.shape[1] // HEAD_WIDTH
    query_group_width = heads_local // kv_local
    rows_per_block = min(512, span)
    query_blocks = span // rows_per_block
    scaling = 1.0 / math.sqrt(HEAD_WIDTH)

    def fetch_attention():
        return (
            lax.all_gather(first_gain, "dp", axis=0, tiled=True),
            lax.all_gather(query_weight, "dp", axis=0, tiled=True),
            lax.all_gather(key_matrix, "dp", axis=0, tiled=True),
            lax.all_gather(value_matrix, "dp", axis=0, tiled=True),
            lax.all_gather(output_weight, "dp", axis=1, tiled=True),
        )

    def fetch_forward():
        return (
            lax.all_gather(second_gain, "dp", axis=0, tiled=True),
            lax.all_gather(gate_weight, "dp", axis=0, tiled=True),
            lax.all_gather(up_weight, "dp", axis=0, tiled=True),
            lax.all_gather(down_weight, "dp", axis=1, tiled=True),
        )

    def row_gather(row_block):
        return lax.all_gather(row_block, "tensor", axis=0, tiled=True)

    def grad_gather(row_block):
        return lax.all_gather(row_block, "tensor", axis=0, tiled=True)

    def branch_reduce(left_side, right_side):
        return lax.psum_scatter(
            dot_plain(left_side, right_side).astype(jnp.bfloat16),
            "tensor",
            scatter_dimension=0,
            tiled=True,
        ).astype(jnp.float32)

    def norm_reduce(products):
        summed = None
        for gradient, weight in products:
            piece_term = dot_tail(gradient, weight)
            summed = piece_term if summed is None else summed + piece_term
        return lax.psum_scatter(
            summed.astype(jnp.bfloat16), "tensor", scatter_dimension=0, tiled=True
        ).astype(jnp.float32)

    def block_scores(query_block, query_info, key_block, key_info):
        raw_scores = jnp.einsum(
            "qhgd,khd->hgqk", query_block, key_block, preferred_element_type=jnp.float32
        )
        allowed = permitted(query_info, key_info)
        return jnp.where(allowed[None, None], raw_scores * scaling, negative)

    attention_full = fetch_attention()
    gain_one = attention_full[0].astype(jnp.float32)
    stream_rows = inputs.astype(jnp.float32)
    normed_one, scale_one = rms_forward(stream_rows, gain_one)
    first_norm_output = row_gather(normed_one.astype(jnp.bfloat16))
    own_index = data_index * span + jnp.arange(span, dtype=jnp.int32)
    own_seg, own_idx, own_piece, own_pos = token_tables(own_index, seq_lengths, piece_starts)
    q_pre = dot_plain(first_norm_output, attention_full[1]).reshape(span, heads_local, HEAD_WIDTH)
    key_unrotated = dot_plain(first_norm_output, attention_full[2]).reshape(
        span, kv_local, HEAD_WIDTH
    )
    v_pre = dot_plain(first_norm_output, attention_full[3]).reshape(span, kv_local, HEAD_WIDTH)
    query_states = rotate(q_pre, own_pos).astype(jnp.bfloat16)
    keys = rotate(key_unrotated, own_pos).astype(jnp.bfloat16)
    values = v_pre.astype(jnp.bfloat16)
    above = shifted((keys, values), "dp", -1)
    key_list = [keys, above[0]]
    value_list = [values, above[1]]
    sources = [data_index, (data_index + 1) % data_count]
    moving = (keys, values)
    for distance in range(1, REACH + 1):
        moving = shifted((moving[0], moving[1]), "dp", 1)
        key_list.append(moving[0])
        value_list.append(moving[1])
        sources.append((data_index - distance) % data_count)
    block_count = len(key_list)
    key_infos = []
    for source in sources:
        seg_k, idx_k, piece_k, pos_k = token_tables(
            source * span + jnp.arange(span, dtype=jnp.int32), seq_lengths, piece_starts
        )
        key_infos.append((seg_k, idx_k, piece_k))
    query_split = query_states.reshape(
        query_blocks, rows_per_block, kv_local, query_group_width, HEAD_WIDTH
    )
    seg_split = own_seg.reshape(query_blocks, rows_per_block)
    idx_split = own_idx.reshape(query_blocks, rows_per_block)
    piece_split = own_piece.reshape(query_blocks, rows_per_block)

    def forward_block(inputs_block):
        query_block, seg_q, idx_q, piece_q = inputs_block
        query_info = (seg_q, idx_q, piece_q)
        running_max = jnp.full((kv_local, query_group_width, rows_per_block), negative, jnp.float32)
        running_sum = jnp.zeros((kv_local, query_group_width, rows_per_block), jnp.float32)
        for block_id in range(block_count):
            scores = block_scores(query_block, query_info, key_list[block_id], key_infos[block_id])
            new_max = jnp.maximum(running_max, jnp.max(scores, axis=-1))
            running_sum = running_sum * jnp.exp(running_max - new_max) + jnp.sum(
                jnp.exp(scores - new_max[..., None]), axis=-1
            )
            running_max = new_max
        log_total = running_max + jnp.log(running_sum)
        mixed_heads = jnp.zeros(
            (rows_per_block, kv_local, query_group_width, HEAD_WIDTH), jnp.float32
        )
        for block_id in range(block_count):
            scores = block_scores(query_block, query_info, key_list[block_id], key_infos[block_id])
            probabilities = jnp.exp(scores - log_total[..., None]).astype(jnp.bfloat16)
            mixed_heads = mixed_heads + jnp.einsum(
                "hgqk,khd->qhgd",
                probabilities,
                value_list[block_id],
                preferred_element_type=jnp.float32,
            )
        return (mixed_heads, log_total)

    mixed_all, log_totals = lax.map(forward_block, (query_split, seg_split, idx_split, piece_split))
    mixed_float = mixed_all.reshape(span, heads_local * HEAD_WIDTH)
    mixed_low = mixed_float.astype(jnp.bfloat16)
    after_attn = stream_rows + branch_reduce(mixed_low, attention_full[4])
    forward_full = fetch_forward()
    gain_two = forward_full[0].astype(jnp.float32)
    normed_two, scale_two = rms_forward(after_attn, gain_two)
    norm_two = row_gather(normed_two.astype(jnp.bfloat16))
    gate = dot_plain(norm_two, forward_full[1])
    up_part = dot_plain(norm_two, forward_full[2])
    sigmoid_gate = jax.nn.sigmoid(gate)
    silu_gate = gate * sigmoid_gate
    hidden = (silu_gate * up_part).astype(jnp.bfloat16)
    layer_out = (after_attn + branch_reduce(hidden, forward_full[3])).astype(jnp.bfloat16)
    forward_back = fetch_forward()
    attention_back = fetch_attention()
    grad_full = grad_gather(out_cotangent)
    down_part = dot_head(hidden, grad_full)
    d_hidden = dot_tail(grad_full, forward_back[3])
    d_gate = (d_hidden * up_part * sigmoid_gate * (1.0 + gate * (1.0 - sigmoid_gate))).astype(
        jnp.bfloat16
    )
    d_up = (d_hidden * silu_gate).astype(jnp.bfloat16)
    gate_part = dot_head(norm_two, d_gate)
    up_grad_part = dot_head(norm_two, d_up)
    d_norm_two = norm_reduce(((d_gate, forward_back[1]), (d_up, forward_back[2])))
    d_two, gain_two_part = rms_backward(after_attn, scale_two, gain_two, d_norm_two)
    grad_mid = out_cotangent.astype(jnp.float32) + d_two
    grad_mid_full = grad_gather(grad_mid.astype(jnp.bfloat16))
    output_part = dot_head(mixed_low, grad_mid_full)
    d_mixed = dot_tail(grad_mid_full, attention_back[4]).astype(jnp.bfloat16)
    d_mixed_split = d_mixed.reshape(
        query_blocks, rows_per_block, kv_local, query_group_width, HEAD_WIDTH
    )
    delta_rows = jnp.sum(
        d_mixed.astype(jnp.float32).reshape(span, kv_local, query_group_width, HEAD_WIDTH)
        * mixed_float.reshape(span, kv_local, query_group_width, HEAD_WIDTH),
        axis=-1,
    )
    delta_split = jnp.transpose(
        delta_rows.reshape(query_blocks, rows_per_block, kv_local, query_group_width), (0, 2, 3, 1)
    )

    def backward_block(carried, inputs_block):
        key_acc, value_acc = carried
        query_block, d_mixed_block, log_total, delta_block, seg_q, idx_q, piece_q = inputs_block
        query_info = (seg_q, idx_q, piece_q)
        d_query_block = jnp.zeros(
            (rows_per_block, kv_local, query_group_width, HEAD_WIDTH), jnp.float32
        )
        new_keys = []
        new_values = []
        for block_id in range(block_count):
            scores = block_scores(query_block, query_info, key_list[block_id], key_infos[block_id])
            probabilities = jnp.exp(scores - log_total[..., None])
            d_probs = jnp.einsum(
                "qhgd,khd->hgqk",
                d_mixed_block,
                value_list[block_id],
                preferred_element_type=jnp.float32,
            )
            d_scores = (probabilities * (d_probs - delta_block[..., None])).astype(jnp.bfloat16)
            d_query_block = d_query_block + jnp.einsum(
                "hgqk,khd->qhgd", d_scores, key_list[block_id], preferred_element_type=jnp.float32
            )
            new_keys.append(
                key_acc[block_id]
                + jnp.einsum(
                    "hgqk,qhgd->khd", d_scores, query_block, preferred_element_type=jnp.float32
                )
            )
            new_values.append(
                value_acc[block_id]
                + jnp.einsum(
                    "hgqk,qhgd->khd",
                    probabilities.astype(jnp.bfloat16),
                    d_mixed_block,
                    preferred_element_type=jnp.float32,
                )
            )
        return ((jnp.stack(new_keys), jnp.stack(new_values)), d_query_block * scaling)

    empty_acc = jnp.zeros((block_count, span, kv_local, HEAD_WIDTH), jnp.float32)
    (key_acc, value_acc), d_query_all = lax.scan(
        backward_block,
        (empty_acc, empty_acc),
        (query_split, d_mixed_split, log_totals, delta_split, seg_split, idx_split, piece_split),
    )
    key_acc = key_acc * scaling
    from_below = (
        shifted(key_acc[1].astype(jnp.bfloat16), "dp", 1).astype(jnp.float32),
        shifted(value_acc[1].astype(jnp.bfloat16), "dp", 1).astype(jnp.float32),
    )
    returned = (
        jnp.zeros((span, kv_local, HEAD_WIDTH), jnp.float32),
        jnp.zeros((span, kv_local, HEAD_WIDTH), jnp.float32),
    )
    for distance in range(REACH, 0, -1):
        returned = (
            shifted(shortened(returned[0] + key_acc[distance + 1]), "dp", -1),
            shifted((returned[1] + value_acc[distance + 1]).astype(jnp.bfloat16), "dp", -1).astype(
                jnp.float32
            ),
        )
    d_keys_rot = key_acc[0] + from_below[0] + returned[0]
    d_values = value_acc[0] + from_below[1] + returned[1]
    d_q = (
        unrotate(d_query_all.reshape(span, heads_local, HEAD_WIDTH), own_pos)
        .astype(jnp.bfloat16)
        .reshape(span, heads_local * HEAD_WIDTH)
    )
    d_k = unrotate(d_keys_rot, own_pos).astype(jnp.bfloat16).reshape(span, kv_local * HEAD_WIDTH)
    d_v = d_values.astype(jnp.bfloat16).reshape(span, kv_local * HEAD_WIDTH)
    query_part = dot_head(first_norm_output, d_q)
    key_part = dot_head(first_norm_output, d_k)
    value_part = dot_head(first_norm_output, d_v)
    d_norm_one = norm_reduce(
        ((d_q, attention_back[1]), (d_k, attention_back[2]), (d_v, attention_back[3]))
    )
    d_one, gain_one_part = rms_backward(stream_rows, scale_one, gain_one, d_norm_one)
    input_grad = (grad_mid + d_one).astype(jnp.bfloat16)
    every_grad = (
        lax.psum_scatter(gain_one_part, "dp", scatter_dimension=0, tiled=True),
        lax.psum_scatter(query_part, "dp", scatter_dimension=0, tiled=True),
        lax.psum_scatter(key_part, "dp", scatter_dimension=0, tiled=True),
        lax.psum_scatter(value_part, "dp", scatter_dimension=0, tiled=True),
        lax.psum_scatter(output_part, "dp", scatter_dimension=1, tiled=True),
        lax.psum_scatter(gain_two_part, "dp", scatter_dimension=0, tiled=True),
        lax.psum_scatter(gate_part, "dp", scatter_dimension=0, tiled=True),
        lax.psum_scatter(up_grad_part, "dp", scatter_dimension=0, tiled=True),
        lax.psum_scatter(down_part, "dp", scatter_dimension=1, tiled=True),
    )
    attention_grads = every_grad[0:5]
    forward_grads = every_grad[5:9]
    gain_totals = lax.psum((attention_grads[0], forward_grads[0]), "tensor")
    return (
        layer_out,
        input_grad,
        gain_totals[0],
        attention_grads[1],
        attention_grads[2],
        attention_grads[3],
        attention_grads[4],
        gain_totals[1],
        forward_grads[1],
        forward_grads[2],
        forward_grads[3],
    )


def solution(mesh):
    return jax.shard_map(
        body,
        mesh=mesh,
        in_specs=(
            P(("dp", "tensor"), None),
            P("dp"),
            P("dp", "tensor"),
            P("dp", "tensor"),
            P("dp", "tensor"),
            P("tensor", "dp"),
            P("dp"),
            P("dp", "tensor"),
            P("dp", "tensor"),
            P("tensor", "dp"),
            P(),
            P(),
            P(("dp", "tensor"), None),
        ),
        out_specs=(
            P(("dp", "tensor"), None),
            P(("dp", "tensor"), None),
            P("dp"),
            P("dp", "tensor"),
            P("dp", "tensor"),
            P("dp", "tensor"),
            P("tensor", "dp"),
            P("dp"),
            P("dp", "tensor"),
            P("dp", "tensor"),
            P("tensor", "dp"),
        ),
        check_vma=False,
    )
```

profile of v0, /device:TPU:0, one launch (start us, length us, event | category | flops | bytes accessed | tf_op | source)
XLA Modules:
  0.0 1640.8 jit_solution(3753912584356473304)
XLA Ops:
  13.0 16.0 all-reduce.6
  59.7 35.2 %all-gather.10.cloned.1.call-done = bf16[1024,1536]{1,0:T(8,128)(2,1)} async-done(((bf16[256,1536]{1,0:T(8,128)(2,1)}), bf16[1024,1536]{1,0:T(8,128)(2,1)}) %all-gather.10.cloned.1.call-update) | async-done | bytes 3145744 | tf_op jit(solution)/shard_map/all_gather | solution.py:153
  142.3 175.7 %while.28 = (s32[]{:T(128)}, f32[2,512,2,2,96]{1,4,3,2,0:T(8,128)}, f32[2,2,2,512]{3,2,1,0:T(2,128)}, s32[2,512]{1,0:T(2,128)}, s32[1024]{0:T(1024)S(1)}, /*inde...) while((s32[]{:T(128)}, f32[2,512,2,2,96]{1,4,3,2,0:T(8,128)}, ...), condition=%wide.region_28.29_spmd.clone, body=%wide.region_15.28_spmd.clone.sunk | while | flops 4990194176 | bytes 277983360 | solution.py:248
  327.4 73.6 %reduce-scatter.12.cloned.1.call-done = bf16[256,1536]{1,0:T(8,128)(2,1)} async-done(((bf16[1024,1536]{1,0:T(8,128)(2,1)}), bf16[256,1536]{1,0:T(8,128)(2,1)}) %reduce-scatter.12.cloned.1.call-update) | async-done | bytes 786448 | tf_op jit(solution)/shard_map/reduce_scatter | solution.py:159
  407.9 27.2 %all-gather.20.cloned.1.call-done = bf16[1536,1024]{1,0:T(8,128)(2,1)} async-done(((bf16[192,1024]{1,0:T(8,128)(2,1)}), bf16[1536,1024]{1,0:T(8,128)(2,1)}) %all-gather.20.cloned.1.call-update) | async-done | bytes 3145744 | tf_op jit(solution)/shard_map/all_gather | solution.py:148
  435.1 65.5 %all-gather.16.cloned.1.call-done = bf16[1024,1536]{1,0:T(8,128)(2,1)} async-done(((bf16[256,1536]{1,0:T(8,128)(2,1)}), bf16[1024,1536]{1,0:T(8,128)(2,1)}) %all-gather.16.cloned.1.call-update) | async-done | bytes 3145744 | tf_op jit(solution)/shard_map/all_gather | solution.py:153
  508.9 24.6 %all-gather.18.cloned.1.call-done = bf16[1536,1024]{1,0:T(8,128)(2,1)} async-done(((bf16[192,1024]{1,0:T(8,128)(2,1)}), bf16[1536,1024]{1,0:T(8,128)(2,1)}) %all-gather.18.cloned.1.call-update) | async-done | bytes 3145744 | tf_op jit(solution)/shard_map/all_gather | solution.py:147
  541.8 56.9 %all-gather.24.cloned.1.call-done = bf16[1024,1536]{1,0:T(8,128)(2,1)} async-done(((bf16[256,1536]{1,0:T(8,128)(2,1)}), bf16[1024,1536]{1,0:T(8,128)(2,1)}) %all-gather.24.cloned.1.call-update) | async-done | bytes 3145744 | tf_op jit(solution)/shard_map/all_gather | solution.py:156
  598.6 32.9 %all-gather.22.cloned.1.call-done = bf16[1024,1536]{0,1:T(8,128)(2,1)} async-done(((bf16[1024,192]{0,1:T(8,128)(2,1)}), bf16[1024,1536]{0,1:T(8,128)(2,1)}) %all-gather.22.cloned.1.call-update) | async-done | bytes 3145744 | tf_op jit(solution)/shard_map/all_gather | solution.py:149
  651.9 60.4 %reduce-scatter.16.cloned.1.call-done = bf16[256,1536]{1,0:T(8,128)(2,1)} async-done(((bf16[1024,1536]{1,0:T(8,128)(2,1)}), bf16[256,1536]{1,0:T(8,128)(2,1)}) %reduce-scatter.16.cloned.1.call-update) | async-done | bytes 786448 | tf_op jit(solution)/shard_map/reduce_scatter | solution.py:171
  719.7 62.0 %all-gather.26.cloned.1.call-done = bf16[1024,1536]{1,0:T(8,128)(2,1)} async-done(((bf16[256,1536]{1,0:T(8,128)(2,1)}), bf16[1024,1536]{1,0:T(8,128)(2,1)}) %all-gather.26.cloned.1.call-update) | async-done | bytes 3145744 | tf_op jit(solution)/shard_map/all_gather | solution.py:156
  800.4 272.4 %while.29 = (s32[]{:T(128)}, f32[6,1024,2,96]{1,3,2,0:T(8,128)}, f32[6,1024,2,96]{1,3,2,0:T(8,128)}, f32[2,512,2,2,96]{1,0,4,3,2:T(2,128)}, bf16[2,512,2,2,96]{1...) while((s32[]{:T(128)}, f32[6,1024,2,96]{1,3,2,0:T(8,128)}, ...), condition=%wide.region_36.37_spmd.clone, body=%wide.region_35.36_spmd.clone.sunk | while | flops 12227844096 | bytes 467988800 | solution.py:331
  917.5 15.0 dynamic_update_slice.21
  1049.4 15.0 dynamic_update_slice.21
  1179.0 16.6 %reduce-scatter.18.cloned.1.call-done = bf16[256,1536]{1,0:T(8,128)(2,1)} async-done(((bf16[1024,1536]{1,0:T(8,128)(2,1)}), bf16[256,1536]{1,0:T(8,128)(2,1)}) %reduce-scatter.18.cloned.1.call-update) | async-done | bytes 786448 | tf_op jit(solution)/shard_map/reduce_scatter | solution.py:171
  1197.2 24.7 %all-reduce.4 = (f32[1536]{0:T(1024)S(1)}, f32[1536]{0:T(1024)S(1)}) all-reduce(f32[1536]{0:T(1024)S(1)} %get-tuple-element.872, f32[1536]{0:T(1024)S(1)} %copy-done.43), channel_id=6, replica_groups=mesh['dp'=8,'tensor'=4] {'dp'}, use_global_device_ids=true, to_apply=%region_40.41.clone | all-reduce | flops 3072 | bytes 24576
  1234.2 24.2 %reduce-scatter.14.cloned.1.call-done = bf16[256,1536]{1,0:T(8,128)(2,1)} async-done(((bf16[1024,1536]{1,0:T(8,128)(2,1)}), bf16[256,1536]{1,0:T(8,128)(2,1)}) %reduce-scatter.14.cloned.1.call-update) | async-done | bytes 786448 | tf_op jit(solution)/shard_map/reduce_scatter | solution.py:159
  1262.1 61.9 %reduce-scatter.32.cloned.1.call-done = f32[1024,192]{0,1:T(8,128)} async-done(((f32[1024,1536]{0,1:T(8,128)}), f32[1024,192]{0,1:T(8,128)}) %reduce-scatter.32.cloned.1.call-update) | async-done | bytes 786448 | tf_op jit(solution)/shard_map/reduce_scatter | solution.py:378
  1324.0 66.0 %reduce-scatter.30.cloned.1.call-done = f32[192,1024]{1,0:T(8,128)} async-done(((f32[1536,1024]{1,0:T(8,128)}), f32[192,1024]{1,0:T(8,128)}) %reduce-scatter.30.cloned.1.call-update) | async-done | bytes 786448 | tf_op jit(solution)/shard_map/reduce_scatter | solution.py:377
  1390.0 65.6 %reduce-scatter.28.cloned.1.call-done = f32[192,1024]{1,0:T(8,128)} async-done(((f32[1536,1024]{1,0:T(8,128)}), f32[192,1024]{1,0:T(8,128)}) %reduce-scatter.28.cloned.1.call-update) | async-done | bytes 786448 | tf_op jit(solution)/shard_map/reduce_scatter | solution.py:376
  1455.5 42.6 %reduce-scatter.24.cloned.1.call-done = f32[192,192]{1,0:T(8,128)} async-done(((f32[1536,192]{1,0:T(8,128)}), f32[192,192]{1,0:T(8,128)}) %reduce-scatter.24.cloned.1.call-update) | async-done | bytes 147472 | tf_op jit(solution)/shard_map/reduce_scatter | solution.py:373
  1498.1 42.6 %reduce-scatter.22.cloned.1.call-done = f32[192,192]{1,0:T(8,128)} async-done(((f32[1536,192]{1,0:T(8,128)}), f32[192,192]{1,0:T(8,128)}) %reduce-scatter.22.cloned.1.call-update) | async-done | bytes 147472 | tf_op jit(solution)/shard_map/reduce_scatter | solution.py:372
  1540.7 46.8 %reduce-scatter.26.cloned.1.call-done = f32[384,192]{0,1:T(8,128)} async-done(((f32[384,1536]{0,1:T(8,128)}), f32[384,192]{0,1:T(8,128)}) %reduce-scatter.26.cloned.1.call-update) | async-done | bytes 294928 | tf_op jit(solution)/shard_map/reduce_scatter | solution.py:374
  1587.4 46.3 %reduce-scatter.20.cloned.1.call-done = f32[192,384]{1,0:T(8,128)} async-done(((f32[1536,384]{1,0:T(8,128)}), f32[192,384]{1,0:T(8,128)}) %reduce-scatter.20.cloned.1.call-update) | async-done | bytes 294928 | tf_op jit(solution)/shard_map/reduce_scatter | solution.py:371
  (523 shorter events, 671.7 us)
Async XLA Ops:
  7.2 87.7 %all-gather.10.cloned.1.call-start = ((), (), s32[]{:S(2)}) async-start(), calls=%async_computation.11 | async-start | bytes 3932160 | tf_op jit(solution)/shard_map/all_gather | solution.py:153
  31.9 96.4 %all-gather.12.cloned.1.call-start = ((), (), s32[]{:S(2)}) async-start(), calls=%async_computation.12 | async-start | bytes 1327104 | tf_op jit(solution)/shard_map/all_gather | solution.py:138
  32.6 289.0 %all-gather.14.cloned.1.call-start = ((), (), s32[]{:S(2)}) async-start(), calls=%async_computation.13 | async-start | bytes 1327104 | tf_op jit(solution)/shard_map/all_gather | solution.py:141
  33.4 367.6 %reduce-scatter.12.cloned.1.call-start = ((), (), s32[]{:S(2)}) async-start(), calls=%async_computation.14 | async-start | bytes 3932160 | tf_op jit(solution)/shard_map/reduce_scatter | solution.py:159
  116.4 25.9 %collective-permute-start.5 = (bf16[1024,2,96]{0,2,1:T(8,128)(2,1)}, bf16[1024,2,96]{0,2,1:T(8,128)(2,1)}, u32[]{:S(2)}, u32[]{:S(2)}) collective-permute-start(bf16[1024,2,96]{0,2,1:T(8,128)(2,1)} %bitcast.5), channel_id=1, source_target_pairs={{4,0},{8,4},{12,8},{16,12},{20,16},{24,20},{28,24},{5,1},{9,5},{13... | collective-permute-start | bytes 1179656 | tf_op jit(solution)/shard_map/ppermute | solution.py:21
  117.8 24.5 %collective-permute-start = (bf16[1024,2,96]{0,2,1:T(8,128)(2,1)S(1)}, bf16[1024,2,96]{0,2,1:T(8,128)(2,1)S(1)}, u32[]{:S(2)}, u32[]{:S(2)}) collective-permute-start(bf16[1024,2,96]{0,2,1:T(8,128)(2,1)S(1)} %pad_maximum_fusion.2), channel_id=1, source_target_pairs={{4,0},{8,4},{12,8},{16,12},{20,16},{24,20},{28,24},{5,1},{9,5},{13... | collective-permute-start | bytes 1179656 | tf_op jit(solution)/shard_map/ppermute | solution.py:21
  326.8 108.3 %all-gather.20.cloned.1.call-start = ((), (), s32[]{:S(2)}) async-start(), calls=%async_computation.17 | async-start | bytes 3538944 | tf_op jit(solution)/shard_map/all_gather | solution.py:148
  327.3 173.3 %all-gather.16.cloned.1.call-start = ((), (), s32[]{:S(2)}) async-start(), calls=%async_computation.15 | async-start | bytes 3932160 | tf_op jit(solution)/shard_map/all_gather | solution.py:153
  405.4 128.1 %all-gather.18.cloned.1.call-start = ((), (), s32[]{:S(2)}) async-start(), calls=%async_computation.16 | async-start | bytes 3538944 | tf_op jit(solution)/shard_map/all_gather | solution.py:147
  406.2 192.5 %all-gather.24.cloned.1.call-start = ((), (), s32[]{:S(2)}) async-start(), calls=%async_computation.20 | async-start | bytes 3932160 | tf_op jit(solution)/shard_map/all_gather | solution.py:156
  406.9 224.6 %all-gather.22.cloned.1.call-start = ((), (), s32[]{:S(2)}) async-start(), calls=%async_computation.18 | async-start | bytes 3538944 | tf_op jit(solution)/shard_map/all_gather | solution.py:149
  407.6 304.6 %reduce-scatter.16.cloned.1.call-start = ((), (), s32[]{:S(2)}) async-start(), calls=%async_computation.21 | async-start | bytes 3932160 | tf_op jit(solution)/shard_map/reduce_scatter | solution.py:171
  651.9 129.8 %all-gather.26.cloned.1.call-start = ((), (), s32[]{:S(2)}) async-start(), calls=%async_computation.22 | async-start | bytes 3932160 | tf_op jit(solution)/shard_map/all_gather | solution.py:156
  718.0 477.5 %reduce-scatter.18.cloned.1.call-start = ((), (), s32[]{:S(2)}) async-start(), calls=%async_computation.23 | async-start | bytes 3932160 | tf_op jit(solution)/shard_map/reduce_scatter | solution.py:171
  1090.1 31.7 %collective-permute-start.15 = (bf16[1024,2,96]{0,2,1:T(8,128)(2,1)S(1)}, bf16[1024,2,96]{0,2,1:T(8,128)(2,1)S(1)}, u32[]{:S(2)}, u32[]{:S(2)}) collective-permute-start(bf16[1024,2,96]{0,2,1:T(8,128)(2,1)S(1)} %get-tuple-element.1102), channel_id=1, source_target_pairs={{0,4},{4,8},{8,12},{12,16},{16,20},{20,24},{24,28},{1,5},{5,9},{9,... | collective-permute-start | bytes 1179656 | tf_op jit(solution)/shard_map/ppermute | solution.py:21
  1094.5 22.5 %collective-permute-start.10 = (bf16[1024,2,96]{0,2,1:T(8,128)(2,1)S(1)}, bf16[1024,2,96]{0,2,1:T(8,128)(2,1)S(1)}, u32[]{:S(2)}, u32[]{:S(2)}) collective-permute-start(bf16[1024,2,96]{0,2,1:T(8,128)(2,1)S(1)} %get-tuple-element.1104), channel_id=1, source_target_pairs={{0,4},{4,8},{8,12},{12,16},{16,20},{20,24},{24,28},{1,5},{5,9},{9,... | collective-permute-start | bytes 1179656 | tf_op jit(solution)/shard_map/ppermute | solution.py:21
  1128.6 129.7 %reduce-scatter.14.cloned.1.call-start = ((), (), s32[]{:S(2)}) async-start(), calls=%async_computation.19 | async-start | bytes 3932160 | tf_op jit(solution)/shard_map/reduce_scatter | solution.py:159
  1136.5 187.5 %reduce-scatter.32.cloned.1.call-start = ((), (), s32[]{:S(2)}) async-start(), calls=%async_computation.30 | async-start | bytes 7077888 | tf_op jit(solution)/shard_map/reduce_scatter | solution.py:378
  1143.8 246.2 %reduce-scatter.30.cloned.1.call-start = ((), (), s32[]{:S(2)}) async-start(), calls=%async_computation.29 | async-start | bytes 7077888 | tf_op jit(solution)/shard_map/reduce_scatter | solution.py:377
  1152.8 302.8 %reduce-scatter.28.cloned.1.call-start = ((), (), s32[]{:S(2)}) async-start(), calls=%async_computation.28 | async-start | bytes 7077888 | tf_op jit(solution)/shard_map/reduce_scatter | solution.py:376
  1159.9 338.2 %reduce-scatter.24.cloned.1.call-start = ((), (), s32[]{:S(2)}) async-start(), calls=%async_computation.26 | async-start | bytes 1769472 | tf_op jit(solution)/shard_map/reduce_scatter | solution.py:373
  1165.0 375.7 %reduce-scatter.22.cloned.1.call-start = ((), (), s32[]{:S(2)}) async-start(), calls=%async_computation.25 | async-start | bytes 1769472 | tf_op jit(solution)/shard_map/reduce_scatter | solution.py:372
  1167.3 420.1 %reduce-scatter.26.cloned.1.call-start = ((), (), s32[]{:S(2)}) async-start(), calls=%async_computation.27 | async-start | bytes 2654208 | tf_op jit(solution)/shard_map/reduce_scatter | solution.py:374
  1172.9 460.9 %reduce-scatter.20.cloned.1.call-start = ((), (), s32[]{:S(2)}) async-start(), calls=%async_computation.24 | async-start | bytes 2654208 | tf_op jit(solution)/shard_map/reduce_scatter | solution.py:371
  (110 other events, 2170.6 us)
Sparse Core Ops, SparseCore 0:
  32.0 62.8 all-gather.9
  96.8 24.8 all-gather.11
  123.6 27.5 all-gather.13
  326.9 74.0 reduce-scatter.11
  402.7 32.3 all-gather.19
  437.1 63.4 all-gather.15
  502.5 30.9 all-gather.17
  535.1 63.4 all-gather.23
  600.5 30.9 all-gather.21
  652.0 60.2 reduce-scatter.15
  718.2 63.5 all-gather.25
  1128.7 66.8 reduce-scatter.17
  1197.9 60.4 reduce-scatter.13
  1262.1 61.8 reduce-scatter.31
  1328.2 61.7 reduce-scatter.29
  1393.8 61.7 reduce-scatter.27
  1459.6 38.4 reduce-scatter.23
  1502.2 38.4 reduce-scatter.21
  1544.9 42.4 reduce-scatter.25
  1591.2 42.5 reduce-scatter.19
where the time goes:
time: 1650 us; the launch traced here: 1640 us
  waiting for transfers between devices  871 us (53%)
  matrix products  402 us (24%)
  other arithmetic  109 us (7%)
  local copies, waits for them, and re-layouts  84.9 us (5%)
  blocking collectives  72.6 us (4%)
  starting transfers between devices  54.1 us (3%)
  loops' own time  30.6 us (2%)
  between operations  17.2 us (1%)
    all_gather x2, waiting for transfers between devices, grad_gather(): return lax.all_gather(row_block, 'tensor', axis=0, tiled=True)  119 us
    all_gather x2, waiting for transfers between devices, row_gather(): return lax.all_gather(row_block, 'tensor', axis=0, tiled=True)  101 us
    reduce_scatter x2, waiting for transfers between devices, branch_reduce(): lax.psum_scatter(dot_plain(left_side, right_side).astype(jnp.bfloat16), '...  97.7 us
    reduce_scatter x2, waiting for transfers between devices, norm_reduce(): lax.psum_scatter(summed.astype(jnp.bfloat16), 'tensor', scatter_dimension...  76.9 us
    dot_general x24, matrix products, block_scores(): jnp.einsum('qhgd,khd->hgqk', query_block, key_block, preferred_element_ty...  74 us
    reduce_scatter x1, waiting for transfers between devices, body(): lax.psum_scatter(up_grad_part, 'dp', scatter_dimension=0, tiled=True)  66 us
    reduce_scatter x1, waiting for transfers between devices, body(): lax.psum_scatter(gate_part, 'dp', scatter_dimension=0, tiled=True)  65.6 us
    dot_general x12, matrix products, backward_block(): jnp.einsum('hgqk,qhgd->khd', probabilities.astype(jnp.bfloat16), d_mixed_...  64.7 us
  transfers between devices with their start and end apart: 40, of which 23 were waited for; matrix products, arithmetic and copies ran while one was open for 16% of the time, Pallas kernels for 0%

commit v1 on v0

v1 whole, which is shorter than its diff:
```python
import functools
import math

import jax
import jax.numpy as jnp
from jax import lax
from jax.experimental import pallas as pl
from jax.experimental.pallas import tpu as pltpu
from jax.sharding import Mesh, PartitionSpec as P

HEAD = 96
LANES = 128
PIECE = 256
LEN_FIRST = 4096
LEN_LAST = 2048
LEN_MAX = 4096
epsilon = 1e-05
rope_base = 100000.0
negative = -1e30
far_away = 1 << 30
log2_e = 1.4426950408889634
score_scale = 1.0 / math.sqrt(HEAD)
BF = jnp.bfloat16
F32 = jnp.float32
AXES = ("g", "c", "zh", "zl")
MIB = 1024 * 1024


def params(mib):
    return pltpu.CompilerParams(vmem_limit_bytes=mib * MIB)


def nn(left, right):
    return lax.dot_general(left, right, (((1,), (0,)), ((), ())), preferred_element_type=F32)


def nt(left, right):
    return lax.dot_general(left, right, (((1,), (1,)), ((), ())), preferred_element_type=F32)


def tn(left, right):
    return lax.dot_general(left, right, (((0,), (0,)), ((), ())), preferred_element_type=F32)


def flip(value, axis, bit=1):
    count = lax.axis_size(axis)
    return lax.ppermute(value, axis, [(s, s ^ bit) for s in range(count)])


def bits_of(count):
    return [1 << b for b in range(count.bit_length() - 1)]


def lowest(k):
    return k & -k


def highest(k):
    return 1 << (k.bit_length() - 1)


def spread(value):
    count = lax.axis_size("g")
    half = value.shape[0] // 2
    front, back, whole = {0: value[:half]}, {0: value[half:]}, {0: value}
    for k in range(1, count):
        if lowest(k) == k:
            whole[k] = flip(value, "g", k)
            front[k], back[k] = whole[k][:half], whole[k][half:]
    for k in range(1, count):
        if k not in front:
            front[k] = flip(front[k ^ highest(k)], "g", highest(k))
    for k in sorted(range(1, count), key=lowest, reverse=True):
        if k not in back:
            back[k] = flip(back[k ^ lowest(k)], "g", lowest(k))
    pieces = []
    for k in range(count):
        pieces.append(whole[k] if k in whole else jnp.concatenate([front[k], back[k]], 0))
    return pieces


def collect(pieces):
    count = len(pieces)
    half = pieces[0].shape[-2] // 2
    front = [p[..., :half, :].astype(F32) for p in pieces]
    back = [p[..., half:, :].astype(F32) for p in pieces]
    for k in range(count - 1, 0, -1):
        h = highest(k)
        front[k ^ h] = front[k ^ h] + flip(front[k].astype(BF), "g", h).astype(F32)
    for k in sorted(range(1, count), key=lambda k: (lowest(k), k)):
        h = lowest(k)
        back[k ^ h] = back[k ^ h] + flip(back[k].astype(BF), "g", h).astype(F32)
    return jnp.concatenate([front[0], back[0]], -2)


def gather_rows(own):
    beside = flip(own, "zl")
    across = flip(own, "c")
    both = flip(beside, "c")
    return [own, beside, across, both]


def reduce_rows(parts):
    across_both = flip(parts[3].astype(BF), "c")
    across = flip(parts[2].astype(BF), "c")
    beside = flip((parts[1].astype(F32) + across_both.astype(F32)).astype(BF), "zl")
    return parts[0].astype(F32) + across.astype(F32) + beside.astype(F32)


def gather_weights(shard):
    c, zh, g = lax.axis_index("c"), lax.axis_index("zh"), lax.axis_index("g")
    rows, _, width = shard.shape
    keep = lax.dynamic_index_in_dim(shard, c, 1, False)
    give = lax.dynamic_index_in_dim(shard, 1 - c, 1, False)
    got = flip(give, "c")
    pair = jnp.where(c == 0, jnp.concatenate([keep, got], 0), jnp.concatenate([got, keep], 0))
    other = flip(pair, "zh")
    count = lax.axis_size("g")
    full = jnp.zeros((2, count * 2 * rows, width), shard.dtype)
    for block, index in ((pair, zh), (other, 1 - zh)):
        for k, piece in enumerate(spread(block)):
            full = lax.dynamic_update_slice(full, piece[None], (index, (g ^ k) * 2 * rows, 0))
    return full


def scatter_weights(partial):
    c, zh, g = lax.axis_index("c"), lax.axis_index("zh"), lax.axis_index("g")
    count = lax.axis_size("g")
    rows = partial.shape[1] // count
    pieces = [lax.dynamic_slice_in_dim(partial, (g ^ k) * rows, rows, 1) for k in range(count)]
    summed = collect(pieces)
    keep = lax.dynamic_index_in_dim(summed, zh, 0, False)
    give = lax.dynamic_index_in_dim(summed, 1 - zh, 0, False)
    mine = keep + flip(give.astype(BF), "zh").astype(F32)
    half = rows // 2
    own = lax.dynamic_slice_in_dim(mine, c * half, half, 0)
    got = flip(lax.dynamic_slice_in_dim(mine, (1 - c) * half, half, 0).astype(BF), "c").astype(F32)
    return jnp.where(c == 0, jnp.stack([own, got], 1), jnp.stack([got, own], 1))


def add_everywhere(value):
    for axis in AXES:
        for bit in bits_of(lax.axis_size(axis)):
            value = value + flip(value, axis, bit)
    return value


def swap_halves(value):
    width = value.shape[1]
    lane = lax.broadcasted_iota(jnp.int32, value.shape, 1)
    front = lax.rem(lane, HEAD) < HEAD // 2
    return jnp.where(front, pltpu.roll(value, width - HEAD // 2, 1), pltpu.roll(value, HEAD // 2, 1))


def widen(value):
    pad = jnp.zeros((value.shape[0], LANES - HEAD), value.dtype)
    return jnp.concatenate([value, pad], 1)


def qkv_kernel(x_ref, gain_ref, weight_ref, cos_ref, sin_ref, norm_ref, query_ref, kv_ref):
    x = x_ref[0].astype(F32)
    r = lax.rsqrt(jnp.mean(x * x, axis=-1, keepdims=True) + epsilon)
    normed = (x * r * gain_ref[...]).astype(BF)
    norm_ref[0] = normed
    packs = []
    for j in range(2):
        pre = nn(normed, weight_ref[j])
        turned = pre * cos_ref[0] + swap_halves(pre) * sin_ref[0]
        query_ref[j, 0, 0:PIECE] = widen(turned[:, 0:HEAD]).astype(BF)
        query_ref[j, 0, PIECE : 2 * PIECE] = widen(turned[:, HEAD : 2 * HEAD]).astype(BF)
        packs.append(turned[:, 2 * HEAD :])
    kv_ref[...] = jnp.concatenate(packs, 1).astype(BF)


def project_qkv(x_rows, gain, weights, cos_table, sin_table):
    count, rows, width = x_rows.shape
    return pl.pallas_call(
        qkv_kernel,
        grid=(count,),
        in_specs=[
            pl.BlockSpec((1, rows, width), lambda i: (i, 0, 0)),
            pl.BlockSpec((1, width), lambda i: (0, 0)),
            pl.BlockSpec((2, width, 4 * HEAD), lambda i: (0, 0, 0)),
            pl.BlockSpec((1, rows, 4 * HEAD), lambda i: (i, 0, 0)),
            pl.BlockSpec((1, rows, 4 * HEAD), lambda i: (i, 0, 0)),
        ],
        out_specs=[
            pl.BlockSpec((1, rows, width), lambda i: (i, 0, 0)),
            pl.BlockSpec((2, 1, 2 * rows, LANES), lambda i: (0, i, 0, 0)),
            pl.BlockSpec((rows, 4 * HEAD), lambda i: (i, 0)),
        ],
        out_shape=[
            jax.ShapeDtypeStruct((count, rows, width), BF),
            jax.ShapeDtypeStruct((2, count, 2 * rows, LANES), BF),
            jax.ShapeDtypeStruct((count * rows, 4 * HEAD), BF),
        ],
        compiler_params=params(40),
        name="project_qkv",
    )(x_rows, gain, weights, cos_table, sin_table)


def qkv_back_kernel(dq_ref, dkv_ref, weight_ref, cos_ref, sin_ref, grad_ref, share_ref):
    total = None
    for j in range(2):
        packed = jnp.concatenate(
            [
                dq_ref[j, 0, 0:PIECE][:, 0:HEAD],
                dq_ref[j, 0, PIECE : 2 * PIECE][:, 0:HEAD],
                dkv_ref[...][:, 2 * HEAD * j : 2 * HEAD * (j + 1)],
            ],
            1,
        )
        turned = (packed * cos_ref[0] - swap_halves(packed) * sin_ref[0]).astype(BF)
        grad_ref[j, 0] = turned
        term = nt(turned, weight_ref[j])
        total = term if total is None else total + term
    share_ref[0] = total.astype(BF)


def project_back(d_query, d_kv, weights, cos_table, sin_table):
    _, count, _, _ = d_query.shape
    rows = PIECE
    width = weights.shape[1]
    return pl.pallas_call(
        qkv_back_kernel,
        grid=(count,),
        in_specs=[
            pl.BlockSpec((2, 1, 2 * rows, LANES), lambda i: (0, i, 0, 0)),
            pl.BlockSpec((rows, 4 * HEAD), lambda i: (i, 0)),
            pl.BlockSpec((2, width, 4 * HEAD), lambda i: (0, 0, 0)),
            pl.BlockSpec((1, rows, 4 * HEAD), lambda i: (i, 0, 0)),
            pl.BlockSpec((1, rows, 4 * HEAD), lambda i: (i, 0, 0)),
        ],
        out_specs=[
            pl.BlockSpec((2, 1, rows, 4 * HEAD), lambda i: (0, i, 0, 0)),
            pl.BlockSpec((1, rows, width), lambda i: (i, 0, 0)),
        ],
        out_shape=[
            jax.ShapeDtypeStruct((2, count, rows, 4 * HEAD), BF),
            jax.ShapeDtypeStruct((count, rows, width), BF),
        ],
        compiler_params=params(40),
        name="project_back",
    )(d_query, d_kv, weights, cos_table, sin_table)


CHUNK = 2 * PIECE


def unpack_kv(block_refs, key_scratch, value_scratch):
    lane = lax.broadcasted_iota(jnp.int32, (CHUNK, LANES - HEAD), 1)
    ones = jnp.where(lane < 3, 1.0, 0.0).astype(BF)
    at = 0
    for ref in block_refs:
        for start in range(0, ref.shape[0], CHUNK):
            block = ref[start : start + CHUNK, :]
            for j in range(2):
                k = block[:, 2 * HEAD * j : 2 * HEAD * j + HEAD]
                v = block[:, 2 * HEAD * j + HEAD : 2 * HEAD * (j + 1)]
                key_scratch[j, at : at + CHUNK, :] = jnp.concatenate([k, ones], 1)
                value_scratch[j, at : at + CHUNK, :] = jnp.concatenate([v, ones], 1)
            at += CHUNK


def chunk_state(info_ref, base, i):
    last = base + (CHUNK - 1)
    touched = (base <= info_ref[i, 3]) & (last >= info_ref[i, 0])
    full = (base >= info_ref[i, 1]) & (last <= info_ref[i, 2])
    return touched, full


def forward_kernel(n_blocks, first, last, info_ref, base_ref, zl_ref, *refs):
    refs = list(refs)
    query_ref, low_ref, high_ref = refs[:3]
    block_refs = refs[3 : 3 + n_blocks]
    refs = refs[3 + n_blocks :]
    if not first:
        acc_in, top_in = refs[:2]
        refs = refs[2:]
    if last:
        mixed_ref, kept_ref = refs[:2]
    else:
        acc_out, top_out = refs[:2]
    key_scratch, value_scratch, acc, top = refs[2:]
    i = pl.program_id(0)

    @pl.when(i == 0)
    def _():
        unpack_kv(block_refs, key_scratch, value_scratch)

    for j in range(2):
        if first:
            acc[j] = jnp.zeros((CHUNK, LANES), F32)
            top[j] = jnp.full((CHUNK, LANES), negative, F32)
        else:
            acc[j] = acc_in[j, 0]
            top[j] = top_in[j, 0]
    n_chunks = sum(r.shape[0] for r in block_refs) // CHUNK

    def visit(n, masked):
        rows = pl.ds(pl.multiple_of(n * CHUNK, CHUNK), CHUNK)
        if masked:
            at = lax.broadcasted_iota(jnp.int32, (PIECE, CHUNK), 1)
            token = base_ref[n] + lax.rem(at + zl_ref[0] * PIECE, CHUNK)
            low = jnp.concatenate([low_ref[0]] * (CHUNK // LANES), 1)
            high = jnp.concatenate([high_ref[0]] * (CHUNK // LANES), 1)
            allowed = (token >= low) & (token <= high)
        for j in range(2):
            scores = nt(query_ref[j, 0], key_scratch[j, rows, :])
            if masked:
                scores = jnp.concatenate(
                    [jnp.where(allowed, scores[h * PIECE : (h + 1) * PIECE], negative) for h in range(2)], 0
                )
            old = top[j]
            new = jnp.maximum(old, jnp.max(scores, axis=1, keepdims=True))
            top[j] = new
            probs = jnp.exp2(scores - jnp.concatenate([new] * (CHUNK // LANES), 1)).astype(BF)
            acc[j] = acc[j] * jnp.exp2(old - new) + nn(probs, value_scratch[j, rows, :])

    @pl.loop(0, n_chunks)
    def _(n):
        touched, full = chunk_state(info_ref, base_ref[n], i)

        @pl.when(touched & full)
        def _():
            visit(n, False)

        @pl.when(touched & jnp.logical_not(full))
        def _():
            visit(n, True)

    if last:
        lane = lax.broadcasted_iota(jnp.int32, (CHUNK, LANES), 1)
        for j in range(2):
            total = acc[j][:, HEAD : HEAD + 1]
            out = acc[j] / total
            kept_ref[j, 0] = jnp.where(lane < HEAD, out, top[j] + jnp.log2(total))
            mixed_ref[j, 0] = jnp.concatenate([out[0:PIECE, 0:HEAD], out[PIECE:, 0:HEAD]], 1).astype(BF)
    else:
        for j in range(2):
            acc_out[j, 0] = acc[j]
            top_out[j, 0] = top[j]


def attend(query, low, high, info, bases, zl, blocks, state, last):
    count = query.shape[1]
    n_keys = sum(b.shape[0] for b in blocks)
    per_piece = pl.BlockSpec((2, 1, CHUNK, LANES), lambda i, *_: (0, i, 0, 0))
    bound = pl.BlockSpec((1, PIECE, LANES), lambda i, *_: (i, 0, 0))
    in_specs = [per_piece, bound, bound]
    in_specs += [pl.BlockSpec(b.shape, lambda i, *_: (0, 0)) for b in blocks]
    args = [query, low, high, *blocks]
    if state is not None:
        in_specs += [per_piece, per_piece]
        args += list(state)
    wide = jax.ShapeDtypeStruct((2, count, CHUNK, LANES), F32)
    if last:
        out_shape = [jax.ShapeDtypeStruct((2, count, PIECE, 2 * HEAD), BF), wide]
        out_specs = [pl.BlockSpec((2, 1, PIECE, 2 * HEAD), lambda i, *_: (0, i, 0, 0)), per_piece]
    else:
        out_shape = [wide, wide]
        out_specs = [per_piece, per_piece]
    return pl.pallas_call(
        functools.partial(forward_kernel, len(blocks), state is None, last),
        grid_spec=pltpu.PrefetchScalarGridSpec(
            num_scalar_prefetch=3,
            grid=(count,),
            in_specs=in_specs,
            out_specs=out_specs,
            scratch_shapes=[
                pltpu.VMEM((2, n_keys, LANES), BF),
                pltpu.VMEM((2, n_keys, LANES), BF),
                pltpu.VMEM((2, CHUNK, LANES), F32),
                pltpu.VMEM((2, CHUNK, LANES), F32),
            ],
        ),
        out_shape=out_shape,
        compiler_params=params(48),
        name="attend",
    )(info, bases, zl, *args)


def split_three(value):
    first = value.astype(BF)
    rest = value - first.astype(F32)
    second = rest.astype(BF)
    third = (rest - second.astype(F32)).astype(BF)
    return first, second, third


def augment(wide, extra):
    lane = lax.broadcasted_iota(jnp.int32, wide.shape, 1)
    a, b, c = (part.astype(F32) for part in split_three(extra))
    out = wide.astype(F32)
    out = jnp.where(lane == HEAD, a, out)
    out = jnp.where(lane == HEAD + 1, b, out)
    out = jnp.where(lane == HEAD + 2, c, out)
    return out.astype(BF)


def backward_kernel(n_blocks, has_dq, info_ref, base_ref, zl_ref, *refs):
    refs = list(refs)
    query_ref, d_mixed_ref, kept_ref, low_ref, high_ref = refs[:5]
    block_refs = refs[5 : 5 + n_blocks]
    refs = refs[5 + n_blocks :]
    if has_dq:
        dq_in = refs.pop(0)
    dq_ref = refs.pop(0)
    out_refs = refs[:n_blocks]
    key_scratch, value_scratch, d_key, d_value, q_aug, o_aug = refs[n_blocks:]
    i = pl.program_id(0)

    @pl.when(i == 0)
    def _():
        unpack_kv(block_refs, key_scratch, value_scratch)
        d_key[...] = jnp.zeros(d_key.shape, F32)
        d_value[...] = jnp.zeros(d_value.shape, F32)

    for j in range(2):
        kept = kept_ref[j, 0]
        grad = d_mixed_ref[j, 0]
        wide = jnp.concatenate([widen(grad[:, 0:HEAD]), widen(grad[:, HEAD:])], 0)
        delta = jnp.sum(wide.astype(F32) * kept, axis=1, keepdims=True)
        q_aug[j] = augment(query_ref[j, 0], -kept[:, HEAD : HEAD + 1])
        o_aug[j] = augment(wide, -delta)
        if has_dq:
            dq_ref[j, 0] = dq_in[j, 0]
        else:
            dq_ref[j, 0] = jnp.zeros((CHUNK, LANES), F32)
    n_chunks = sum(r.shape[0] for r in block_refs) // CHUNK

    def visit(n, masked):
        rows = pl.ds(pl.multiple_of(n * CHUNK, CHUNK), CHUNK)
        if masked:
            at = lax.broadcasted_iota(jnp.int32, (CHUNK, CHUNK), 0)
            token = base_ref[n] + lax.rem(at + zl_ref[0] * PIECE, CHUNK)
            allowed = (token >= low_ref[0, 0:1, :]) & (token <= high_ref[0, 0:1, :])
        for j in range(2):
            keys = key_scratch[j, rows, :]
            probs = jnp.exp2(nt(keys, q_aug[j]))
            if masked:
                probs = jnp.where(allowed, probs, 0.0)
            d_probs = nt(value_scratch[j, rows, :], o_aug[j])
            low_probs = probs.astype(BF)
            d_scores = (probs * d_probs).astype(BF)
            d_value[j, rows, :] += nn(low_probs, o_aug[j])
            d_key[j, rows, :] += nn(d_scores, q_aug[j])
            dq_ref[j, 0] += tn(d_scores, keys)

    @pl.loop(0, n_chunks)
    def _(n):
        touched, full = chunk_state(info_ref, base_ref[n], i)

        @pl.when(touched & full)
        def _():
            visit(n, False)

        @pl.when(touched & jnp.logical_not(full))
        def _():
            visit(n, True)

    @pl.when(i == pl.num_programs(0) - 1)
    def _():
        at = 0
        for ref in out_refs:
            for start in range(0, ref.shape[0], CHUNK):
                parts = []
                for j in range(2):
                    parts.append(d_key[j, at : at + CHUNK, :][:, 0:HEAD])
                    parts.append(d_value[j, at : at + CHUNK, :][:, 0:HEAD])
                ref[start : start + CHUNK, :] = jnp.concatenate(parts, 1).astype(ref.dtype)
                at += CHUNK


def attend_back(query, d_mixed, kept, low, high, info, bases, zl, blocks, d_query, kinds):
    count = query.shape[1]
    n_keys = sum(b.shape[0] for b in blocks)
    per_piece = pl.BlockSpec((2, 1, CHUNK, LANES), lambda i, *_: (0, i, 0, 0))
    grads = pl.BlockSpec((2, 1, PIECE, 2 * HEAD), lambda i, *_: (0, i, 0, 0))
    bound = pl.BlockSpec((1, 8, CHUNK), lambda i, *_: (i, 0, 0))
    whole = [pl.BlockSpec(b.shape, lambda i, *_: (0, 0)) for b in blocks]
    in_specs = [per_piece, grads, per_piece, bound, bound, *whole]
    args = [query, d_mixed, kept, low, high, *blocks]
    if d_query is not None:
        in_specs.append(per_piece)
        args.append(d_query)
    return pl.pallas_call(
        functools.partial(backward_kernel, len(blocks), d_query is not None),
        grid_spec=pltpu.PrefetchScalarGridSpec(
            num_scalar_prefetch=3,
            grid=(count,),
            in_specs=in_specs,
            out_specs=[per_piece, *whole],
            scratch_shapes=[
                pltpu.VMEM((2, n_keys, LANES), BF),
                pltpu.VMEM((2, n_keys, LANES), BF),
                pltpu.VMEM((2, n_keys, LANES), F32),
                pltpu.VMEM((2, n_keys, LANES), F32),
                pltpu.VMEM((2, CHUNK, LANES), BF),
                pltpu.VMEM((2, CHUNK, LANES), BF),
            ],
        ),
        out_shape=[jax.ShapeDtypeStruct((2, count, CHUNK, LANES), F32)]
        + [jax.ShapeDtypeStruct(b.shape, k) for b, k in zip(blocks, kinds)],
        compiler_params=params(56),
        name="attend_back",
    )(info, bases, zl, *args)


def ffn_kernel(norm_ref, grad_ref, gate_ref, up_ref, down_ref, out_ref, back_ref, hidden_ref, dg_ref, du_ref, acc_out, acc_back):
    step = pl.program_id(0)
    rows = norm_ref[...].reshape(-1, norm_ref.shape[-1])
    grad = grad_ref[...].reshape(-1, grad_ref.shape[-1])
    gate_w, up_w, down_w = gate_ref[0], up_ref[0], down_ref[0]
    gate = nn(rows, gate_w)
    up = nn(rows, up_w)
    d_hidden = nn(grad, down_w)
    sig = jax.nn.sigmoid(gate)
    silu = gate * sig
    hidden = (silu * up).astype(BF)
    d_gate = (d_hidden * up * sig * (1.0 + gate * (1.0 - sig))).astype(BF)
    d_up = (d_hidden * silu).astype(BF)
    hidden_ref[0] = hidden
    dg_ref[0] = d_gate
    du_ref[0] = d_up
    out = nt(hidden, down_w)
    back = nt(d_gate, gate_w) + nt(d_up, up_w)

    @pl.when(step == 0)
    def _():
        acc_out[...] = out
        acc_back[...] = back

    @pl.when(step > 0)
    def _():
        acc_out[...] += out
        acc_back[...] += back

    @pl.when(step == pl.num_programs(0) - 1)
    def _():
        out_ref[...] = acc_out[...].astype(BF).reshape(out_ref.shape)
        back_ref[...] = acc_back[...].astype(BF).reshape(back_ref.shape)


def feed_forward(norm_rows, grad_rows, weights):
    count, rows, width = norm_rows.shape
    half = weights.shape[2] // 3
    tile = 256
    tiles = half // tile
    whole = pl.BlockSpec((count, rows, width), lambda s: (0, 0, 0))

    def weight_spec(which):
        return pl.BlockSpec((1, width, tile), lambda s: (s // tiles, 0, which * tiles + s % tiles))

    hid = pl.BlockSpec((1, count * rows, tile), lambda s: (s // tiles, 0, s % tiles))
    return pl.pallas_call(
        ffn_kernel,
        grid=(2 * tiles,),
        in_specs=[whole, whole, weight_spec(0), weight_spec(1), weight_spec(2)],
        out_specs=[whole, whole, hid, hid, hid],
        out_shape=[jax.ShapeDtypeStruct((count, rows, width), BF)] * 2
        + [jax.ShapeDtypeStruct((2, count * rows, half), BF)] * 3,
        scratch_shapes=[pltpu.VMEM((count * rows, width), F32)] * 2,
        compiler_params=params(56),
        name="feed_forward",
    )(norm_rows, grad_rows, weights, weights, weights)


def rms_backward(rows, scaling, gain, upstream):
    weighted = upstream * gain
    gain_part = jnp.sum(upstream * rows * scaling, axis=0)
    inner = jnp.mean(weighted * rows, axis=-1, keepdims=True)
    return scaling * weighted - rows * (scaling * scaling * scaling) * inner, gain_part


def rms_scale(rows):
    return lax.rsqrt(jnp.mean(rows * rows, axis=-1, keepdims=True) + epsilon)


def token_tables(token, seq_lengths, piece_starts):
    n = seq_lengths.shape[0]
    upto = jnp.arange(n)[None, :] <= jnp.arange(n)[:, None]
    ends = jnp.sum(jnp.where(upto, seq_lengths[None, :], 0), axis=1)
    after = token[:, None] >= ends[None, :]
    start = jnp.sum(jnp.where(after, seq_lengths[None, :], 0), axis=1)
    end = jnp.min(jnp.where(after, far_away, ends[None, :]), axis=1)
    inside = (token[:, None] >= piece_starts[None, :]) & (token[:, None] < piece_starts[None, :] + PIECE)
    piece_end = jnp.max(jnp.where(inside, piece_starts[None, :] + PIECE, 0), axis=1)
    high = jnp.maximum(token, jnp.minimum(piece_end, end) - 1)
    return start, high


def may_meet(one, two, group_tokens, count):
    total = group_tokens * count
    regions = ((0, LEN_FIRST, LEN_FIRST), (LEN_FIRST, total - LEN_LAST, LEN_MAX), (total - LEN_LAST, total, LEN_LAST))
    for start, end, longest in regions:
        both = all(g * group_tokens < end and (g + 1) * group_tokens > start for g in (one, two))
        if both and (abs(one - two) - 1) * group_tokens + 1 < longest:
            return True
    return False


def body(
    inputs,
    first_gain,
    query_weight,
    key_matrix,
    value_matrix,
    output_weight,
    second_gain,
    gate_weight,
    up_weight,
    down_weight,
    seq_lengths,
    piece_starts,
    out_cotangent,
):
    g, c, zh, zl = (lax.axis_index(a) for a in AXES)
    groups = lax.axis_size("g")
    rows, width = inputs.shape
    span = 4 * rows
    group_tokens = 2 * span
    shard_rows = query_weight.shape[0]

    def halves(matrix):
        return matrix.reshape(matrix.shape[0], 2, -1)

    spare = jnp.zeros((shard_rows, 2, 62), BF)
    gains = jnp.stack([first_gain, second_gain], 1)
    gains = jnp.broadcast_to(gains[:, None, :], (shard_rows, 2, 2))
    attn_shard = jnp.concatenate(
        [
            halves(query_weight),
            halves(key_matrix),
            halves(value_matrix),
            halves(output_weight.T),
            gains,
            spare,
        ],
        2,
    )
    ffn_shard = jnp.concatenate([halves(gate_weight), halves(up_weight), halves(down_weight.T)], 2)
    x_pieces = gather_rows(inputs)
    attn_w = gather_weights(attn_shard)
    gain_one = attn_w[0, :, 6 * HEAD].astype(F32)[None, :]
    gain_two = attn_w[0, :, 6 * HEAD + 1].astype(F32)[None, :]

    order = jnp.arange(4)
    piece_base = (2 * g + (c ^ (order >> 1))) * span + zh * CHUNK + (zl ^ (order & 1)) * rows
    token = (piece_base[:, None] + jnp.arange(rows)[None, :]).reshape(-1).astype(jnp.int32)
    low, high = token_tables(token, seq_lengths, piece_starts)
    position = (token - low).astype(F32)
    low, high = low.reshape(4, rows), high.reshape(4, rows)
    info = jnp.stack([low.min(1), low.max(1), high.min(1), high.max(1)], 1).astype(jnp.int32)
    low_wide = jnp.broadcast_to(low[:, :, None], (4, rows, LANES)).astype(jnp.int32)
    high_wide = jnp.broadcast_to(high[:, :, None], (4, rows, LANES)).astype(jnp.int32)
    low_rows = jnp.broadcast_to(jnp.tile(low, (1, 2))[:, None, :], (4, 8, CHUNK)).astype(jnp.int32)
    high_rows = jnp.broadcast_to(jnp.tile(high, (1, 2))[:, None, :], (4, 8, CHUNK)).astype(jnp.int32)
    zl_info = jnp.reshape(zl, (1,)).astype(jnp.int32)
    frequency = rope_base ** (-(2.0 / HEAD) * jnp.arange(HEAD // 2, dtype=F32))
    angles = position[:, None] * frequency[None, :]
    cosine, sine = jnp.cos(angles), jnp.sin(angles)
    cos_head = jnp.concatenate([cosine, cosine], 1)
    sin_head = jnp.concatenate([-sine, sine], 1)

    def table(part, q_scale, k_scale, rest):
        wide = jnp.concatenate([part * q_scale, part * q_scale, part * k_scale, jnp.full(part.shape, rest, F32)], 1)
        return wide.reshape(4, rows, 4 * HEAD)

    into = score_scale * log2_e
    x_rows = jnp.stack(x_pieces)
    norm_one, query, kv = project_qkv(
        x_rows, gain_one, attn_w, table(cos_head, into, 1.0, 1.0), table(sin_head, into, 1.0, 0.0)
    )

    def chunk_bases(group, half):
        return jnp.stack([(2 * group + (c ^ i)) * span + half * CHUNK for i in range(2)])

    def shift_pairs(steps):
        return [(s, s + steps) for s in range(groups) if 0 <= s + steps < groups and may_meet(s, s + steps, group_tokens, groups)]

    def present(pairs, bases):
        target = functools.reduce(jnp.logical_or, [g == t for _, t in pairs])
        return jnp.where(target, bases, far_away)

    near, near_bases = [kv], [chunk_bases(g, zh)]
    kv_other = flip(kv, "zh")
    rest, rest_bases = [kv_other], [chunk_bases(g, 1 - zh)]
    shifts = [d for d in range(1, groups) if shift_pairs(d)]
    for d in shifts:
        near.append(lax.ppermute(kv, "g", shift_pairs(d)))
        near_bases.append(present(shift_pairs(d), chunk_bases(g - d, zh)))
    for d in shifts:
        rest.append(lax.ppermute(kv_other, "g", shift_pairs(d)))
        rest_bases.append(present(shift_pairs(d), chunk_bases(g - d, 1 - zh)))
    above_groups = [s for s in range(1, groups) if may_meet(s - 1, s, group_tokens, groups)]
    if above_groups:
        first_chunk = lax.dynamic_slice_in_dim(kv, c * CHUNK, CHUNK, 0)
        above_pairs = [(2 * s, 2 * (s - 1) + 1) for s in above_groups]
        rest.append(lax.ppermute(first_chunk, ("g", "zh"), above_pairs))
        is_target = functools.reduce(jnp.logical_or, [(g == s - 1) & (zh == 1) for s in above_groups])
        rest_bases.append(jnp.where(is_target, jnp.reshape(2 * (g + 1) * span, (1,)), far_away))
    near_bases = jnp.concatenate(near_bases).astype(jnp.int32)
    rest_bases = jnp.concatenate(rest_bases).astype(jnp.int32)

    state = attend(query, low_wide, high_wide, info, near_bases, zl_info, near, None, False)
    mixed, kept = attend(query, low_wide, high_wide, info, rest_bases, zl_info, rest, state, True)

    out_w = attn_w[:, :, 4 * HEAD : 6 * HEAD]

    def out_projection(k):
        return nt(mixed[0, k], out_w[0]) + nt(mixed[1, k], out_w[1])

    stream = inputs.astype(F32)
    after_attn = stream + reduce_rows([out_projection(k) for k in range(4)])
    scale_two = rms_scale(after_attn)
    norm_two_own = (after_attn * scale_two * gain_two).astype(BF)
    norm_two = gather_rows(norm_two_own)
    cotangents = gather_rows(out_cotangent)
    ffn_w = gather_weights(ffn_shard)

    early = feed_forward(jnp.stack([norm_two[0], norm_two[2]]), jnp.stack([cotangents[0], cotangents[2]]), ffn_w)
    late = feed_forward(jnp.stack([norm_two[1], norm_two[3]]), jnp.stack([cotangents[1], cotangents[3]]), ffn_w)

    def ordered(n):
        return [early[n][0], late[n][0], early[n][1], late[n][1]]

    layer_out = (after_attn + reduce_rows(ordered(0))).astype(BF)
    d_norm_two = reduce_rows(ordered(1))

    def weight_term(left, n):
        first = left[0], left[2]
        second = left[1], left[3]
        return [
            (tn(jnp.concatenate(first, 0), early[n][j]) + tn(jnp.concatenate(second, 0), late[n][j])).astype(BF)
            for j in range(2)
        ]

    gate_part = weight_term(norm_two, 3)
    up_part = weight_term(norm_two, 4)
    down_part = weight_term(cotangents, 2)
    ffn_part = jnp.stack([jnp.concatenate([gate_part[j], up_part[j], down_part[j]], 1) for j in range(2)])
    ffn_grads = scatter_weights(ffn_part)

    d_two, gain_two_part = rms_backward(after_attn, scale_two, gain_two, d_norm_two)
    grad_mid = out_cotangent.astype(F32) + d_two
    grad_mid_rows = jnp.stack(gather_rows(grad_mid.astype(BF)))
    d_mixed = jnp.stack(
        [nn(grad_mid_rows.reshape(span, width), out_w[j]).astype(BF).reshape(4, rows, 2 * HEAD) for j in range(2)]
    )

    back_rest = attend_back(
        query, d_mixed, kept, low_rows, high_rows, info, rest_bases, zl_info, rest, None, [BF] * len(rest)
    )
    d_query, d_rest = back_rest[0], list(back_rest[1:])
    n_far = len(shifts)
    back_near = attend_back(
        query, d_mixed, kept, low_rows, high_rows, info, near_bases, zl_info, near, d_query, [F32] + [BF] * n_far
    )
    d_query, d_kv, d_near = back_near[0], back_near[1], list(back_near[2:])

    def reverse(pairs):
        return [(t, s) for s, t in pairs]

    other_sum = d_rest[0].astype(F32)
    for n, d in enumerate(shifts):
        other_sum = other_sum + lax.ppermute(d_rest[1 + n], "g", reverse(shift_pairs(d))).astype(F32)
        d_kv = d_kv + lax.ppermute(d_near[n], "g", reverse(shift_pairs(d))).astype(F32)
    d_kv = d_kv + flip(other_sum.astype(BF), "zh").astype(F32)
    if above_groups:
        returned = lax.ppermute(d_rest[-1], ("g", "zh"), reverse(above_pairs)).astype(F32)
        at = lax.broadcasted_iota(jnp.int32, (2, 1, 1), 0)
        d_kv = d_kv + jnp.where(at == c, returned[None], 0.0).reshape(d_kv.shape)

    d_qkv, shares = project_back(
        d_query,
        d_kv,
        attn_w,
        table(cos_head, score_scale, 1.0 / log2_e, 1.0),
        table(sin_head, score_scale, 1.0 / log2_e, 0.0),
    )
    d_norm_one = reduce_rows([shares[k] for k in range(4)])
    norm_one_rows = norm_one.reshape(span, width)
    grad_mid_all = grad_mid_rows.reshape(span, width)
    attn_part = jnp.stack(
        [
            jnp.concatenate(
                [
                    tn(norm_one_rows, d_qkv[j].reshape(span, 4 * HEAD)).astype(BF),
                    tn(grad_mid_all, mixed[j].reshape(span, 2 * HEAD)).astype(BF),
                    jnp.zeros((width, 64), BF),
                ],
                1,
            )
            for j in range(2)
        ]
    )
    attn_grads = scatter_weights(attn_part)
    d_one, gain_one_part = rms_backward(stream, rms_scale(stream), gain_one, d_norm_one)
    input_grad = (grad_mid + d_one).astype(BF)
    gain_sums = add_everywhere(jnp.stack([gain_one_part, gain_two_part]))
    gain_shard = lax.dynamic_slice_in_dim(gain_sums, (2 * g + c) * shard_rows, shard_rows, 1)

    def both_halves(part, start, size):
        return part[:, :, start : start + size].reshape(shard_rows, 2 * size)

    half = gate_weight.shape[1] // 2
    return (
        layer_out,
        input_grad,
        gain_shard[0],
        both_halves(attn_grads, 0, 2 * HEAD),
        both_halves(attn_grads, 2 * HEAD, HEAD),
        both_halves(attn_grads, 3 * HEAD, HEAD),
        both_halves(attn_grads, 4 * HEAD, 2 * HEAD).T,
        gain_shard[1],
        both_halves(ffn_grads, 0, half),
        both_halves(ffn_grads, half, half),
        both_halves(ffn_grads, 2 * half, half).T,
    )


def solution(mesh):
    outer, inner = mesh.devices.shape
    fine = Mesh(mesh.devices.reshape(outer // 2, 2, inner // 2, 2), AXES)
    data, tensor = ("g", "c"), ("zh", "zl")
    rows, first = P(AXES, None), P(data)
    wide, tall = P(data, tensor), P(tensor, data)
    return jax.shard_map(
        body,
        mesh=fine,
        in_specs=(rows, first, wide, wide, wide, tall, first, wide, wide, tall, P(), P(), rows),
        out_specs=(rows, rows, first, wide, wide, wide, tall, first, wide, wide, tall),
        check_vma=False,
    )
```

time: 1650 us -> 681 us (0.41)
  waiting for transfers between devices: 871 us -> 302 us
  matrix products: 402 us -> 37.2 us
  Pallas kernels: 0 us -> 103 us
  blocking collectives: 72.6 us -> 0 us
  other arithmetic: 109 us -> 59.9 us
  starting transfers between devices: 54.1 us -> 99.1 us
  loops' own time: 30.6 us -> 0 us
  local copies, waits for them, and re-layouts: 84.9 us -> 66.1 us
    reduce_scatter x11 -> x0, waiting for transfers between devices: 546 us -> none  [the longest x2 97.7 us: branch_reduce(): lax.psum_scatter(dot_plain(left_side, right_side).astype(jnp.bfloat16), '...]
    dot_general x105 -> x26, matrix products: 402 us -> 37.2 us  [the longest x16 27.5 us: tn(): lax.dot_general(left, right, (((0,), (0,)), ((), ())), preferred_element_...]
    all_gather x9 -> x0, waiting for transfers between devices: 304 us -> none  [the longest x2 119 us: grad_gather(): return lax.all_gather(row_block, 'tensor', axis=0, tiled=True)]
    ppermute x20 -> x73, waiting for transfers between devices: 16.3 us -> 302 us  [the longest x67 273 us: flip(): return lax.ppermute(value, axis, [(s, s ^ bit) for s in range(count)])]
    pallas_call x0 -> x8, Pallas kernels: none -> 103 us  [the longest x2 37.5 us: feed_forward(): pl.pallas_call(ffn_kernel, grid=(2 * tiles,), in_specs=[whole, whole, wei...]
    ppermute x20 -> x73, starting transfers between devices: 53.1 us -> 99.1 us  [the longest x67 88.4 us: flip(): return lax.ppermute(value, axis, [(s, s ^ bit) for s in range(count)])]
    reduce_sum x19 -> x5, other arithmetic: 49.1 us -> 3.67 us  [the longest x2 3.22 us: rms_backward(): gain_part = jnp.sum(upstream * rows * scaling, axis=0)]
    unnamed x2 -> x0, blocking collectives: 40.7 us -> none
  transfers between devices with their start and end apart: 40 -> 73, of which waited for: 23 -> 30; matrix products, arithmetic and copies ran while one was open for 16% -> 21% of each run, Pallas kernels for 0% -> 15%
where the time goes in v1:
time: 681 us; the launch traced here: 670 us
  waiting for transfers between devices  302 us (44%)
  Pallas kernels  103 us (15%)
  starting transfers between devices  99.1 us (15%)
  local copies, waits for them, and re-layouts  66.1 us (10%)
  other arithmetic  59.9 us (9%)
  matrix products  37.2 us (5%)
    ppermute x67, waiting for transfers between devices, flip(): return lax.ppermute(value, axis, [(s, s ^ bit) for s in range(count)])  273 us
    ppermute x67, starting transfers between devices, flip(): return lax.ppermute(value, axis, [(s, s ^ bit) for s in range(count)])  88.4 us
    pallas_call x2, Pallas kernels, feed_forward(): pl.pallas_call(ffn_kernel, grid=(2 * tiles,), in_specs=[whole, whole, wei...  37.5 us
    pallas_call x2, Pallas kernels, attend_back(): pl.pallas_call(functools.partial(backward_kernel, len(blocks), d_query is...  32.9 us
    dot_general x16, matrix products, tn(): lax.dot_general(left, right, (((0,), (0,)), ((), ())), preferred_element_...  27.5 us
    unnamed x191, local copies, waits for them, and re-layouts  20 us
    ppermute x1, waiting for transfers between devices, body(): near.append(lax.ppermute(kv, 'g', shift_pairs(d)))  19.1 us
    pallas_call x2, Pallas kernels, attend(): pl.pallas_call(functools.partial(forward_kernel, len(blocks), state is No...  18.5 us
  transfers between devices with their start and end apart: 73, of which 30 were waited for; matrix products, arithmetic and copies ran while one was open for 21% of the time, Pallas kernels for 15%

profile of v1, /device:TPU:0, one launch (start us, length us, event | category | flops | bytes accessed | tf_op | source)
XLA Modules:
  0.0 670.1 jit_solution(5387533182579449252)
XLA Ops:
  46.8 20.6 %collective-permute-done.8 = bf16[384,640]{1,0:T(8,128)(2,1)S(1)} collective-permute-done((bf16[384,640]{1,0:T(8,128)(2,1)S(1)}, bf16[384,640]{1,0:T(8,128)(2,1)S(1)}, u32[]{:S(2)}, u32[]{:S(2)}) %collective-permute-start.8) | collective-permute-done | bytes 491552 | tf_op jit(solution)/shard_map/ppermute | solution.py:47
  76.0 9.0 %collective-permute-done.10 = bf16[384,640]{1,0:T(8,128)(2,1)S(1)} collective-permute-done((bf16[384,640]{1,0:T(8,128)(2,1)S(1)}, bf16[384,640]{1,0:T(8,128)(2,1)S(1)}, u32[]{:S(2)}, u32[]{:S(2)}) %collective-permute-start.10) | collective-permute-done | bytes 491552 | tf_op jit(solution)/shard_map/ppermute | solution.py:47
  121.6 42.8 %collective-permute-done.27 = bf16[384,1536]{1,0:T(8,128)(2,1)S(1)} collective-permute-done((bf16[384,1536]{1,0:T(8,128)(2,1)}, bf16[384,1536]{1,0:T(8,128)(2,1)S(1)}, u32[]{:S(2)}, u32[]{:S(2)}) %collective-permute-start.27) | collective-permute-done | bytes 1179680 | tf_op jit(solution)/shard_map/ppermute | solution.py:47
  168.5 8.8 %collective-permute-done.13.refs_3_.refs_5_ = bf16[1024,384]{1,0:T(8,128)(2,1)S(1)} collective-permute-done((bf16[1024,384]{1,0:T(8,128)(2,1)S(1)}, bf16[1024,384]{1,0:T(8,128)(2,1)S(1)}, u32[]{:S(2)}, u32[]{:S(2)}) %collective-permute-start.13) | collective-permute-done | bytes 786464 | tf_op jit(solution)/shard_map/ppermute | solution.py:47
  186.7 19.1 %collective-permute-done.16.refs_4_.refs_6_ = bf16[1024,384]{1,0:T(8,128)(2,1)S(1)} collective-permute-done((bf16[1024,384]{1,0:T(8,128)(2,1)S(1)}, bf16[1024,384]{1,0:T(8,128)(2,1)S(1)}, u32[]{:S(2)}, u32[]{:S(2)}) %collective-permute-start.16) | collective-permute-done | bytes 786464 | tf_op jit(solution)/shard_map/ppermute | solution.py:691
  206.2 9.2 %attend.2 = (f32[2,4,512,128]{3,2,1,0:T(8,128)S(1)}, f32[2,4,512,128]{3,2,1,0:T(8,128)}) custom-call(s32[4,4]{1,0:T(4,128)S(1)} %pad_add_fusion.info_ref, s32[4]{0:T(128)S(1)} %pad_add_fusion.2.base_ref, s32[1]{0:T(128)} %bitcast.9.zl_ref, bf16[2,4,512,128]{3,2,1,0:T(8,128)(2,1)S(1)} %get-tuple-element.37.refs_0_, ...), custom_call_target="tpu_custom_call" | custom-call | tf_op jit(solution)/shard_map/attend/pallas_call | solution.py:363
  215.5 10.3 %collective-permute-start.31 = (bf16[192,1536]{1,0:T(8,128)(2,1)S(1)}, bf16[192,1536]{1,0:T(8,128)(2,1)}, u32[]{:S(2)}, u32[]{:S(2)}) collective-permute-start(bf16[192,1536]{1,0:T(8,128)(2,1)S(1)} %slice.314), channel_id=1, source_target_pairs={{0,8},{8,0},{16,24},{24,16},{1,9},{9,1},{17,25},{25,17},{2,10},{10... | collective-permute-start | bytes 1769480 | tf_op jit(solution)/shard_map/ppermute | solution.py:47
  227.2 9.3 %attend.3 = (bf16[2,4,256,192]{3,2,1,0:T(8,128)(2,1)S(1)}, f32[2,4,512,128]{3,2,1,0:T(8,128)}) custom-call(s32[4,4]{1,0:T(4,128)S(1)} %pad_add_fusion.info_ref, s32[5]{0:T(128)S(1)} %pad_add_fusion.1.base_ref, s32[1]{0:T(128)} %bitcast.9.zl_ref, bf16[2,4,512,128]{3,2,1,0:T(8,128)(2,1)S(1)} %get-tuple-element.37.refs_0_, ...), custom_call_target="tpu_custom_call" | custom-call | tf_op jit(solution)/shard_map/attend/pallas_call | solution.py:363
  241.7 18.0 %collective-permute-done.19 = bf16[256,1536]{1,0:T(8,128)(2,1)S(1)} collective-permute-done((bf16[256,1536]{1,0:T(8,128)(2,1)S(1)}, bf16[256,1536]{1,0:T(8,128)(2,1)S(1)}, u32[]{:S(2)}, u32[]{:S(2)}) %collective-permute-start.19) | collective-permute-done | bytes 786464 | tf_op jit(solution)/shard_map/ppermute | solution.py:47
  264.8 18.7 %feed_forward.2 = (bf16[2,256,1536]{2,1,0:T(8,128)(2,1)}, bf16[2,256,1536]{2,1,0:T(8,128)(2,1)}, bf16[2,512,512]{2,1,0:T(8,128)(2,1)}, bf16[2,512,512]{2,1,0:T(8,128)(2,1)}, bf16[2,512,512]{2,1,0:T(8,128)(2,1)}) custom-call(bf16[2,256,1536]{2,1,0:T(8,128)(2,1)} %pad_maximum_fusion.2.norm_ref, bf16[2,256,1536]{2,1,0:T(8,128)(2,1)} %pad_maximum_fusion.3.grad_ref, ...), custom_call_target="tpu_custom_call" | custom-call | tf_op jit(solution)/shard_map/feed_forward/pallas_call | solution.py:556
  304.0 18.8 %feed_forward.3 = (bf16[2,256,1536]{2,1,0:T(8,128)(2,1)}, bf16[2,256,1536]{2,1,0:T(8,128)(2,1)}, bf16[2,512,512]{2,1,0:T(8,128)(2,1)}, bf16[2,512,512]{2,1,0:T(8,128)(2,1)}, bf16[2,512,512]{2,1,0:T(8,128)(2,1)}) custom-call(bf16[2,256,1536]{2,1,0:T(8,128)(2,1)} %pad_maximum_fusion.4.norm_ref, bf16[2,256,1536]{2,1,0:T(8,128)(2,1)} %pad_maximum_fusion.5.grad_ref, ...), custom_call_target="tpu_custom_call" | custom-call | tf_op jit(solution)/shard_map/feed_forward/pallas_call | solution.py:556
  353.2 21.7 %collective-permute-done.69 = bf16[2,192,1536]{2,1,0:T(8,128)(2,1)S(1)} collective-permute-done((bf16[2,192,1536]{2,1,0:T(8,128)(2,1)S(1)}, bf16[2,192,1536]{2,1,0:T(8,128)(2,1)S(1)}, u32[]{:S(2)}, u32[]{:S(2)}) %collective-permute-start.69) | collective-permute-done | bytes 1179680 | tf_op jit(solution)/shard_map/ppermute | solution.py:47
  382.4 13.0 %collective-permute-done.41 = bf16[256,1536]{1,0:T(8,128)(2,1)S(1)} collective-permute-done((bf16[256,1536]{1,0:T(8,128)(2,1)S(1)}, bf16[256,1536]{1,0:T(8,128)(2,1)S(1)}, u32[]{:S(2)}, u32[]{:S(2)}) %collective-permute-start.41) | collective-permute-done | bytes 786464 | tf_op jit(solution)/shard_map/ppermute | solution.py:47
  399.8 11.0 %collective-permute-done.38 = bf16[256,1536]{1,0:T(8,128)(2,1)S(1)} collective-permute-done((bf16[256,1536]{1,0:T(8,128)(2,1)S(1)}, bf16[256,1536]{1,0:T(8,128)(2,1)S(1)}, u32[]{:S(2)}, u32[]{:S(2)}) %collective-permute-start.38) | collective-permute-done | bytes 786464 | tf_op jit(solution)/shard_map/ppermute | solution.py:47
  421.1 12.2 %collective-permute-done.42 = bf16[256,1536]{1,0:T(8,128)(2,1)} collective-permute-done((bf16[256,1536]{1,0:T(8,128)(2,1)}, bf16[256,1536]{1,0:T(8,128)(2,1)}, u32[]{:S(2)}, u32[]{:S(2)}) %collective-permute-start.42) | collective-permute-done | bytes 786464 | tf_op jit(solution)/shard_map/ppermute | solution.py:47
  458.9 13.2 %attend_back.2 = (f32[2,4,512,128]{3,2,1,0:T(8,128)}, bf16[1024,384]{1,0:T(8,128)(2,1)}, bf16[1024,384]{1,0:T(8,128)(2,1)}, bf16[512,384]{1,0:T(8,128)(2,1)}) custom-call(s32[4,4]{1,0:T(4,128)} %copy-done.11, s32[5]{0:T(128)} %copy-done.12, s32[1]{0:T(128)} %bitcast.9.zl_ref, bf16[2,4,512,128]{3,2,1,0:T(8,128)(2,1)} %copy-done, ...), custom_call_target="tpu_custom_call" | custom-call | tf_op jit(solution)/shard_map/attend_back/pallas_call | solution.py:487
  474.3 19.7 %attend_back.3 = (f32[2,4,512,128]{3,2,1,0:T(8,128)}, f32[1024,384]{1,0:T(8,128)}, bf16[1024,384]{1,0:T(8,128)(2,1)}) custom-call(s32[4,4]{1,0:T(4,128)} %copy-done.11, s32[4]{0:T(128)} %copy-done.13, s32[1]{0:T(128)} %bitcast.9.zl_ref, bf16[2,4,512,128]{3,2,1,0:T(8,128)(2,1)} %copy-done, bf16[2,4,256,192]{3,2,1,0:T(8,128)(2,1)} %pad_maximum_fusion.9.refs_1_, ...), custom_call_target="tpu_custom_call" | custom-call | tf_op jit(solution)/shard_map/attend_back/pallas_call | solution.py:487
  503.5 25.6 %collective-permute-start.47 = (bf16[1024,384]{1,0:T(8,128)(2,1)S(1)}, bf16[1024,384]{1,0:T(8,128)(2,1)S(1)}, u32[]{:S(2)}, u32[]{:S(2)}) collective-permute-start(bf16[1024,384]{1,0:T(8,128)(2,1)S(1)} %add_convert_fusion.2), channel_id=1, source_target_pairs={{0,2},{2,0},{1,3},{3,1},{4,6},{6,4},{5,7},{7,5},{8,10},{10,8},{9,1... | collective-permute-start | bytes 2359304 | tf_op jit(solution)/shard_map/ppermute | solution.py:47
  537.0 37.5 %collective-permute-done.47 = bf16[1024,384]{1,0:T(8,128)(2,1)S(1)} collective-permute-done((bf16[1024,384]{1,0:T(8,128)(2,1)S(1)}, bf16[1024,384]{1,0:T(8,128)(2,1)S(1)}, u32[]{:S(2)}, u32[]{:S(2)}) %collective-permute-start.47) | collective-permute-done | bytes 786464 | tf_op jit(solution)/shard_map/ppermute | solution.py:47
  592.9 11.4 %collective-permute-done.61 = bf16[2,192,640]{2,1,0:T(8,128)(2,1)S(1)} collective-permute-done((bf16[2,192,640]{2,1,0:T(8,128)(2,1)S(1)}, bf16[2,192,640]{2,1,0:T(8,128)(2,1)S(1)}, u32[]{:S(2)}, u32[]{:S(2)}) %collective-permute-start.61) | collective-permute-done | bytes 491552 | tf_op jit(solution)/shard_map/ppermute | solution.py:47
  607.0 7.8 %collective-permute-done.60 = bf16[2,192,640]{2,1,0:T(8,128)(2,1)S(1)} collective-permute-done((bf16[2,192,640]{2,1,0:T(8,128)(2,1)S(1)}, bf16[2,192,640]{2,1,0:T(8,128)(2,1)S(1)}, u32[]{:S(2)}, u32[]{:S(2)}) %collective-permute-start.60) | collective-permute-done | bytes 491552 | tf_op jit(solution)/shard_map/ppermute | solution.py:47
  618.5 8.8 %collective-permute-done.62 = bf16[2,192,640]{2,1,0:T(8,128)(2,1)S(1)} collective-permute-done((bf16[2,192,640]{2,1,0:T(8,128)(2,1)S(1)}, bf16[2,192,640]{2,1,0:T(8,128)(2,1)S(1)}, u32[]{:S(2)}, u32[]{:S(2)}) %collective-permute-start.62) | collective-permute-done | bytes 491552 | tf_op jit(solution)/shard_map/ppermute | solution.py:47
  627.8 8.8 %collective-permute-done.51 = bf16[256,1536]{1,0:T(8,128)(2,1)S(1)} collective-permute-done((bf16[256,1536]{1,0:T(8,128)(2,1)S(1)}, bf16[256,1536]{1,0:T(8,128)(2,1)S(1)}, u32[]{:S(2)}, u32[]{:S(2)}) %collective-permute-start.51) | collective-permute-done | bytes 786464 | tf_op jit(solution)/shard_map/ppermute | solution.py:47
  637.6 13.2 %collective-permute-done.63 = bf16[384,640]{1,0:T(8,128)(2,1)S(1)} collective-permute-done((bf16[384,640]{1,0:T(8,128)(2,1)S(1)}, bf16[384,640]{1,0:T(8,128)(2,1)S(1)}, u32[]{:S(2)}, u32[]{:S(2)}) %collective-permute-start.63) | collective-permute-done | bytes 491552 | tf_op jit(solution)/shard_map/ppermute | solution.py:47
  (518 shorter events, 279.0 us)
Async XLA Ops:
  0.7 72.9 %collective-permute-start.35 = (bf16[256,1536]{1,0:T(8,128)(2,1)}, bf16[256,1536]{1,0:T(8,128)(2,1)}, u32[]{:S(2)}, u32[]{:S(2)}) collective-permute-start(bf16[256,1536]{1,0:T(8,128)(2,1)} %param.25), channel_id=1, source_target_pairs={{0,1},{1,0},{2,3},{3,2},{4,5},{5,4},{6,7},{7,6},{8,9},{9,8},{10,11... | collective-permute-start | bytes 2359304 | tf_op jit(solution)/shard_map/ppermute | solution.py:47
  3.8 65.1 %collective-permute-start.21 = (bf16[256,1536]{1,0:T(8,128)(2,1)}, bf16[256,1536]{1,0:T(8,128)(2,1)}, u32[]{:S(2)}, u32[]{:S(2)}) collective-permute-start(bf16[256,1536]{1,0:T(8,128)(2,1)} %param.25), channel_id=1, source_target_pairs={{0,4},{4,0},{1,5},{5,1},{2,6},{6,2},{3,7},{7,3},{8,12},{12,8},{9,1... | collective-permute-start | bytes 2359304 | tf_op jit(solution)/shard_map/ppermute | solution.py:47
  9.3 65.9 %collective-permute-start = (bf16[256,1536]{1,0:T(8,128)(2,1)S(1)}, bf16[256,1536]{1,0:T(8,128)(2,1)}, u32[]{:S(2)}, u32[]{:S(2)}) collective-permute-start(bf16[256,1536]{1,0:T(8,128)(2,1)S(1)} %copy-done.23), channel_id=1, source_target_pairs={{0,1},{1,0},{2,3},{3,2},{4,5},{5,4},{6,7},{7,6},{8,9},{9,8},{10,11... | collective-permute-start | bytes 2359304 | tf_op jit(solution)/shard_map/ppermute | solution.py:47
  95.4 69.0 %collective-permute-start.27 = (bf16[384,1536]{1,0:T(8,128)(2,1)}, bf16[384,1536]{1,0:T(8,128)(2,1)S(1)}, u32[]{:S(2)}, u32[]{:S(2)}) collective-permute-start(bf16[384,1536]{1,0:T(8,128)(2,1)} %maximum_select_fusion.2), channel_id=1, source_target_pairs={{0,2},{2,0},{1,3},{3,1},{4,6},{6,4},{5,7},{7,5},{8,10},{10,8},{9,1... | collective-permute-start | bytes 3538952 | tf_op jit(solution)/shard_map/ppermute | solution.py:47
  107.8 69.4 %collective-permute-start.13 = (bf16[1024,384]{1,0:T(8,128)(2,1)S(1)}, bf16[1024,384]{1,0:T(8,128)(2,1)S(1)}, u32[]{:S(2)}, u32[]{:S(2)}) collective-permute-start(bf16[1024,384]{1,0:T(8,128)(2,1)S(1)} %get-tuple-element.38.refs_3_.refs_5_), channel_id=1, source_target_pairs={{0,2},{2,0},{1,3},{3,1},{4,6},{6,4},{5,7},{7,5},{8,10},{10,8},{9,1... | collective-permute-start | bytes 2359304 | tf_op jit(solution)/shard_map/ppermute | solution.py:47
  120.2 59.4 %collective-permute-start.26 = (bf16[192,1536]{1,0:T(8,128)(2,1)S(1)}, bf16[192,1536]{1,0:T(8,128)(2,1)S(1)}, u32[]{:S(2)}, u32[]{:S(2)}) collective-permute-start(bf16[192,1536]{1,0:T(8,128)(2,1)S(1)} %slice.312), channel_id=1, source_target_pairs={{0,8},{8,0},{16,24},{24,16},{1,9},{9,1},{17,25},{25,17},{2,10},{10... | collective-permute-start | bytes 1769480 | tf_op jit(solution)/shard_map/ppermute | solution.py:47
  120.3 60.0 %collective-permute-start.25 = (bf16[192,1536]{1,0:T(8,128)(2,1)S(1)}, bf16[192,1536]{1,0:T(8,128)(2,1)S(1)}, u32[]{:S(2)}, u32[]{:S(2)}) collective-permute-start(bf16[192,1536]{1,0:T(8,128)(2,1)S(1)} %slice.311), channel_id=1, source_target_pairs={{0,16},{8,24},{16,0},{24,8},{1,17},{9,25},{17,1},{25,9},{2,18},{10... | collective-permute-start | bytes 1769480 | tf_op jit(solution)/shard_map/ppermute | solution.py:47
  164.4 61.4 %collective-permute-start.28 = (bf16[384,1536]{1,0:T(8,128)(2,1)S(1)}, bf16[384,1536]{1,0:T(8,128)(2,1)S(1)}, u32[]{:S(2)}, u32[]{:S(2)}) collective-permute-start(bf16[384,1536]{1,0:T(8,128)(2,1)S(1)} %collective-permute-done.27), channel_id=1, source_target_pairs={{0,8},{8,0},{16,24},{24,16},{1,9},{9,1},{17,25},{25,17},{2,10},{10... | collective-permute-start | bytes 3538952 | tf_op jit(solution)/shard_map/ppermute | solution.py:47
  164.4 51.0 %collective-permute-start.29 = (bf16[384,1536]{1,0:T(8,128)(2,1)S(1)}, bf16[384,1536]{1,0:T(8,128)(2,1)S(1)}, u32[]{:S(2)}, u32[]{:S(2)}) collective-permute-start(bf16[384,1536]{1,0:T(8,128)(2,1)S(1)} %collective-permute-done.27), channel_id=1, source_target_pairs={{0,16},{8,24},{16,0},{24,8},{1,17},{9,25},{17,1},{25,9},{2,18},{10... | collective-permute-start | bytes 3538952 | tf_op jit(solution)/shard_map/ppermute | solution.py:47
  179.6 47.5 %collective-permute-start.15 = (bf16[512,384]{1,0:T(8,128)(2,1)S(1)}, bf16[512,384]{1,0:T(8,128)(2,1)S(1)}, u32[]{:S(2)}, u32[]{:S(2)}) collective-permute-start(bf16[512,384]{1,0:T(8,128)(2,1)S(1)} %constant_dynamic-slice_fusion.2), channel_id=1, source_target_pairs={{8,2},{9,3},{12,6},{13,7}} | collective-permute-start | bytes 1179656 | tf_op jit(solution)/shard_map/ppermute | solution.py:700
  180.3 46.8 %collective-permute-start.14 = (bf16[1024,384]{1,0:T(8,128)(2,1)S(1)}, bf16[1024,384]{1,0:T(8,128)(2,1)S(1)}, u32[]{:S(2)}, u32[]{:S(2)}) collective-permute-start(bf16[1024,384]{1,0:T(8,128)(2,1)S(1)} %collective-permute-done.13.refs_3_.refs_5_), channel_id=1, source_target_pairs={{0,8},{1,9},{2,10},{3,11},{4,12},{5,13},{6,14},{7,15}} | collective-permute-start | bytes 2359304 | tf_op jit(solution)/shard_map/ppermute | solution.py:694
  215.5 45.4 %collective-permute-start.31 = (bf16[192,1536]{1,0:T(8,128)(2,1)S(1)}, bf16[192,1536]{1,0:T(8,128)(2,1)}, u32[]{:S(2)}, u32[]{:S(2)}) collective-permute-start(bf16[192,1536]{1,0:T(8,128)(2,1)S(1)} %slice.314), channel_id=1, source_target_pairs={{0,8},{8,0},{16,24},{24,16},{1,9},{9,1},{17,25},{25,17},{2,10},{10... | collective-permute-start | bytes 1769480 | tf_op jit(solution)/shard_map/ppermute | solution.py:47
  285.6 96.5 %collective-permute-start.39 = (bf16[256,1536]{1,0:T(8,128)(2,1)}, bf16[256,1536]{1,0:T(8,128)(2,1)}, u32[]{:S(2)}, u32[]{:S(2)}) collective-permute-start(bf16[256,1536]{1,0:T(8,128)(2,1)} %slice_bitcast_fusion.8), channel_id=1, source_target_pairs={{0,4},{4,0},{1,5},{5,1},{2,6},{6,2},{3,7},{7,3},{8,12},{12,8},{9,1... | collective-permute-start | bytes 2359304 | tf_op jit(solution)/shard_map/ppermute | solution.py:47
  348.2 49.5 %collective-permute-start.32 = (bf16[256,1536]{1,0:T(8,128)(2,1)S(1)}, bf16[256,1536]{1,0:T(8,128)(2,1)S(1)}, u32[]{:S(2)}, u32[]{:S(2)}) collective-permute-start(bf16[256,1536]{1,0:T(8,128)(2,1)S(1)} %slice_bitcast_fusion.10), channel_id=1, source_target_pairs={{0,4},{4,0},{1,5},{5,1},{2,6},{6,2},{3,7},{7,3},{8,12},{12,8},{9,1... | collective-permute-start | bytes 2359304 | tf_op jit(solution)/shard_map/ppermute | solution.py:47
  351.5 69.6 %collective-permute-start.68 = (bf16[2,192,1536]{2,1,0:T(8,128)(2,1)}, bf16[2,192,1536]{2,1,0:T(8,128)(2,1)}, u32[]{:S(2)}, u32[]{:S(2)}) collective-permute-start(bf16[2,192,1536]{2,1,0:T(8,128)(2,1)} %slice.334), channel_id=1, source_target_pairs={{0,8},{8,0},{16,24},{24,16},{1,9},{9,1},{17,25},{25,17},{2,10},{10... | collective-permute-start | bytes 3538952 | tf_op jit(solution)/shard_map/ppermute | solution.py:47
  382.1 51.2 %collective-permute-start.65 = (bf16[2,192,1536]{2,1,0:T(8,128)(2,1)}, bf16[2,192,1536]{2,1,0:T(8,128)(2,1)}, u32[]{:S(2)}, u32[]{:S(2)}) collective-permute-start(bf16[2,192,1536]{2,1,0:T(8,128)(2,1)} %slice.330), channel_id=1, source_target_pairs={{0,16},{8,24},{16,0},{24,8},{1,17},{9,25},{17,1},{25,9},{2,18},{10... | collective-permute-start | bytes 3538952 | tf_op jit(solution)/shard_map/ppermute | solution.py:47
  395.3 39.7 %collective-permute-start.70 = (bf16[2,192,1536]{2,1,0:T(8,128)(2,1)}, bf16[2,192,1536]{2,1,0:T(8,128)(2,1)}, u32[]{:S(2)}, u32[]{:S(2)}) collective-permute-start(bf16[2,192,1536]{2,1,0:T(8,128)(2,1)} %add_convert_fusion), channel_id=1, source_target_pairs={{0,16},{8,24},{16,0},{24,8},{1,17},{9,25},{17,1},{25,9},{2,18},{10... | collective-permute-start | bytes 3538952 | tf_op jit(solution)/shard_map/ppermute | solution.py:47
  397.7 37.4 %collective-permute-start.67 = (bf16[2,192,1536]{2,1,0:T(8,128)(2,1)}, bf16[2,192,1536]{2,1,0:T(8,128)(2,1)}, u32[]{:S(2)}, u32[]{:S(2)}) collective-permute-start(bf16[2,192,1536]{2,1,0:T(8,128)(2,1)} %add_convert_fusion.1), channel_id=1, source_target_pairs={{0,8},{8,0},{16,24},{24,16},{1,9},{9,1},{17,25},{25,17},{2,10},{10... | collective-permute-start | bytes 3538952 | tf_op jit(solution)/shard_map/ppermute | solution.py:47
  440.9 88.3 %collective-permute-start.71 = (bf16[384,1536]{1,0:T(8,128)(2,1)}, bf16[384,1536]{1,0:T(8,128)(2,1)}, u32[]{:S(2)}, u32[]{:S(2)}) collective-permute-start(bf16[384,1536]{1,0:T(8,128)(2,1)} %fusion.38), channel_id=1, source_target_pairs={{0,2},{2,0},{1,3},{3,1},{4,6},{6,4},{5,7},{7,5},{8,10},{10,8},{9,1... | collective-permute-start | bytes 3538952 | tf_op jit(solution)/shard_map/ppermute | solution.py:47
  494.0 43.0 %collective-permute-start.45 = (bf16[1024,384]{1,0:T(8,128)(2,1)}, bf16[1024,384]{1,0:T(8,128)(2,1)S(1)}, u32[]{:S(2)}, u32[]{:S(2)}) collective-permute-start(bf16[1024,384]{1,0:T(8,128)(2,1)} %get-tuple-element.50), channel_id=1, source_target_pairs={{8,0},{9,1},{10,2},{11,3},{12,4},{13,5},{14,6},{15,7}} | collective-permute-start | bytes 2359304 | tf_op jit(solution)/shard_map/ppermute | solution.py:768
  495.4 35.7 %collective-permute-start.48 = (bf16[512,384]{1,0:T(8,128)(2,1)S(1)}, bf16[512,384]{1,0:T(8,128)(2,1)S(1)}, u32[]{:S(2)}, u32[]{:S(2)}) collective-permute-start(bf16[512,384]{1,0:T(8,128)(2,1)S(1)} %copy-done.86), channel_id=1, source_target_pairs={{2,8},{3,9},{6,12},{7,13}} | collective-permute-start | bytes 1179656 | tf_op jit(solution)/shard_map/ppermute | solution.py:771
  503.5 71.0 %collective-permute-start.47 = (bf16[1024,384]{1,0:T(8,128)(2,1)S(1)}, bf16[1024,384]{1,0:T(8,128)(2,1)S(1)}, u32[]{:S(2)}, u32[]{:S(2)}) collective-permute-start(bf16[1024,384]{1,0:T(8,128)(2,1)S(1)} %add_convert_fusion.2), channel_id=1, source_target_pairs={{0,2},{2,0},{1,3},{3,1},{4,6},{6,4},{5,7},{7,5},{8,10},{10,8},{9,1... | collective-permute-start | bytes 2359304 | tf_op jit(solution)/shard_map/ppermute | solution.py:47
  530.9 59.5 %collective-permute-start.72 = (bf16[192,1536]{1,0:T(8,128)(2,1)S(1)}, bf16[192,1536]{1,0:T(8,128)(2,1)S(1)}, u32[]{:S(2)}, u32[]{:S(2)}) collective-permute-start(bf16[192,1536]{1,0:T(8,128)(2,1)S(1)} %dynamic-slice_convert_fusion), channel_id=1, source_target_pairs={{0,4},{4,0},{1,5},{5,1},{2,6},{6,2},{3,7},{7,3},{8,12},{12,8},{9,1... | collective-permute-start | bytes 1769480 | tf_op jit(solution)/shard_map/ppermute | solution.py:47
  590.5 37.3 %collective-permute-start.49 = (bf16[256,1536]{1,0:T(8,128)(2,1)S(1)}, bf16[256,1536]{1,0:T(8,128)(2,1)S(1)}, u32[]{:S(2)}, u32[]{:S(2)}) collective-permute-start(bf16[256,1536]{1,0:T(8,128)(2,1)S(1)} %get-tuple-element.152), channel_id=1, source_target_pairs={{0,4},{4,0},{1,5},{5,1},{2,6},{6,2},{3,7},{7,3},{8,12},{12,8},{9,1... | collective-permute-start | bytes 2359304 | tf_op jit(solution)/shard_map/ppermute | solution.py:47
  (138 other events, 2376.3 us)

commit v2 on v1

v2 whole, which is shorter than its diff:
```python
import functools
import math

import jax
import jax.numpy as jnp
from jax import lax
from jax.experimental import pallas as pl
from jax.experimental.layout import Layout, with_layout_constraint
from jax.experimental.pallas import tpu as pltpu
from jax.sharding import Mesh, PartitionSpec as P

HEAD = 96
LANES = 128
PIECE = 256
LEN_FIRST = 4096
LEN_LAST = 2048
LEN_MAX = 4096
epsilon = 1e-05
rope_base = 100000.0
negative = -1e30
far_away = 1 << 30
log2_e = 1.4426950408889634
score_scale = 1.0 / math.sqrt(HEAD)
BF = jnp.bfloat16
F32 = jnp.float32
AXES = ("g", "c", "zh", "zl")
MIB = 1024 * 1024
COST_SHARE = 0.01


def params(mib):
    return pltpu.CompilerParams(vmem_limit_bytes=mib * MIB)


def nn(left, right):
    return lax.dot_general(left, right, (((1,), (0,)), ((), ())), preferred_element_type=F32)


def nt(left, right):
    return lax.dot_general(left, right, (((1,), (1,)), ((), ())), preferred_element_type=F32)


def tn(left, right):
    return lax.dot_general(left, right, (((0,), (0,)), ((), ())), preferred_element_type=F32)


def after(value, *earlier):
    return lax.optimization_barrier((value, *earlier))[0]


def sync(*values):
    return lax.optimization_barrier(values)


def all_groups(value):
    return lax.all_gather(value, "g", axis=0, tiled=True)


def flip(value, axis, bit=1):
    count = lax.axis_size(axis)
    return lax.ppermute(value, axis, [(s, s ^ bit) for s in range(count)])


def cost(us):
    us = us * COST_SHARE
    return pl.CostEstimate(flops=int(us * 1.15e9), bytes_accessed=int(us * 3.6e6), transcendentals=0)


def gather_rows(own):
    beside = flip(own, "zl")
    across = flip(own, "c")
    both = flip(beside, "c")
    return [own, beside, across, both]


def from_groups(value):
    return [value] + [flip(value, "g", k) for k in range(1, lax.axis_size("g"))]


def split_core(shard):
    c = lax.axis_index("c")
    keep = lax.dynamic_index_in_dim(shard, c, 0, False)
    got = flip(lax.dynamic_index_in_dim(shard, 1 - c, 0, False), "c")
    return keep, got


def in_order(keep, got, axis=0):
    c = lax.axis_index("c")
    return jnp.where(c == 0, jnp.concatenate([keep, got], axis), jnp.concatenate([got, keep], axis))


def by_rows(value):
    return with_layout_constraint(value, Layout(major_to_minor=(0, 1)))


def over_groups(value):
    return lax.psum_scatter(value, "g", scatter_dimension=0, tiled=True)


def to_owner(mine):
    c = lax.axis_index("c")
    half = mine.shape[0] // 2
    own = lax.dynamic_slice_in_dim(mine, c * half, half, 0).astype(F32)
    got = flip(lax.dynamic_slice_in_dim(mine, (1 - c) * half, half, 0).astype(BF), "c").astype(F32)
    return own, got


def joined(own, got):
    return in_order(own, got, 1)


def swap_halves(value):
    lane = lax.broadcasted_iota(jnp.int32, value.shape, 1)
    return jnp.where(lane < HEAD // 2, pltpu.roll(value, LANES - HEAD // 2, 1), pltpu.roll(value, HEAD // 2, 1))


def turn(value, cosine, sine):
    return value * cosine + swap_halves(value) * sine


def unturn(value, cosine, sine):
    return value * cosine - swap_halves(value) * sine


def widen(value):
    pad = jnp.zeros((value.shape[0], LANES - HEAD), value.dtype)
    return jnp.concatenate([value, pad], 1)


def qkv_kernel(count, where_ref, *refs):
    pieces, refs = refs[: 2 * count], refs[2 * count :]
    x0, x1, x_far, cos_ref, sin_ref, norm_ref, query_ref, kv_ref, weight_ref, gains_ref, x_ref = refs
    step = pl.program_id(0)

    @pl.when(step == 0)
    def _():
        half = pieces[0].shape[0] // 2
        for n, piece in enumerate(pieces):
            for part in range(2):
                at = pl.multiple_of(where_ref[2 * (n % count) + part], 64)
                weight_ref[n // count, pl.ds(at, half), :] = piece[part * half : (part + 1) * half, :]
        row = lax.broadcasted_iota(jnp.int32, (8, LANES), 0)
        lane = lax.broadcasted_iota(jnp.int32, (8, LANES), 1)
        pick = jnp.where(row == lane, 1.0, 0.0).astype(BF)
        gains_ref[...] = nt(pick, weight_ref[0][:, 4 * HEAD :])

    for k in range(4):

        @pl.when(step == k)
        def _():
            x_ref[...] = (x0, x1)[k][...] if k < 2 else x_far[(k - 2) * PIECE : (k - 1) * PIECE, :]

    x = x_ref[...].astype(F32)
    r = lax.rsqrt(jnp.mean(x * x, axis=-1, keepdims=True) + epsilon)
    normed = (x * r * gains_ref[0:1, :]).astype(BF)
    norm_ref[0] = normed
    cosine, sine = cos_ref[0], sin_ref[0]
    packs = []
    for j in range(2):
        pre = nn(normed, weight_ref[j][:, 0 : 4 * HEAD])
        for h in range(2):
            turned = turn(widen(pre[:, h * HEAD : (h + 1) * HEAD]), cosine, sine)
            query_ref[j, 0, h * PIECE : (h + 1) * PIECE] = (turned * (score_scale * log2_e)).astype(BF)
        packs.append(turn(widen(pre[:, 2 * HEAD : 3 * HEAD]), cosine, sine)[:, 0:HEAD])
        packs.append(pre[:, 3 * HEAD :])
    kv_ref[...] = jnp.concatenate(packs, 1).astype(BF)


def project_qkv(where, pieces, x_rows, x_far, cos_table, sin_table):
    rows, width = x_rows[0].shape
    n_cols = pieces[0].shape[1]
    table = pl.BlockSpec((1, rows, LANES), lambda i, *_: (i, 0, 0))
    return pl.pallas_call(
        functools.partial(qkv_kernel, len(pieces) // 2),
        grid_spec=pltpu.PrefetchScalarGridSpec(
            num_scalar_prefetch=1,
            grid=(4,),
            in_specs=[pl.BlockSpec(v.shape, lambda i, *_: (0, 0)) for v in (*pieces, *x_rows, x_far)] + [table, table],
            out_specs=[
                pl.BlockSpec((1, rows, width), lambda i, *_: (i, 0, 0)),
                pl.BlockSpec((2, 1, 2 * rows, LANES), lambda i, *_: (0, i, 0, 0)),
                pl.BlockSpec((rows, 4 * HEAD), lambda i, *_: (i, 0)),
                pl.BlockSpec((2, width, n_cols), lambda i, *_: (0, 0, 0)),
                pl.BlockSpec((8, width), lambda i, *_: (0, 0)),
            ],
            scratch_shapes=[pltpu.VMEM((rows, width), BF)],
        ),
        out_shape=[
            jax.ShapeDtypeStruct((4, rows, width), BF),
            jax.ShapeDtypeStruct((2, 4, 2 * rows, LANES), BF),
            jax.ShapeDtypeStruct((4 * rows, 4 * HEAD), BF),
            jax.ShapeDtypeStruct((2, width, n_cols), BF),
            jax.ShapeDtypeStruct((8, width), F32),
        ],
        compiler_params=params(48),
        cost_estimate=cost(8),
        name="project_qkv",
    )(where, *pieces, *x_rows, x_far, cos_table, sin_table)


def query_back_kernel(core_ref, dq_ref, weight_ref, cos_ref, sin_ref, grad_ref, share_ref):
    total = None
    for j in range(2):
        heads = []
        for h in range(2):
            turned = unturn(dq_ref[j, 0, h * PIECE : (h + 1) * PIECE], cos_ref[0], sin_ref[0])
            heads.append((turned * score_scale)[:, 0:HEAD])
        grad = jnp.concatenate(heads, 1).astype(BF)
        grad_ref[j, 0] = grad
        term = nt(grad, weight_ref[j][:, 0 : 2 * HEAD])
        total = term if total is None else total + term
    share_ref[0] = total.astype(BF)


def kv_back_kernel(n_same, has_above, core_ref, *refs):
    refs = list(refs)
    own_ref, first_ref, second_ref = refs[:3]
    same_refs = refs[3 : 3 + n_same]
    refs = refs[3 + n_same :]
    i = pl.program_id(0)
    late = i >= 2
    d_kv = own_ref[...] + jnp.where(late, second_ref[...], first_ref[...]).astype(F32)
    for ref in same_refs:
        d_kv = d_kv + ref[...].astype(F32)
    if has_above:
        d_kv = d_kv + jnp.where(i == core_ref[0], refs.pop(0)[...], 0).astype(F32)
    share_in_ref, weight_ref, cos_ref, sin_ref, grad_ref, share_ref = refs
    total = share_in_ref[0].astype(F32)
    for j in range(2):
        both = d_kv[:, 2 * HEAD * j : 2 * HEAD * (j + 1)]
        turned = unturn(widen(both[:, 0:HEAD]), cos_ref[0], sin_ref[0]) * (1.0 / log2_e)
        grad = jnp.concatenate([turned[:, 0:HEAD], both[:, HEAD:]], 1).astype(BF)
        grad_ref[j, 0] = grad
        total = total + nt(grad, weight_ref[j][:, 2 * HEAD : 4 * HEAD])
    share_ref[0] = total.astype(BF)


def project_back(kernel, core, args, specs, weights, cos_table, sin_table, name):
    count, rows, _ = cos_table.shape
    width = weights.shape[1]
    piece = pl.BlockSpec((1, rows, width), lambda i, *_: (i, 0, 0))
    table = pl.BlockSpec((1, rows, cos_table.shape[2]), lambda i, *_: (i, 0, 0))
    return pl.pallas_call(
        kernel,
        grid_spec=pltpu.PrefetchScalarGridSpec(
            num_scalar_prefetch=1,
            grid=(count,),
            in_specs=specs + [pl.BlockSpec((2, width, 4 * HEAD), lambda i, *_: (0, 0, 0)), table, table],
            out_specs=[pl.BlockSpec((2, 1, rows, 2 * HEAD), lambda i, *_: (0, i, 0, 0)), piece],
        ),
        out_shape=[
            jax.ShapeDtypeStruct((2, count, rows, 2 * HEAD), BF),
            jax.ShapeDtypeStruct((count, rows, width), BF),
        ],
        compiler_params=params(40),
        cost_estimate=cost(4),
        name=name,
    )(core, *args, weights, cos_table, sin_table)


def query_back(core, d_query, weights, cos_table, sin_table):
    spec = pl.BlockSpec((2, 1, 2 * PIECE, LANES), lambda i, *_: (0, i, 0, 0))
    return project_back(query_back_kernel, core, [d_query], [spec], weights, cos_table, sin_table, "query_back")


def kv_back(core, own, other, same, above, shares, weights, cos_table, sin_table):
    rows = pl.BlockSpec((PIECE, 4 * HEAD), lambda i, *_: (i, 0))
    chunk = pl.BlockSpec((PIECE, 4 * HEAD), lambda i, *_: (i % 2, 0))
    args = [own, *other, *same, *above, shares]
    specs = [rows, chunk, chunk] + [rows] * len(same)
    specs += [pl.BlockSpec((PIECE, 4 * HEAD), lambda i, *_: (0, 0))] * len(above)
    specs.append(pl.BlockSpec((1, *shares.shape[1:]), lambda i, *_: (i, 0, 0)))
    kernel = functools.partial(kv_back_kernel, len(same), bool(above))
    return project_back(kernel, core, args, specs, weights, cos_table, sin_table, "kv_back")


CHUNK = 2 * PIECE


def unpack_kv(swaps, block_refs, key_scratch, value_scratch):
    lane = lax.broadcasted_iota(jnp.int32, (CHUNK, LANES - HEAD), 1)
    ones = jnp.where(lane < 3, 1.0, 0.0).astype(BF)
    at = 0
    for swap, ref in zip(swaps, block_refs):
        for start in range(0, ref.shape[0], CHUNK):
            block = ref[start : start + CHUNK, :]
            for j in range(2):
                first = 2 * HEAD * (j ^ swap)
                k = block[:, first : first + HEAD]
                v = block[:, first + HEAD : first + 2 * HEAD]
                key_scratch[j, at : at + CHUNK, :] = jnp.concatenate([k, ones], 1)
                value_scratch[j, at : at + CHUNK, :] = jnp.concatenate([v, ones], 1)
            at += CHUNK


def chunk_state(info_ref, base, i):
    last = base + (CHUNK - 1)
    touched = (base <= info_ref[i, 3]) & (last >= info_ref[i, 0])
    full = (base >= info_ref[i, 1]) & (last <= info_ref[i, 2])
    return touched, full


def forward_kernel(swaps, first, last, info_ref, base_ref, zl_ref, *refs):
    refs = list(refs)
    n_blocks = len(swaps)
    query_ref, low_ref, high_ref = refs[:3]
    block_refs = refs[3 : 3 + n_blocks]
    refs = refs[3 + n_blocks :]
    if not first:
        acc_in = refs.pop(0)
    if last:
        mixed_ref = refs.pop(0)
    kept_ref = refs.pop(0)
    key_scratch, value_scratch, acc, top = refs
    i = pl.program_id(0)

    @pl.when(i == 0)
    def _():
        unpack_kv(swaps, block_refs, key_scratch, value_scratch)

    for j in range(2):
        if first:
            acc[j] = jnp.zeros((CHUNK, LANES), F32)
            top[j] = jnp.full((CHUNK, LANES), negative, F32)
        else:
            acc[j] = acc_in[j, 0]
            top[j] = jnp.broadcast_to(acc_in[j, 0][:, HEAD + 1 : HEAD + 2], (CHUNK, LANES))
    n_chunks = sum(r.shape[0] for r in block_refs) // CHUNK

    def visit(n, masked):
        rows = pl.ds(pl.multiple_of(n * CHUNK, CHUNK), CHUNK)
        if masked:
            at = lax.broadcasted_iota(jnp.int32, (PIECE, CHUNK), 1)
            token = base_ref[n] + lax.rem(at + zl_ref[0] * PIECE, CHUNK)
            low = jnp.concatenate([low_ref[0]] * (CHUNK // LANES), 1)
            high = jnp.concatenate([high_ref[0]] * (CHUNK // LANES), 1)
            allowed = (token >= low) & (token <= high)
        for j in range(2):
            scores = nt(query_ref[j, 0], key_scratch[j, rows, :])
            if masked:
                scores = jnp.concatenate(
                    [jnp.where(allowed, scores[h * PIECE : (h + 1) * PIECE], negative) for h in range(2)], 0
                )
            old = top[j]
            new = jnp.maximum(old, jnp.max(scores, axis=1, keepdims=True))
            top[j] = new
            probs = jnp.exp2(scores - jnp.concatenate([new] * (CHUNK // LANES), 1)).astype(BF)
            acc[j] = acc[j] * jnp.exp2(old - new) + nn(probs, value_scratch[j, rows, :])

    @pl.loop(0, n_chunks)
    def _(n):
        touched, full = chunk_state(info_ref, base_ref[n], i)

        @pl.when(touched & full)
        def _():
            visit(n, False)

        @pl.when(touched & jnp.logical_not(full))
        def _():
            visit(n, True)

    lane = lax.broadcasted_iota(jnp.int32, (CHUNK, LANES), 1)
    if last:
        for j in range(2):
            total = acc[j][:, HEAD : HEAD + 1]
            out = acc[j] / total
            kept_ref[j, 0] = jnp.where(lane < HEAD, out, top[j] + jnp.log2(total))
            mixed_ref[j, 0] = jnp.concatenate([out[0:PIECE, 0:HEAD], out[PIECE:, 0:HEAD]], 1).astype(BF)
    else:
        for j in range(2):
            kept_ref[j, 0] = jnp.where(lane == HEAD + 1, top[j], acc[j])


def attend(query, low, high, info, bases, zl, blocks, swaps, state, last):
    count = query.shape[1]
    n_keys = sum(b.shape[0] for b in blocks)
    per_piece = pl.BlockSpec((2, 1, CHUNK, LANES), lambda i, *_: (0, i, 0, 0))
    bound = pl.BlockSpec((1, PIECE, LANES), lambda i, *_: (i, 0, 0))
    in_specs = [per_piece, bound, bound]
    in_specs += [pl.BlockSpec(b.shape, lambda i, *_: (0, 0)) for b in blocks]
    args = [query, low, high, *blocks]
    if state is not None:
        in_specs.append(per_piece)
        args.append(state)
    wide = jax.ShapeDtypeStruct((2, count, CHUNK, LANES), F32)
    if last:
        out_shape = [jax.ShapeDtypeStruct((2, count, PIECE, 2 * HEAD), BF), wide]
        out_specs = [pl.BlockSpec((2, 1, PIECE, 2 * HEAD), lambda i, *_: (0, i, 0, 0)), per_piece]
    else:
        out_shape = wide
        out_specs = per_piece
    return pl.pallas_call(
        functools.partial(forward_kernel, swaps, state is None, last),
        grid_spec=pltpu.PrefetchScalarGridSpec(
            num_scalar_prefetch=3,
            grid=(count,),
            in_specs=in_specs,
            out_specs=out_specs,
            scratch_shapes=[
                pltpu.VMEM((2, n_keys, LANES), BF),
                pltpu.VMEM((2, n_keys, LANES), BF),
                pltpu.VMEM((2, CHUNK, LANES), F32),
                pltpu.VMEM((2, CHUNK, LANES), F32),
            ],
        ),
        out_shape=out_shape,
        compiler_params=params(48),
        cost_estimate=cost(n_keys / 100),
        name="attend",
    )(info, bases, zl, *args)


def split_three(value):
    first = value.astype(BF)
    rest = value - first.astype(F32)
    second = rest.astype(BF)
    third = (rest - second.astype(F32)).astype(BF)
    return first, second, third


def augment(wide, extra):
    lane = lax.broadcasted_iota(jnp.int32, wide.shape, 1)
    a, b, c = (part.astype(F32) for part in split_three(extra))
    out = wide.astype(F32)
    out = jnp.where(lane == HEAD, a, out)
    out = jnp.where(lane == HEAD + 1, b, out)
    out = jnp.where(lane == HEAD + 2, c, out)
    return out.astype(BF)


def prepare_kernel(m0, m1, m2, m3, w0, w1, kept_ref, query_ref, q_aug_ref, o_aug_ref, mid_ref):
    step = pl.program_id(0)
    for k, ref in enumerate((m0, m1, m2, m3)):

        @pl.when(step == k)
        def _():
            mid_ref[...] = ref[...]

    mid = mid_ref[...]
    for j, weight_ref in enumerate((w0, w1)):
        grad = nn(mid, weight_ref[...][:, 0 : 2 * HEAD])
        wide = jnp.concatenate([widen(grad[:, 0:HEAD]), widen(grad[:, HEAD : 2 * HEAD])], 0).astype(BF)
        kept = kept_ref[j, 0]
        delta = jnp.sum(wide.astype(F32) * kept, axis=1, keepdims=True)
        q_aug_ref[j, 0] = augment(query_ref[j, 0], -kept[:, HEAD : HEAD + 1])
        o_aug_ref[j, 0] = augment(wide, -delta)


def prepare_back(mid, weights, tile, kept, query):
    count = len(mid)
    rows, width = mid[0].shape
    per_piece = pl.BlockSpec((2, 1, CHUNK, LANES), lambda i: (0, i, 0, 0))
    return pl.pallas_call(
        prepare_kernel,
        grid=(count,),
        in_specs=[pl.BlockSpec((rows, width), lambda i: (0, 0))] * count
        + [pl.BlockSpec((width, 256), lambda i: (0, tile))] * 2
        + [per_piece, per_piece],
        out_specs=[per_piece, per_piece],
        out_shape=[jax.ShapeDtypeStruct(query.shape, BF)] * 2,
        scratch_shapes=[pltpu.VMEM((rows, width), BF)],
        compiler_params=params(40),
        cost_estimate=cost(6),
        name="prepare_back",
    )(*mid, *weights, kept, query)


def backward_kernel(swaps, has_dq, info_ref, base_ref, zl_ref, *refs):
    refs = list(refs)
    n_blocks = len(swaps)
    q_aug, o_aug, low_ref, high_ref = refs[:4]
    block_refs = refs[4 : 4 + n_blocks]
    refs = refs[4 + n_blocks :]
    if has_dq:
        dq_in = refs.pop(0)
    dq_ref = refs.pop(0)
    out_refs = refs[:n_blocks]
    key_scratch, value_scratch, d_key, d_value = refs[n_blocks:]
    i = pl.program_id(0)

    @pl.when(i == 0)
    def _():
        unpack_kv(swaps, block_refs, key_scratch, value_scratch)
        d_key[...] = jnp.zeros(d_key.shape, F32)
        d_value[...] = jnp.zeros(d_value.shape, F32)

    for j in range(2):
        if has_dq:
            dq_ref[j, 0] = dq_in[j, 0]
        else:
            dq_ref[j, 0] = jnp.zeros((CHUNK, LANES), F32)
    n_chunks = sum(r.shape[0] for r in block_refs) // CHUNK

    def visit(n, masked):
        rows = pl.ds(pl.multiple_of(n * CHUNK, CHUNK), CHUNK)
        if masked:
            at = lax.broadcasted_iota(jnp.int32, (CHUNK, CHUNK), 0)
            token = base_ref[n] + lax.rem(at + zl_ref[0] * PIECE, CHUNK)
            allowed = (token >= low_ref[0, 0:1, :]) & (token <= high_ref[0, 0:1, :])
        for j in range(2):
            keys = key_scratch[j, rows, :]
            probs = jnp.exp2(nt(keys, q_aug[j, 0]))
            if masked:
                probs = jnp.where(allowed, probs, 0.0)
            d_probs = nt(value_scratch[j, rows, :], o_aug[j, 0])
            low_probs = probs.astype(BF)
            d_scores = (probs * d_probs).astype(BF)
            d_value[j, rows, :] += nn(low_probs, o_aug[j, 0])
            d_key[j, rows, :] += nn(d_scores, q_aug[j, 0])
            dq_ref[j, 0] += tn(d_scores, keys)

    @pl.loop(0, n_chunks)
    def _(n):
        touched, full = chunk_state(info_ref, base_ref[n], i)

        @pl.when(touched & full)
        def _():
            visit(n, False)

        @pl.when(touched & jnp.logical_not(full))
        def _():
            visit(n, True)

    @pl.when(i == pl.num_programs(0) - 1)
    def _():
        at = 0
        for swap, ref in zip(swaps, out_refs):
            for start in range(0, ref.shape[0], CHUNK):
                parts = []
                for j in (swap, 1 - swap):
                    parts.append(d_key[j, at : at + CHUNK, :][:, 0:HEAD])
                    parts.append(d_value[j, at : at + CHUNK, :][:, 0:HEAD])
                ref[start : start + CHUNK, :] = jnp.concatenate(parts, 1).astype(ref.dtype)
                at += CHUNK


def attend_back(q_aug, o_aug, low, high, info, bases, zl, blocks, swaps, d_query, kinds):
    count = q_aug.shape[1]
    n_keys = sum(b.shape[0] for b in blocks)
    per_piece = pl.BlockSpec((2, 1, CHUNK, LANES), lambda i, *_: (0, i, 0, 0))
    bound = pl.BlockSpec((1, 8, CHUNK), lambda i, *_: (i, 0, 0))
    whole = [pl.BlockSpec(b.shape, lambda i, *_: (0, 0)) for b in blocks]
    in_specs = [per_piece, per_piece, bound, bound, *whole]
    args = [q_aug, o_aug, low, high, *blocks]
    if d_query is not None:
        in_specs.append(per_piece)
        args.append(d_query)
    return pl.pallas_call(
        functools.partial(backward_kernel, swaps, d_query is not None),
        grid_spec=pltpu.PrefetchScalarGridSpec(
            num_scalar_prefetch=3,
            grid=(count,),
            in_specs=in_specs,
            out_specs=[per_piece, *whole],
            scratch_shapes=[
                pltpu.VMEM((2, n_keys, LANES), BF),
                pltpu.VMEM((2, n_keys, LANES), BF),
                pltpu.VMEM((2, n_keys, LANES), F32),
                pltpu.VMEM((2, n_keys, LANES), F32),
            ],
        ),
        out_shape=[jax.ShapeDtypeStruct((2, count, CHUNK, LANES), F32)]
        + [jax.ShapeDtypeStruct(b.shape, k) for b, k in zip(blocks, kinds)],
        compiler_params=params(56),
        cost_estimate=cost(n_keys / 64),
        name="attend_back",
    )(info, bases, zl, *args)


def ffn_kernel(tiles, n0, n1, g0, g1, *refs):
    own_refs, other_refs, refs = refs[0:3], refs[3:6], refs[6:]
    o0, o1, b0, b1, hidden_ref, dg_ref, du_ref, norm_t, grad_t, norm_ref, grad_ref, acc_out, acc_back = refs
    step = pl.program_id(0)

    @pl.when(step == 0)
    def _():
        norm_ref[0:PIECE] = n0[...]
        norm_ref[PIECE:] = n1[...]
        grad_ref[0:PIECE] = g0[...]
        grad_ref[PIECE:] = g1[...]

    def run(gate_ref, up_ref, down_ref, first):
        gate_w, up_w, down_w = gate_ref[...], up_ref[...], down_ref[...]
        gate = nn(norm_ref[...], gate_w)
        up = nn(norm_ref[...], up_w)
        d_hidden = nn(grad_ref[...], down_w)
        sig = jax.nn.sigmoid(gate)
        silu = gate * sig
        hidden = (silu * up).astype(BF)
        d_gate = (d_hidden * up * sig * (1.0 + gate * (1.0 - sig))).astype(BF)
        d_up = (d_hidden * silu).astype(BF)
        hidden_ref[...] = hidden
        dg_ref[...] = d_gate
        du_ref[...] = d_up
        norm_t[...] = norm_ref[pl.ds(pl.multiple_of(step * LANES, LANES), LANES), :].T
        grad_t[...] = grad_ref[pl.ds(pl.multiple_of(step * LANES, LANES), LANES), :].T
        out = nt(hidden, down_w)
        back = nt(d_gate, gate_w) + nt(d_up, up_w)
        if first:
            acc_out[...] = out
            acc_back[...] = back
        else:
            acc_out[...] += out
            acc_back[...] += back

    @pl.when(step == 0)
    def _():
        run(*own_refs, True)

    @pl.when((step > 0) & (step < tiles))
    def _():
        run(*own_refs, False)

    @pl.when(step >= tiles)
    def _():
        run(*other_refs, False)

    @pl.when(step == pl.num_programs(0) - 1)
    def _():
        o0[...] = acc_out[0:PIECE].astype(BF)
        o1[...] = acc_out[PIECE:].astype(BF)
        b0[...] = acc_back[0:PIECE].astype(BF)
        b1[...] = acc_back[PIECE:].astype(BF)


def feed_forward(norm_rows, grad_rows, own, other):
    rows, width = norm_rows[0].shape
    half = 512
    tile = 256
    tiles = half // tile
    whole = pl.BlockSpec((rows, width), lambda s: (0, 0))

    def own_spec(at):
        return pl.BlockSpec((width, tile), lambda s: (0, at // tile + jnp.minimum(s, tiles - 1)))

    def other_spec(at):
        return pl.BlockSpec((width, tile), lambda s: (0, at // tile + jnp.maximum(s - tiles, 0)))

    hid = pl.BlockSpec((2 * rows, tile), lambda s: (0, s))
    turned = pl.BlockSpec((width, LANES), lambda s: (0, s))
    return pl.pallas_call(
        functools.partial(ffn_kernel, tiles),
        grid=(2 * tiles,),
        in_specs=[whole] * 4 + [own_spec(at) for _, at in own] + [other_spec(at) for _, at in other],
        out_specs=[whole] * 4 + [hid] * 3 + [turned] * 2,
        out_shape=[jax.ShapeDtypeStruct((rows, width), BF)] * 4
        + [jax.ShapeDtypeStruct((2 * rows, 2 * half), BF)] * 3
        + [jax.ShapeDtypeStruct((width, 2 * rows), BF)] * 2,
        scratch_shapes=[pltpu.VMEM((2 * rows, width), BF)] * 2 + [pltpu.VMEM((2 * rows, width), F32)] * 2,
        compiler_params=params(56),
        cost_estimate=cost(18),
        name="feed_forward",
    )(*norm_rows, *grad_rows, *(w for w, _ in own), *(w for w, _ in other))


def weight_grad_kernel(n_jobs, *refs):
    out_ref = refs[-1]
    for n in range(n_jobs):
        left_early, left_late, early, late = refs[4 * n : 4 * n + 4]

        @pl.when(pl.program_id(1) == n)
        def _():
            total = nn(left_early[...], early[...]) + nn(left_late[...], late[...])
            out_ref[...] = total.astype(BF)


def weight_grad(jobs, us):
    width, depth = jobs[0][0].shape
    half = jobs[0][2].shape[1] // 2
    count = len(jobs)
    left = pl.BlockSpec((width, depth), lambda s, n: (0, 0))
    cols = pl.BlockSpec((depth, half), lambda s, n: (0, s))
    return pl.pallas_call(
        functools.partial(weight_grad_kernel, count),
        grid=(2, count),
        in_specs=[left, left, cols, cols] * count,
        out_specs=pl.BlockSpec((width, half), lambda s, n: (0, s * count + n)),
        out_shape=jax.ShapeDtypeStruct((width, 2 * count * half), BF),
        compiler_params=params(48),
        cost_estimate=cost(us),
        name="weight_grad",
    )(*(value for job in jobs for value in job))


def head_grad_kernel(l0, l1, l2, l3, right_ref, out_ref):
    for j in range(2):
        total = None
        for k, left in enumerate((l0, l1, l2, l3)):
            term = tn(left[...], right_ref[j, k])
            total = term if total is None else total + term
        wide = jnp.concatenate([total, jnp.zeros((total.shape[0], 256 - 2 * HEAD), F32)], 1)
        out_ref[:, j * 256 : (j + 1) * 256] = wide.astype(BF)


def head_grad(left, right):
    rows, width = left[0].shape
    tile = 512
    return pl.pallas_call(
        head_grad_kernel,
        grid=(width // tile,),
        in_specs=[pl.BlockSpec((rows, tile), lambda s: (0, s))] * 4 + [pl.BlockSpec(right.shape, lambda s: (0, 0, 0, 0))],
        out_specs=pl.BlockSpec((tile, 512), lambda s: (s, 0)),
        out_shape=jax.ShapeDtypeStruct((width, 512), BF),
        compiler_params=params(40),
        cost_estimate=cost(3),
        name="head_grad",
    )(*left, right)


def gain_kernel(lane, *refs):
    out_ref = refs[-1]
    count = (len(refs) - 1) // 2
    at = lax.broadcasted_iota(jnp.int32, (PIECE, LANES), 1)
    pick = jnp.where(at == lane, 1.0, 0.0).astype(BF)
    total = None
    for share, normed in zip(refs[:count], refs[count : 2 * count]):
        product = (share[...].astype(F32) * normed[...].astype(F32)).astype(BF)
        term = tn(product, pick)
        total = term if total is None else total + term
    out_ref[...] = total


def gain_columns(shares, normed, lane):
    rows, width = shares[0].shape
    tile = 512
    spec = pl.BlockSpec((rows, tile), lambda s: (0, s))
    return pl.pallas_call(
        functools.partial(gain_kernel, lane),
        grid=(width // tile,),
        in_specs=[spec] * 8,
        out_specs=pl.BlockSpec((tile, LANES), lambda s: (s, 0)),
        out_shape=jax.ShapeDtypeStruct((width, LANES), F32),
        compiler_params=params(40),
        cost_estimate=cost(3),
        name="gain_columns",
    )(*shares, *normed)


def kv_grad_kernel(norm_ref, share_ref, dkv_ref, column_ref, *refs):
    out_ref = refs[-1]
    at = lax.broadcasted_iota(jnp.int32, (PIECE, LANES), 1)
    pick = jnp.where(at == 0, 1.0, 0.0).astype(BF)
    columns = column_ref[...]
    totals = [None, None]
    for k in range(4):
        normed = norm_ref[k]
        product = (share_ref[k].astype(F32) * normed.astype(F32)).astype(BF)
        columns = columns + tn(product, pick)
        for j in range(2):
            term = tn(normed, dkv_ref[j, k])
            totals[j] = term if totals[j] is None else totals[j] + term
    for j in range(2):
        out_ref[:, j * 256 : (j + 1) * 256] = jnp.concatenate([totals[j], columns[:, 0 : 256 - 2 * HEAD]], 1).astype(BF)


def kv_grad(normed, shares, d_kvs, columns):
    count, rows, width = normed.shape
    tile = 512
    spec = pl.BlockSpec((count, rows, tile), lambda s: (0, 0, s))
    return pl.pallas_call(
        kv_grad_kernel,
        grid=(width // tile,),
        in_specs=[
            spec,
            spec,
            pl.BlockSpec(d_kvs.shape, lambda s: (0, 0, 0, 0)),
            pl.BlockSpec((tile, LANES), lambda s: (s, 0)),
        ],
        out_specs=pl.BlockSpec((tile, 512), lambda s: (s, 0)),
        out_shape=jax.ShapeDtypeStruct((width, 512), BF),
        compiler_params=params(40),
        cost_estimate=cost(4),
        name="kv_grad",
    )(normed, shares, d_kvs, columns)


def output_kernel(mixed_ref, w0, w1, far_ref, near_ref):
    step = pl.program_id(0)
    total = None
    for j, weight in enumerate((w0, w1)):
        heads = jnp.concatenate([mixed_ref[j, 0], mixed_ref[j, 1]], 0)
        term = nt(heads, weight[...][:, 0 : 2 * HEAD])
        total = term if total is None else total + term

    @pl.when(step == 0)
    def _():
        far_ref[...] = total.astype(BF)

    @pl.when(step == 1)
    def _():
        near_ref[...] = total


def output_projection(mixed, weights, tile):
    _, count, rows, width_heads = mixed.shape
    width = weights[0].shape[0]
    whole = pl.BlockSpec((2 * rows, width), lambda s: (0, 0))
    return pl.pallas_call(
        output_kernel,
        grid=(2,),
        in_specs=[pl.BlockSpec((2, 2, rows, width_heads), lambda s: (0, 1 - s, 0, 0))]
        + [pl.BlockSpec((width, 256), lambda s: (0, tile))] * 2,
        out_specs=[whole, whole],
        out_shape=[jax.ShapeDtypeStruct((2 * rows, width), BF), jax.ShapeDtypeStruct((2 * rows, width), F32)],
        compiler_params=params(40),
        cost_estimate=cost(4),
        name="output_projection",
    )(mixed, *weights)


def add_kernel(near_ref, across_ref, out_ref):
    out_ref[...] = (near_ref[...].astype(F32) + across_ref[...].astype(F32)).astype(BF)


def add_rows(near, near_at, across, across_at):
    rows, width = PIECE, near.shape[1]
    return pl.pallas_call(
        add_kernel,
        grid=(1,),
        in_specs=[
            pl.BlockSpec((rows, width), lambda s: (near_at, 0)),
            pl.BlockSpec((rows, width), lambda s: (across_at, 0)),
        ],
        out_specs=pl.BlockSpec((rows, width), lambda s: (0, 0)),
        out_shape=jax.ShapeDtypeStruct((rows, width), BF),
        compiler_params=params(32),
        cost_estimate=cost(1),
        name="add_rows",
    )(near, across)


def forward_norm_kernel(x_ref, near_ref, across_ref, beside_ref, gain_ref, after_ref, norm_ref):
    rows = x_ref[...].astype(F32) + (near_ref[...] + across_ref[...].astype(F32) + beside_ref[...].astype(F32))
    after_ref[...] = rows
    r = lax.rsqrt(jnp.mean(rows * rows, axis=-1, keepdims=True) + epsilon)
    norm_ref[...] = (rows * r * gain_ref[1:2, :]).astype(BF)


def row_specs(width, n):
    return [pl.BlockSpec((LANES, width), lambda i: (i, 0))] * n


def forward_norm(x, near, across, beside, gain_rows):
    rows, width = x.shape
    return pl.pallas_call(
        forward_norm_kernel,
        grid=(rows // LANES,),
        in_specs=row_specs(width, 4) + [pl.BlockSpec((8, width), lambda i: (0, 0))],
        out_specs=row_specs(width, 2),
        out_shape=[jax.ShapeDtypeStruct((rows, width), F32), jax.ShapeDtypeStruct((rows, width), BF)],
        compiler_params=params(32),
        cost_estimate=cost(2),
        name="forward_norm",
    )(x, near, across, beside, gain_rows)


def backward_norm_kernel(which, share_ref, across_ref, beside_ref, rows_ref, base_ref, gain_ref, *out_refs):
    upstream = share_ref[...].astype(F32) + across_ref[...].astype(F32) + beside_ref[...].astype(F32)
    rows = rows_ref[...].astype(F32)
    r = lax.rsqrt(jnp.mean(rows * rows, axis=-1, keepdims=True) + epsilon)
    weighted = upstream * gain_ref[which : which + 1, :]
    inner = jnp.mean(weighted * rows, axis=-1, keepdims=True)
    out = base_ref[...].astype(F32) + (r * weighted - rows * (r * r * r) * inner)
    for ref in out_refs:
        ref[...] = out.astype(ref.dtype)


def backward_norm(which, share, across, beside, rows, base, gain_rows, kinds):
    count, width = rows.shape
    return pl.pallas_call(
        functools.partial(backward_norm_kernel, which),
        grid=(count // LANES,),
        in_specs=row_specs(width, 5) + [pl.BlockSpec((8, width), lambda i: (0, 0))],
        out_specs=row_specs(width, len(kinds)),
        out_shape=[jax.ShapeDtypeStruct((count, width), kind) for kind in kinds],
        compiler_params=params(32),
        cost_estimate=cost(2),
        name="backward_norm",
    )(share, across, beside, rows, base, gain_rows)


def token_tables(token, seq_lengths, piece_starts):
    n = seq_lengths.shape[0]
    upto = jnp.arange(n)[None, :] <= jnp.arange(n)[:, None]
    ends = jnp.sum(jnp.where(upto, seq_lengths[None, :], 0), axis=1)
    after = token[:, None] >= ends[None, :]
    start = jnp.sum(jnp.where(after, seq_lengths[None, :], 0), axis=1)
    end = jnp.min(jnp.where(after, far_away, ends[None, :]), axis=1)
    inside = (token[:, None] >= piece_starts[None, :]) & (token[:, None] < piece_starts[None, :] + PIECE)
    piece_end = jnp.max(jnp.where(inside, piece_starts[None, :] + PIECE, 0), axis=1)
    high = jnp.maximum(token, jnp.minimum(piece_end, end) - 1)
    return start, high


def may_meet(one, two, group_tokens, count):
    total = group_tokens * count
    regions = ((0, LEN_FIRST, LEN_FIRST), (LEN_FIRST, total - LEN_LAST, LEN_MAX), (total - LEN_LAST, total, LEN_LAST))
    for start, end, longest in regions:
        both = all(g * group_tokens < end and (g + 1) * group_tokens > start for g in (one, two))
        if both and (abs(one - two) - 1) * group_tokens + 1 < longest:
            return True
    return False


def body(
    inputs,
    first_gain,
    query_weight,
    key_matrix,
    value_matrix,
    output_weight,
    second_gain,
    gate_weight,
    up_weight,
    down_weight,
    seq_lengths,
    piece_starts,
    out_cotangent,
):
    g, c, zh, zl = (lax.axis_index(a) for a in AXES)
    groups = lax.axis_size("g")
    rows, width = inputs.shape
    span = 4 * rows
    group_tokens = 2 * span
    shard_rows = query_weight.shape[0]

    order = jnp.arange(4)
    piece_base = (2 * g + (c ^ (order >> 1))) * span + zh * CHUNK + (zl ^ (order & 1)) * rows
    token = (piece_base[:, None] + jnp.arange(rows)[None, :]).reshape(-1).astype(jnp.int32)
    low, high = token_tables(token, seq_lengths, piece_starts)
    position = (token - low).astype(F32)
    low, high = low.reshape(4, rows), high.reshape(4, rows)
    info = jnp.stack([low.min(1), low.max(1), high.min(1), high.max(1)], 1).astype(jnp.int32)
    low_wide = jnp.broadcast_to(low[:, :, None], (4, rows, LANES)).astype(jnp.int32)
    high_wide = jnp.broadcast_to(high[:, :, None], (4, rows, LANES)).astype(jnp.int32)
    low_rows = jnp.broadcast_to(jnp.tile(low, (1, 2))[:, None, :], (4, 8, CHUNK)).astype(jnp.int32)
    high_rows = jnp.broadcast_to(jnp.tile(high, (1, 2))[:, None, :], (4, 8, CHUNK)).astype(jnp.int32)
    zl_info = jnp.reshape(zl, (1,)).astype(jnp.int32)
    frequency = rope_base ** (-(2.0 / HEAD) * jnp.arange(HEAD // 2, dtype=F32))
    angles = position[:, None] * frequency[None, :]
    cosine, sine = jnp.cos(angles), jnp.sin(angles)
    pad = jnp.zeros((span, LANES - HEAD), F32)
    cos_table = jnp.concatenate([cosine, cosine, pad], 1).reshape(4, rows, LANES)
    sin_table = jnp.concatenate([-sine, sine, pad], 1).reshape(4, rows, LANES)

    def halves(matrix):
        return matrix.reshape(matrix.shape[0], 2, -1).transpose(1, 0, 2)

    blank = functools.partial(jnp.zeros, dtype=BF)
    half = gate_weight.shape[1] // 2
    zl_info = jnp.reshape(zl, (1,)).astype(jnp.int32)
    core = jnp.reshape(2 * c + zl, (1,)).astype(jnp.int32)
    shard_pair = 2 * shard_rows

    gains = jnp.broadcast_to(jnp.stack([first_gain, second_gain], 1)[None], (2, shard_rows, 2))
    qkv_shard = jnp.concatenate(
        [halves(query_weight), halves(key_matrix), halves(value_matrix), gains, blank((2, shard_rows, 126))], 2
    )
    qkv_keep, qkv_got = split_core(qkv_shard)
    ffn_shard = jnp.concatenate(
        [halves(gate_weight), halves(output_weight.T), blank((2, shard_rows, 64)), halves(up_weight), halves(down_weight.T)],
        2,
    )
    ffn_keep, ffn_got = split_core(ffn_shard)
    qkv_pair = jnp.concatenate([qkv_keep, qkv_got], 0)
    inputs, out_cotangent, qkv_pair, ffn_keep, ffn_got = sync(inputs, out_cotangent, qkv_pair, ffn_keep, ffn_got)

    qkv_other = flip(qkv_pair, "zh")
    qkv_near = from_groups(qkv_pair)
    x_beside = flip(inputs, "zl")
    ffn_pair = in_order(ffn_keep, ffn_got)
    up_at = half + 2 * HEAD + 64
    first_pair = ffn_pair[:, :up_at]
    up_pair, down_pair = ffn_pair[:, up_at : up_at + half], ffn_pair[:, up_at + half :]
    (
        qkv_near, qkv_other, x_beside, ffn_pair, first_pair, up_pair, down_pair, cos_table, sin_table,
        info, low_wide, high_wide, low_rows, high_rows,
    ) = sync(
        qkv_near, qkv_other, x_beside, ffn_pair, first_pair, up_pair, down_pair, cos_table, sin_table,
        info, low_wide, high_wide, low_rows, high_rows,
    )
    x_near = jnp.concatenate([inputs, x_beside], 0)

    ffn_own = all_groups(ffn_pair)
    qkv_far = from_groups(qkv_other)
    x_far = flip(x_near, "c")
    first_other = flip(first_pair, "zh")
    qkv_far, x_far, first_other, up_pair = sync(qkv_far, x_far, first_other, up_pair)

    up_other = flip(up_pair, "zh")
    k_order = jnp.arange(groups)[:, None]
    piece_rows = (g ^ k_order) * shard_pair + (c ^ jnp.arange(2)[None, :]) * shard_rows
    norm_one, query, kv, qkv_w, gain_rows = project_qkv(
        piece_rows.reshape(-1).astype(jnp.int32),
        [*qkv_near, *qkv_far],
        [inputs, x_beside],
        x_far,
        cos_table,
        sin_table,
    )
    first_piece = lax.dynamic_slice_in_dim(kv, (2 * c + zl) * rows, rows, 0)
    norm_one, query, kv, qkv_w, gain_rows, kv_chunks, first_piece, out_cotangent, up_other, down_pair, first_other = sync(
        norm_one,
        query,
        kv,
        qkv_w,
        gain_rows,
        [kv[n * CHUNK : (n + 1) * CHUNK] for n in range(2)],
        first_piece,
        out_cotangent,
        up_other,
        down_pair,
        first_other,
    )
    first_far = all_groups(first_other)

    def chunk_bases(group, side):
        return jnp.stack([(2 * group + (c ^ i)) * span + side * CHUNK for i in range(2)]).astype(jnp.int32)

    def shift_pairs(steps):
        return [(s, s + steps) for s in range(groups) if 0 <= s + steps < groups and may_meet(s, s + steps, group_tokens, groups)]

    def present(pairs, bases):
        target = functools.reduce(jnp.logical_or, [g == t for _, t in pairs])
        return jnp.where(target, bases, far_away).astype(jnp.int32)

    def reverse(pairs):
        return [(t, s) for s, t in pairs]

    shifts = [d for d in range(1, groups) if shift_pairs(d)]
    above_groups = [s for s in range(1, groups) if may_meet(s - 1, s, group_tokens, groups)]
    above_pairs = [(2 * s, 2 * (s - 1) + 1) for s in above_groups]
    own_bases, other_bases = chunk_bases(g, zh), chunk_bases(g, 1 - zh)
    same_bases = [present(shift_pairs(d), chunk_bases(g - d, zh)) for d in shifts]
    far_bases = [present(shift_pairs(d), chunk_bases(g - d, 1 - zh)) for d in shifts]
    if above_groups:
        is_target = functools.reduce(jnp.logical_or, [(g == s - 1) & (zh == 1) for s in above_groups])
        far_bases.append(jnp.where(is_target, jnp.reshape(2 * (g + 1) * span, (1,)), far_away).astype(jnp.int32))
    same_bases, far_bases = jnp.concatenate(same_bases), jnp.concatenate(far_bases)

    def step(blocks, bases, swap, state, last=False):
        swaps = [swap] * len(blocks)
        return attend(query, low_wide, high_wide, info, bases, zl_info, blocks, swaps, state, last)

    other = [flip(kv_chunks[0], "zh")]
    same = [lax.ppermute(kv, "g", shift_pairs(d)) for d in shifts]
    g_beside, g_across = flip(out_cotangent, "zl"), flip(out_cotangent, "c")
    state = step([kv], own_bases, 0, None)
    other, same, g_beside, g_across, state, kv_late = sync(other, same, g_beside, g_across, state, kv_chunks[1])

    other.append(flip(kv_late, "zh"))
    far_blocks = [[lax.ppermute(other[0], "g", shift_pairs(d))] for d in shifts]
    g_both = flip(g_beside, "c")
    state = step(same, same_bases, 0, state)
    other, far_blocks, g_both, state, down_pair, first_piece, ffn_own = sync(
        other, far_blocks, g_both, state, down_pair, first_piece, ffn_own
    )

    for n, d in enumerate(shifts):
        far_blocks[n].append(lax.ppermute(other[1], "g", shift_pairs(d)))
    far_blocks = [b for pair in far_blocks for b in pair]
    if above_groups:
        above = lax.ppermute(first_piece, ("g", "zh"), above_pairs)
        far_blocks.append(lax.dynamic_update_slice(jnp.zeros((CHUNK, 4 * HEAD), BF), above, (zl * rows, 0)))
    down_other = flip(down_pair, "zh")
    state = step(other, other_bases, 1, state)
    far_blocks, down_other, state = sync(far_blocks, down_other, state)

    second_far = all_groups(jnp.concatenate([up_other, down_other], 1))
    mixed, kept = step(far_blocks, far_bases, 1, state, True)
    mixed, kept, first_far = sync(mixed, kept, first_far)

    o_tile = half // 256
    far_shares, near_shares = output_projection(mixed, (ffn_own, first_far), o_tile)
    across = flip(far_shares, "c")
    beside_sum = add_rows(near_shares, 1, across, 1)
    beside = flip(beside_sum, "zl")
    after_attn, norm_own = sync(*forward_norm(inputs, near_shares, across, beside, gain_rows))

    norm_beside, norm_across = flip(norm_own, "zl"), flip(norm_own, "c")
    near_w = [(ffn_own, 0), (ffn_own, up_at), (ffn_own, up_at + half)]
    far_w = [(first_far, 0), (second_far, 0), (second_far, half)]
    early = feed_forward([norm_own, norm_across], [out_cotangent, g_across], near_w, far_w)
    norm_beside, norm_across, early = sync(norm_beside, norm_across, early)
    norm_both = flip(norm_beside, "c")
    late = feed_forward([norm_beside, norm_both], [g_beside, g_both], near_w, far_w)
    late, norm_both = sync(late, norm_both)

    across_both = flip(late[3], "c")
    beside_sum = add_rows(late[2], 0, across_both, 0)
    beside_sum, late, early = sync(beside_sum, late, early)
    beside = flip(beside_sum, "zl")
    across = flip(early[3], "c")
    out_across = [flip(late[1], "c"), flip(early[1], "c")]
    gate_part = weight_grad([(early[7], late[7], early[5], late[5])], 4)
    beside, across, out_across, gate_part, early, late = sync(beside, across, out_across, gate_part, early, late)
    gate_sum = over_groups(gate_part)
    grad_mid, mid_low = backward_norm(1, early[2], across, beside, after_attn, out_cotangent, gain_rows, [F32, BF])
    grad_mid, mid_low, early, late = sync(grad_mid, mid_low, early, late)

    mid_beside, mid_across = flip(mid_low, "zl"), flip(mid_low, "c")
    up_down_part = weight_grad(
        [(early[7], late[7], early[6], late[6]), (early[8], late[8], early[4], late[4])], 8
    )
    out_sum = add_rows(late[0], 0, out_across[0], 0)
    mid_beside, mid_across, up_down_part, out_sum, early, late = sync(
        mid_beside, mid_across, up_down_part, out_sum, early, late
    )
    up_down_sum = over_groups(up_down_part)
    mid_rows = [mid_low, mid_beside, mid_across, flip(mid_beside, "c")]
    q_aug, o_aug = prepare_back(mid_rows, (ffn_own, first_far), o_tile, kept, query)
    q_aug, o_aug, mid_rows, out_sum, mixed, early, late = sync(q_aug, o_aug, mid_rows, out_sum, mixed, early, late)

    def step_back(blocks, bases, swap, d_query, kinds):
        swaps = [swap] * len(blocks)
        out = attend_back(q_aug, o_aug, low_rows, high_rows, info, bases, zl_info, blocks, swaps, d_query, kinds)
        return out[0], list(out[1:])

    def other_half(summed):
        return flip(summed[:, summed.shape[1] // 2 :], "zh")

    out_beside = flip(out_sum, "zl")
    d_query, d_far = step_back(far_blocks, far_bases, 1, None, [BF] * len(far_blocks))
    o_part = head_grad(mid_rows, mixed)
    second_column = gain_columns([early[2], late[2], early[3], late[3]], [norm_own, norm_beside, norm_across, norm_both], 1)
    out_beside, d_query, d_far, o_part, gate_sum, second_column = sync(
        out_beside, d_query, d_far, o_part, gate_sum, second_column
    )
    o_sum = over_groups(o_part)

    back = [lax.ppermute(d_far[2 * n + m], "g", reverse(shift_pairs(d))) for n, d in enumerate(shifts) for m in range(2)]
    gate_far = other_half(gate_sum)
    d_query, d_other = step_back(other, other_bases, 1, d_query, [BF] * 2)
    other_sum = [d_other[m].astype(F32) for m in range(2)]
    for n in range(len(shifts)):
        for m in range(2):
            other_sum[m] = other_sum[m] + back[2 * n + m].astype(F32)
    other_sum = [o.astype(BF) for o in other_sum]
    d_query, other_sum, gate_far = sync(d_query, other_sum, gate_far)

    other_back = [flip(other_sum[0], "zh")]
    d_query, d_same = step_back(same, same_bases, 0, d_query, [BF] * len(same))
    d_query, d_same, other_back, d_far, other_late = sync(d_query, d_same, other_back, d_far, other_sum[1])

    other_back.append(flip(other_late, "zh"))
    same_back = [lax.ppermute(d_same[n], "g", reverse(shift_pairs(d))) for n, d in enumerate(shifts)]
    d_query, d_own = step_back([kv], own_bases, 0, d_query, [F32])
    d_q, shares = query_back(core, d_query, qkv_w, cos_table, sin_table)
    q_part = head_grad([norm_one[k] for k in range(4)], d_q)
    above_back = []
    if above_groups:
        above = lax.dynamic_slice_in_dim(d_far[-1], zl * rows, rows, 0)
        above_back.append(lax.ppermute(above, ("g", "zh"), reverse(above_pairs)))
    other_back, same_back, above_back, d_own, d_q, shares, q_part, up_down_sum = sync(
        other_back, same_back, above_back, d_own, d_q, shares, q_part, up_down_sum
    )

    d_kvs, shares = kv_back(core, d_own[0], other_back, same_back, above_back, shares, qkv_w, cos_table, sin_table)
    share_rows = shares.reshape(span, width)
    across = flip(share_rows[2 * rows :], "c")
    kv_part = kv_grad(norm_one, shares, d_kvs, second_column)
    beside_sum = add_rows(share_rows, 1, across, 1)
    def group_slice(part, k):
        return lax.dynamic_slice_in_dim(part, (g ^ k) * shard_pair, shard_pair, 0)

    def one_hop(k):
        return k & -k == k

    q_got = {k: flip(group_slice(q_part, k), "g", k) for k in range(1, groups) if one_hop(k)}
    up_far = flip(up_down_sum[:, 2 * half : 3 * half], "zh")
    beside_sum, kv_part, across, share_rows, up_far, o_sum, q_got, q_part, gate_far, gate_sum, up_down_sum = sync(
        beside_sum, kv_part, across, share_rows, up_far, o_sum, q_got, q_part, gate_far, gate_sum, up_down_sum
    )

    kv_got = [flip(group_slice(kv_part, k), "g", k) for k in range(1, groups) if one_hop(k)]
    diagonal = [
        flip(jnp.concatenate([group_slice(kv_part, k), group_slice(q_part, k)], 1), "g", k)
        for k in range(1, groups)
        if not one_hop(k)
    ]
    beside = flip(beside_sum, "zl")
    do_far = flip(jnp.concatenate([up_down_sum[:, 3 * half :], o_sum[:, 256:]], 1), "zh")
    kv_got, diagonal, beside, do_far, up_far, gate_far = sync(kv_got, diagonal, beside, do_far, up_far, gate_far)

    kv_sum = group_slice(kv_part, 0).astype(F32) + sum(v.astype(F32) for v in kv_got)
    q_sum = group_slice(q_part, 0).astype(F32) + sum(v.astype(F32) for v in q_got.values())
    for value in diagonal:
        kv_sum, q_sum = kv_sum + value[:, :512].astype(F32), q_sum + value[:, 512:].astype(F32)
    kvq_own = jnp.concatenate([kv_sum[:, :256], q_sum[:, :256]], 1)
    kvq_give = jnp.concatenate([kv_sum[:, 256:], q_sum[:, 256:]], 1).astype(BF)
    kvq_own, kvq_give, do_far, beside, gate_far = sync(kvq_own, kvq_give, do_far, beside, gate_far)
    kvq_far = flip(kvq_give, "zh")
    [input_grad] = backward_norm(0, share_rows, across, beside, inputs, grad_mid, gain_rows, [BF])
    gate_up = jnp.concatenate([gate_sum[:, :half], up_down_sum[:, :half]], 1).astype(F32)
    gu_own, gu_got = to_owner(gate_up + jnp.concatenate([gate_far, up_far], 1).astype(F32))
    do_own = jnp.concatenate([up_down_sum[:, half : 2 * half], o_sum[:, :256]], 1)
    do_own, do_got = to_owner(do_own.astype(F32) + do_far.astype(F32))
    layer_out = (after_attn + (early[0].astype(F32) + out_across[1].astype(F32) + out_beside.astype(F32))).astype(BF)
    kvq_far, do_own, do_got, gu_own, gu_got, input_grad, layer_out = sync(
        kvq_far, do_own, do_got, gu_own, gu_got, input_grad, layer_out
    )

    kvq_own, kvq_got = to_owner(kvq_own + kvq_far.astype(F32))
    gain_sums = (kvq_own + kvq_got)[:, 2 * HEAD : 2 * HEAD + 2]
    gain_sums = gain_sums + flip(gain_sums, "zl")

    def columns(own, got, start, size):
        return in_order(own[:, start : start + size], got[:, start : start + size], 1)

    return (
        layer_out,
        input_grad,
        gain_sums[:, 0] / first_gain.astype(F32),
        columns(kvq_own, kvq_got, 256, 2 * HEAD),
        columns(kvq_own, kvq_got, 0, HEAD),
        columns(kvq_own, kvq_got, HEAD, HEAD),
        columns(do_own, do_got, half, 2 * HEAD).T,
        gain_sums[:, 1] / second_gain.astype(F32),
        columns(gu_own, gu_got, 0, half),
        columns(gu_own, gu_got, half, half),
        columns(do_own, do_got, 0, half).T,
    )


def solution(mesh):
    outer, inner = mesh.devices.shape
    fine = Mesh(mesh.devices.reshape(outer // 2, 2, inner // 2, 2), AXES)
    data, tensor = ("g", "c"), ("zh", "zl")
    rows, first = P(AXES, None), P(data)
    wide, tall = P(data, tensor), P(tensor, data)
    return jax.shard_map(
        body,
        mesh=fine,
        in_specs=(rows, first, wide, wide, wide, tall, first, wide, wide, tall, P(), P(), rows),
        out_specs=(rows, rows, first, wide, wide, wide, tall, first, wide, wide, tall),
        check_vma=False,
    )
```

time: 681 us -> 610 us (0.90)
  waiting for transfers between devices: 302 us -> 214 us
  Pallas kernels: 103 us -> 175 us
  matrix products: 37.2 us -> 0 us
  starting transfers between devices: 99.1 us -> 71 us
  other arithmetic: 59.9 us -> 34.4 us
  local copies, waits for them, and re-layouts: 66.1 us -> 89.9 us
  between operations: 2.71 us -> 15.9 us
    ppermute x67 -> x50, waiting for transfers between devices: 273 us -> 172 us  [flip(): return lax.ppermute(value, axis, [(s, s ^ bit) for s in range(count)])]
    pallas_call x8 -> x28, Pallas kernels: 103 us -> 175 us  [the longest x4 38.9 us: attend_back(): pl.pallas_call(functools.partial(backward_kernel, swaps, d_query is not N...]
    ppermute x67 -> x50, starting transfers between devices: 88.4 us -> 48.9 us  [flip(): return lax.ppermute(value, axis, [(s, s ^ bit) for s in range(count)])]
    unnamed x191 -> x217, local copies, waits for them, and re-layouts: 20 us -> 58.2 us
    dot_general x26 -> x0, matrix products: 37.2 us -> none  [the longest x16 27.5 us: tn(): lax.dot_general(left, right, (((0,), (0,)), ((), ())), preferred_element_...]
    another operation x17 -> x3, other arithmetic: 19.2 us -> 0.16 us  [the longest x2 0.15 us: chunk_bases(): jnp.stack([(2 * group + (c ^ i)) * span + side * CHUNK for i in range(2)])]
    ppermute x6 -> x8, starting transfers between devices: 10.7 us -> 21.8 us  [the longest x1 5.24 us: body(): far_blocks = [[lax.ppermute(other[0], 'g', shift_pairs(d))] for d in shifts]]
    slice x23 -> x29, local copies, waits for them, and re-layouts: 5.53 us -> 14.1 us  [the longest x1 2.2 us: body(): up_down_sum[:, :half]]
  transfers between devices with their start and end apart: 73 -> 64, of which waited for: 30 -> 30; matrix products, arithmetic and copies ran while one was open for 21% -> 8% of each run, Pallas kernels for 15% -> 26%
where the time goes in v2:
time: 610 us; the launch traced here: 600 us
  waiting for transfers between devices  214 us (35%)
  Pallas kernels  175 us (29%)
  local copies, waits for them, and re-layouts  89.9 us (15%)
  starting transfers between devices  71 us (12%)
  other arithmetic  34.4 us (6%)
  between operations  15.9 us (3%)
    ppermute x50, waiting for transfers between devices, flip(): return lax.ppermute(value, axis, [(s, s ^ bit) for s in range(count)])  172 us
    unnamed x217, local copies, waits for them, and re-layouts  58.2 us
    ppermute x50, starting transfers between devices, flip(): return lax.ppermute(value, axis, [(s, s ^ bit) for s in range(count)])  48.9 us
    pallas_call x4, Pallas kernels, attend_back(): pl.pallas_call(functools.partial(backward_kernel, swaps, d_query is not N...  38.9 us
    pallas_call x2, Pallas kernels, feed_forward(): pl.pallas_call(functools.partial(ffn_kernel, tiles), grid=(2 * tiles,), i...  35.6 us
    ppermute x2, waiting for transfers between devices, body(): lax.ppermute(d_far[2 * n + m], 'g', reverse(shift_pairs(d)))  28.7 us
    pallas_call x4, Pallas kernels, attend(): pl.pallas_call(functools.partial(forward_kernel, swaps, state is None, la...  26.1 us
    pallas_call x2, Pallas kernels, weight_grad(): pl.pallas_call(functools.partial(weight_grad_kernel, count), grid=(2, cou...  16.5 us
  transfers between devices with their start and end apart: 64, of which 30 were waited for; matrix products, arithmetic and copies ran while one was open for 8% of the time, Pallas kernels for 26%

profile of v2, /device:TPU:0, one launch (start us, length us, event | category | flops | bytes accessed | tf_op | source)
XLA Modules:
  0.0 600.0 jit_solution(18171278109396201517)
XLA Ops:
  39.1 6.7 %collective-permute-done.3.refs_2_ = bf16[384,512]{1,0:T(8,128)(2,1)S(1)} collective-permute-done((bf16[384,512]{1,0:T(8,128)(2,1)S(1)}, bf16[384,512]{1,0:T(8,128)(2,1)S(1)}, u32[]{:S(2)}, u32[]{:S(2)}) %collective-permute-start.3) | collective-permute-done | bytes 393248 | tf_op jit(solution)/shard_map/ppermute | solution.py:61
  60.1 13.7 %collective-permute-done.7.refs_5_ = bf16[384,512]{1,0:T(8,128)(2,1)S(1)} collective-permute-done((bf16[384,512]{1,0:T(8,128)(2,1)}, bf16[384,512]{1,0:T(8,128)(2,1)S(1)}, u32[]{:S(2)}, u32[]{:S(2)}) %collective-permute-start.7) | collective-permute-done | bytes 393248 | tf_op jit(solution)/shard_map/ppermute | solution.py:61
  79.6 11.2 %collective-permute-done.9.refs_7_ = bf16[384,512]{1,0:T(8,128)(2,1)S(1)} collective-permute-done((bf16[384,512]{1,0:T(8,128)(2,1)}, bf16[384,512]{1,0:T(8,128)(2,1)S(1)}, u32[]{:S(2)}, u32[]{:S(2)}) %collective-permute-start.9) | collective-permute-done | bytes 393248 | tf_op jit(solution)/shard_map/ppermute | solution.py:61
  96.6 11.9 %project_qkv.1 = (bf16[4,256,1536]{2,1,0:T(8,128)(2,1)}, bf16[2,4,512,128]{3,2,1,0:T(8,128)(2,1)}, bf16[1024,384]{1,0:T(8,128)(2,1)}, bf16[2,1536,512]{2,1,0:T(8,128)(2,1)}, f32[8,1536]{1,0:T(8,128)S(1)}) custom-call(s32[8]{0:T(128)S(1)} %add.262.where_ref, bf16[384,512]{1,0:T(8,128)(2,1)S(1)} %pad_maximum_fusion.5.refs_0_, bf16[384,512]{1,0:T(8,128)(2,1)S(1)} %copy-done.70, ...), custom_call_target="tpu_custom_call" | custom-call | flops 92000000 | bytes 288000 | tf_op jit(solution)/shard_map/project_qkv/pallas_call | solution.py:173
  122.1 8.9 %attend.4.refs_4_ = f32[2,4,512,128]{3,2,1,0:T(8,128)S(1)} custom-call(s32[4,4]{1,0:T(4,128)S(1)} %pad_add_fusion.info_ref, s32[2]{0:T(128)S(1)} %pad_add_fusion.2.base_ref, s32[1]{0:T(128)} %bitcast.20.zl_ref, bf16[2,4,512,128]{3,2,1,0:T(8,128)(2,1)S(1)} %copy-done.3, s32[4,256,128]{2,1,0:T(8,128)S(1)} %broadcast_in_dim.114.refs_1_, ...), custom_call_target="tpu_custom_call" | custom-call | flops 117760000 | bytes 368640 | tf_op jit(solution)/shard_map/attend/pallas_call | solution.py:392
  132.4 10.6 %collective-permute-done.13.refs_3_.refs_4_ = bf16[512,384]{1,0:T(8,128)(2,1)S(1)} collective-permute-done((bf16[512,384]{1,0:T(8,128)(2,1)}, bf16[512,384]{1,0:T(8,128)(2,1)S(1)}, u32[]{:S(2)}, u32[]{:S(2)}) %collective-permute-start.13) | collective-permute-done | bytes 393248 | tf_op jit(solution)/shard_map/ppermute | solution.py:61
  157.5 7.3 %collective-permute-done.17.refs_4_.refs_5_ = bf16[512,384]{1,0:T(8,128)(2,1)} collective-permute-done((bf16[512,384]{1,0:T(8,128)(2,1)}, bf16[512,384]{1,0:T(8,128)(2,1)}, u32[]{:S(2)}, u32[]{:S(2)}) %collective-permute-start.17) | collective-permute-done | bytes 393248 | tf_op jit(solution)/shard_map/ppermute | solution.py:61
  211.8 19.6 %collective-permute-done.24.beside_ref = bf16[256,1536]{1,0:T(8,128)(2,1)S(1)} collective-permute-done((bf16[256,1536]{1,0:T(8,128)(2,1)S(1)}, bf16[256,1536]{1,0:T(8,128)(2,1)S(1)}, u32[]{:S(2)}, u32[]{:S(2)}) %collective-permute-start.24) | collective-permute-done | bytes 786464 | tf_op jit(solution)/shard_map/ppermute | solution.py:61
  235.6 6.8 %all-gather.8.cloned.1.call-done.refs_4_.refs_5_ = bf16[1536,1024]{1,0:T(8,128)(2,1)} async-done(((bf16[384,1024]{1,0:T(8,128)(2,1)}), bf16[1536,1024]{1,0:T(8,128)(2,1)}) %all-gather.8.cloned.1.call-update) | async-done | bytes 3145744 | tf_op jit(solution)/shard_map/all_gather | solution.py:56
  242.4 17.7 %feed_forward.2 = (bf16[256,1536]{1,0:T(8,128)(2,1)}, bf16[256,1536]{1,0:T(8,128)(2,1)}, bf16[256,1536]{1,0:T(8,128)(2,1)}, bf16[256,1536]{1,0:T(8,128)(2,1)}, b...) custom-call(bf16[256,1536]{1,0:T(8,128)(2,1)} %copy-done.33, ...), custom_call_target="tpu_custom_call" | custom-call | flops 207000000 | bytes 648000 | tf_op jit(solution)/shard_map/feed_forward/pallas_call | solution.py:641
  263.4 17.9 %feed_forward.3 = (bf16[256,1536]{1,0:T(8,128)(2,1)}, bf16[256,1536]{1,0:T(8,128)(2,1)}, bf16[256,1536]{1,0:T(8,128)(2,1)}, bf16[256,1536]{1,0:T(8,128)(2,1)}, b...) custom-call(bf16[256,1536]{1,0:T(8,128)(2,1)} %copy-done.37, ...), custom_call_target="tpu_custom_call" | custom-call | flops 207000000 | bytes 648000 | tf_op jit(solution)/shard_map/feed_forward/pallas_call | solution.py:641
  295.8 10.3 %collective-permute-done.29.beside_ref = bf16[256,1536]{1,0:T(8,128)(2,1)} collective-permute-done((bf16[256,1536]{1,0:T(8,128)(2,1)}, bf16[256,1536]{1,0:T(8,128)(2,1)}, u32[]{:S(2)}, u32[]{:S(2)}) %collective-permute-start.29) | collective-permute-done | bytes 786464 | tf_op jit(solution)/shard_map/ppermute | solution.py:61
  316.6 11.5 %weight_grad.3 = bf16[1536,2048]{1,0:T(8,128)(2,1)} custom-call(bf16[1536,512]{1,0:T(8,128)(2,1)S(1)} %copy-done.20, bf16[1536,512]{1,0:T(8,128)(2,1)} %get-tuple-element.420.refs_1_, bf16[512,1024]{1,0:T(8,128)(2,1)S(1)} %copy-done.58, bf16[512,1024]{1,0:T(8,128)(2,1)S(1)} %copy-done.60, bf16[1536,512]{1,0:T(8,128)(2,1)} %get-tuple-element.423.refs_4_, ...), custom_call_target="tpu_custom_call" | custom-call | flops 92000000 | bytes 288000 | tf_op jit(solution)/shard_map/weight_grad/pallas_call | solution.py:673
  338.2 8.5 %prepare_back.1 = (bf16[2,4,512,128]{3,2,1,0:T(8,128)(2,1)S(1)}, bf16[2,4,512,128]{3,2,1,0:T(8,128)(2,1)S(1)}) custom-call(bf16[256,1536]{1,0:T(8,128)(2,1)} %get-tuple-element.454.m0.l0, bf16[256,1536]{1,0:T(8,128)(2,1)S(1)} %copy-done.50, bf16[256,1536]{1,0:T(8,128)(2,1)} %collective-permute-done.34.m2.l2, ...), custom_call_target="tpu_custom_call" | custom-call | flops 69000000 | bytes 216000 | tf_op jit(solution)/shard_map/prepare_back/pallas_call | solution.py:453
  362.3 7.0 %attend_back.4 = (f32[2,4,512,128]{3,2,1,0:T(8,128)}, bf16[512,384]{1,0:T(8,128)(2,1)}, bf16[512,384]{1,0:T(8,128)(2,1)}, bf16[512,384]{1,0:T(8,128)(2,1)}) custom-call(s32[4,4]{1,0:T(4,128)} %copy-done.81, s32[3]{0:T(128)} %copy-done.85, s32[1]{0:T(128)} %bitcast.20.zl_ref, bf16[2,4,512,128]{3,2,1,0:T(8,128)(2,1)} %copy-done.4, ...), custom_call_target="tpu_custom_call" | custom-call | flops 276000000 | bytes 864000 | tf_op jit(solution)/shard_map/attend_back/pallas_call | solution.py:548
  376.7 9.4 %attend_back.5 = (f32[2,4,512,128]{3,2,1,0:T(8,128)}, bf16[512,384]{1,0:T(8,128)(2,1)}, bf16[512,384]{1,0:T(8,128)(2,1)}) custom-call(s32[4,4]{1,0:T(4,128)} %copy-done.81, s32[2]{0:T(128)} %copy-done.84, s32[1]{0:T(128)} %bitcast.20.zl_ref, bf16[2,4,512,128]{3,2,1,0:T(8,128)(2,1)} %copy-done.4, bf16[2,4,512,128]{3,2,1,0:T(8,128)(2,1)} %copy-done.5, ...), custom_call_target="tpu_custom_call" | custom-call | flops 184000000 | bytes 576000 | tf_op jit(solution)/shard_map/attend_back/pallas_call | solution.py:548
  386.1 21.5 %collective-permute-done.38 = bf16[512,384]{1,0:T(8,128)(2,1)S(1)} collective-permute-done((bf16[512,384]{1,0:T(8,128)(2,1)}, bf16[512,384]{1,0:T(8,128)(2,1)S(1)}, u32[]{:S(2)}, u32[]{:S(2)}) %collective-permute-start.38) | collective-permute-done | bytes 393248 | tf_op jit(solution)/shard_map/ppermute | solution.py:1131
  409.4 7.3 %collective-permute-done.37 = bf16[512,384]{1,0:T(8,128)(2,1)S(1)} collective-permute-done((bf16[512,384]{1,0:T(8,128)(2,1)}, bf16[512,384]{1,0:T(8,128)(2,1)S(1)}, u32[]{:S(2)}, u32[]{:S(2)}) %collective-permute-start.37) | collective-permute-done | bytes 393248 | tf_op jit(solution)/shard_map/ppermute | solution.py:1131
  420.3 6.6 %attend_back.6 = (f32[2,4,512,128]{3,2,1,0:T(8,128)}, bf16[1024,384]{1,0:T(8,128)(2,1)}) custom-call(s32[4,4]{1,0:T(4,128)} %copy-done.81, s32[2]{0:T(128)} %copy-done.82, s32[1]{0:T(128)} %bitcast.20.zl_ref, bf16[2,4,512,128]{3,2,1,0:T(8,128)(2,1)} %copy-done.4, bf16[2,4,512,128]{3,2,1,0:T(8,128)(2,1)} %copy-done.5, ...), custom_call_target="tpu_custom_call" | custom-call | flops 184000000 | bytes 576000 | tf_op jit(solution)/shard_map/attend_back/pallas_call | solution.py:548
  426.9 11.2 %collective-permute-done.40.refs_1_ = bf16[512,384]{1,0:T(8,128)(2,1)S(1)} collective-permute-done((bf16[512,384]{1,0:T(8,128)(2,1)S(1)}, bf16[512,384]{1,0:T(8,128)(2,1)S(1)}, u32[]{:S(2)}, u32[]{:S(2)}) %collective-permute-start.40) | collective-permute-done | bytes 393248 | tf_op jit(solution)/shard_map/ppermute | solution.py:61
  447.9 15.9 %attend_back.7 = (f32[2,4,512,128]{3,2,1,0:T(8,128)}, f32[1024,384]{1,0:T(8,128)}) custom-call(s32[4,4]{1,0:T(4,128)} %copy-done.81, s32[2]{0:T(128)} %copy-done.83, s32[1]{0:T(128)} %bitcast.20.zl_ref, bf16[2,4,512,128]{3,2,1,0:T(8,128)(2,1)} %copy-done.4, bf16[2,4,512,128]{3,2,1,0:T(8,128)(2,1)} %copy-done.5, s32[4,8,512]{2,1,0:T(8,128)} %broadcast_in_dim.116.refs_2_, ...), custom_call_target="tpu_custom_call" | custom-call | flops 184000000 | bytes 576000 | tf_op jit(solution)/shard_map/attend_back/pallas_call | solution.py:548
  504.7 9.8 %collective-permute-done.45 = bf16[384,512]{1,0:T(8,128)(2,1)} collective-permute-done((bf16[384,512]{1,0:T(8,128)(2,1)}, bf16[384,512]{1,0:T(8,128)(2,1)}, u32[]{:S(2)}, u32[]{:S(2)}) %collective-permute-start.45) | collective-permute-done | bytes 393248 | tf_op jit(solution)/shard_map/ppermute | solution.py:61
  525.0 24.2 %collective-permute-done.48 = bf16[384,512]{1,0:T(8,128)(2,1)} collective-permute-done((bf16[384,512]{1,0:T(8,128)(2,1)}, bf16[384,512]{1,0:T(8,128)(2,1)}, u32[]{:S(2)}, u32[]{:S(2)}) %collective-permute-start.48) | collective-permute-done | bytes 393248 | tf_op jit(solution)/shard_map/ppermute | solution.py:61
  568.6 12.6 %collective-permute-done.53 = bf16[384,512]{1,0:T(8,128)(2,1)S(1)} collective-permute-done((bf16[384,512]{1,0:T(8,128)(2,1)S(1)}, bf16[384,512]{1,0:T(8,128)(2,1)S(1)}, u32[]{:S(2)}, u32[]{:S(2)}) %collective-permute-start.53) | collective-permute-done | bytes 393248 | tf_op jit(solution)/shard_map/ppermute | solution.py:61
  (479 shorter events, 296.1 us)
Async XLA Ops:
  7.2 157.7 %all-gather.4.cloned.1.call-start = ((), (), s32[]{:S(2)}) async-start(), calls=%async_computation.3 | async-start | bytes 6881280 | tf_op jit(solution)/shard_map/all_gather | solution.py:56
  20.4 29.3 %collective-permute-start.6 = (bf16[256,1536]{1,0:T(8,128)(2,1)S(1)}, bf16[256,1536]{1,0:T(8,128)(2,1)}, u32[]{:S(2)}, u32[]{:S(2)}) collective-permute-start(bf16[256,1536]{1,0:T(8,128)(2,1)S(1)} %copy-done.9), channel_id=1, source_target_pairs={{0,1},{1,0},{2,3},{3,2},{4,5},{5,4},{6,7},{7,6},{8,9},{9,8},{10,11... | collective-permute-start | bytes 2359304 | tf_op jit(solution)/shard_map/ppermute | solution.py:61
  51.4 148.5 %all-gather.6.cloned.1.call-start = ((), (), s32[]{:S(2)}) async-start(), calls=%async_computation.4 | async-start | bytes 2949120 | tf_op jit(solution)/shard_map/all_gather | solution.py:56
  54.0 37.5 %collective-permute-start.10 = (bf16[512,1536]{1,0:T(8,128)(2,1)}, bf16[512,1536]{1,0:T(8,128)(2,1)}, u32[]{:S(2)}, u32[]{:S(2)}) collective-permute-start(bf16[512,1536]{1,0:T(8,128)(2,1)} %pad_maximum_fusion), channel_id=1, source_target_pairs={{0,4},{4,0},{1,5},{5,1},{2,6},{6,2},{3,7},{7,3},{8,12},{12,8},{9,1... | collective-permute-start | bytes 4718600 | tf_op jit(solution)/shard_map/ppermute | solution.py:61
  54.0 37.5 %collective-permute-start.11 = (bf16[384,768]{1,0:T(8,128)(2,1)S(1)}, bf16[384,768]{1,0:T(8,128)(2,1)}, u32[]{:S(2)}, u32[]{:S(2)}) collective-permute-start(bf16[384,768]{1,0:T(8,128)(2,1)S(1)} %copy-done.93), channel_id=1, source_target_pairs={{0,2},{2,0},{1,3},{3,1},{4,6},{6,4},{5,7},{7,5},{8,10},{10,8},{9,1... | collective-permute-start | bytes 1769480 | tf_op jit(solution)/shard_map/ppermute | solution.py:61
  59.6 31.1 %collective-permute-start.9 = (bf16[384,512]{1,0:T(8,128)(2,1)}, bf16[384,512]{1,0:T(8,128)(2,1)S(1)}, u32[]{:S(2)}, u32[]{:S(2)}) collective-permute-start(bf16[384,512]{1,0:T(8,128)(2,1)} %collective-permute-done.5.refs_4_), channel_id=1, source_target_pairs={{0,24},{8,16},{16,8},{24,0},{1,25},{9,17},{17,9},{25,1},{2,26},{10... | collective-permute-start | bytes 1179656 | tf_op jit(solution)/shard_map/ppermute | solution.py:61
  112.4 130.0 %all-gather.8.cloned.1.call-start = ((), (), s32[]{:S(2)}) async-start(), calls=%async_computation.5 | async-start | bytes 3932160 | tf_op jit(solution)/shard_map/all_gather | solution.py:56
  112.5 31.1 %collective-permute-start.14 = (bf16[1024,384]{1,0:T(8,128)(2,1)}, bf16[1024,384]{1,0:T(8,128)(2,1)}, u32[]{:S(2)}, u32[]{:S(2)}) collective-permute-start(bf16[1024,384]{1,0:T(8,128)(2,1)} %get-tuple-element.308.refs_3_.refs_4_), channel_id=1, source_target_pairs={{0,8},{1,9},{2,10},{3,11},{4,12},{5,13},{6,14},{7,15}} | collective-permute-start | bytes 2359304 | tf_op jit(solution)/shard_map/ppermute | solution.py:1046
  117.4 26.3 %collective-permute-start.15 = (bf16[256,1536]{1,0:T(8,128)(2,1)}, bf16[256,1536]{1,0:T(8,128)(2,1)}, u32[]{:S(2)}, u32[]{:S(2)}) collective-permute-start(bf16[256,1536]{1,0:T(8,128)(2,1)} %base_ref), channel_id=1, source_target_pairs={{0,1},{1,0},{2,3},{3,2},{4,5},{5,4},{6,7},{7,6},{8,9},{9,8},{10,11... | collective-permute-start | bytes 2359304 | tf_op jit(solution)/shard_map/ppermute | solution.py:61
  192.1 177.2 %reduce-scatter.4.cloned.1.call-start = ((), (), s32[]{:S(2)}) async-start(), calls=%async_computation.6 | async-start | bytes 3932160 | tf_op jit(solution)/shard_map/reduce_scatter | solution.py:97
  233.3 26.8 %collective-permute-start.25 = (bf16[256,1536]{1,0:T(8,128)(2,1)S(1)}, bf16[256,1536]{1,0:T(8,128)(2,1)S(1)}, u32[]{:S(2)}, u32[]{:S(2)}) collective-permute-start(bf16[256,1536]{1,0:T(8,128)(2,1)S(1)} %get-tuple-element.338.n0.refs_4_), channel_id=1, source_target_pairs={{0,1},{1,0},{2,3},{3,2},{4,5},{5,4},{6,7},{7,6},{8,9},{9,8},{10,11... | collective-permute-start | bytes 2359304 | tf_op jit(solution)/shard_map/ppermute | solution.py:61
  306.1 168.9 %reduce-scatter.6.cloned.1.call-start = ((), (), s32[]{:S(2)}) async-start(), calls=%async_computation.7 | async-start | bytes 7864320 | tf_op jit(solution)/shard_map/reduce_scatter | solution.py:97
  332.8 171.9 %reduce-scatter.8.cloned.1.call-start = ((), (), s32[]{:S(2)}) async-start(), calls=%async_computation.8 | async-start | bytes 1966080 | tf_op jit(solution)/shard_map/reduce_scatter | solution.py:97
  369.4 38.2 %collective-permute-start.38 = (bf16[512,384]{1,0:T(8,128)(2,1)}, bf16[512,384]{1,0:T(8,128)(2,1)S(1)}, u32[]{:S(2)}, u32[]{:S(2)}) collective-permute-start(bf16[512,384]{1,0:T(8,128)(2,1)} %get-tuple-element.471), channel_id=1, source_target_pairs={{8,0},{9,1},{10,2},{11,3},{12,4},{13,5},{14,6},{15,7}} | collective-permute-start | bytes 1179656 | tf_op jit(solution)/shard_map/ppermute | solution.py:1131
  370.7 46.0 %collective-permute-start.37 = (bf16[512,384]{1,0:T(8,128)(2,1)}, bf16[512,384]{1,0:T(8,128)(2,1)S(1)}, u32[]{:S(2)}, u32[]{:S(2)}) collective-permute-start(bf16[512,384]{1,0:T(8,128)(2,1)} %get-tuple-element.469), channel_id=1, source_target_pairs={{8,0},{9,1},{10,2},{11,3},{12,4},{13,5},{14,6},{15,7}} | collective-permute-start | bytes 1179656 | tf_op jit(solution)/shard_map/ppermute | solution.py:1131
  373.1 44.7 %collective-permute-start.39 = (bf16[384,512]{1,0:T(8,128)(2,1)S(1)}, bf16[384,512]{1,0:T(8,128)(2,1)S(1)}, u32[]{:S(2)}, u32[]{:S(2)}) collective-permute-start(bf16[384,512]{1,0:T(8,128)(2,1)S(1)} %slice.133), channel_id=1, source_target_pairs={{0,2},{2,0},{1,3},{3,1},{4,6},{6,4},{5,7},{7,5},{8,10},{10,8},{9,1... | collective-permute-start | bytes 1179656 | tf_op jit(solution)/shard_map/ppermute | solution.py:61
  438.1 36.1 %collective-permute-start.42 = (bf16[1024,384]{1,0:T(8,128)(2,1)}, bf16[1024,384]{1,0:T(8,128)(2,1)S(1)}, u32[]{:S(2)}, u32[]{:S(2)}) collective-permute-start(bf16[1024,384]{1,0:T(8,128)(2,1)} %get-tuple-element.481), channel_id=1, source_target_pairs={{8,0},{9,1},{10,2},{11,3},{12,4},{13,5},{14,6},{15,7}} | collective-permute-start | bytes 2359304 | tf_op jit(solution)/shard_map/ppermute | solution.py:1146
  440.1 34.1 %collective-permute-start.43 = (bf16[256,384]{1,0:T(8,128)(2,1)}, bf16[256,384]{1,0:T(8,128)(2,1)}, u32[]{:S(2)}, u32[]{:S(2)}) collective-permute-start(bf16[256,384]{1,0:T(8,128)(2,1)} %constant_dynamic-slice_fusion.8), channel_id=1, source_target_pairs={{2,8},{3,9},{6,12},{7,13}} | collective-permute-start | bytes 589832 | tf_op jit(solution)/shard_map/ppermute | solution.py:1153
  441.4 32.7 %collective-permute-start.41 = (bf16[512,384]{1,0:T(8,128)(2,1)}, bf16[512,384]{1,0:T(8,128)(2,1)}, u32[]{:S(2)}, u32[]{:S(2)}) collective-permute-start(bf16[512,384]{1,0:T(8,128)(2,1)} %add_convert_fusion.1), channel_id=1, source_target_pairs={{0,2},{2,0},{1,3},{3,1},{4,6},{6,4},{5,7},{7,5},{8,10},{10,8},{9,1... | collective-permute-start | bytes 1179656 | tf_op jit(solution)/shard_map/ppermute | solution.py:61
  519.8 32.9 %collective-permute-start.50 = (bf16[384,1024]{1,0:T(8,128)(2,1)}, bf16[384,1024]{1,0:T(8,128)(2,1)}, u32[]{:S(2)}, u32[]{:S(2)}) collective-permute-start(bf16[384,1024]{1,0:T(8,128)(2,1)} %pad_maximum_fusion.2), channel_id=1, source_target_pairs={{0,24},{8,16},{16,8},{24,0},{1,25},{9,17},{17,9},{25,1},{2,26},{10... | collective-permute-start | bytes 2359304 | tf_op jit(solution)/shard_map/ppermute | solution.py:61
  522.7 32.1 %collective-permute-start.51 = (bf16[256,1536]{1,0:T(8,128)(2,1)}, bf16[256,1536]{1,0:T(8,128)(2,1)}, u32[]{:S(2)}, u32[]{:S(2)}) collective-permute-start(bf16[256,1536]{1,0:T(8,128)(2,1)} %add_rows.7), channel_id=1, source_target_pairs={{0,1},{1,0},{2,3},{3,2},{4,5},{5,4},{6,7},{7,6},{8,9},{9,8},{10,11... | collective-permute-start | bytes 2359304 | tf_op jit(solution)/shard_map/ppermute | solution.py:61
  523.6 29.0 %collective-permute-start.52 = (bf16[384,768]{1,0:T(8,128)(2,1)}, bf16[384,768]{1,0:T(8,128)(2,1)}, u32[]{:S(2)}, u32[]{:S(2)}) collective-permute-start(bf16[384,768]{1,0:T(8,128)(2,1)} %pad_maximum_fusion.4), channel_id=1, source_target_pairs={{0,2},{2,0},{1,3},{3,1},{4,6},{6,4},{5,7},{7,5},{8,10},{10,8},{9,1... | collective-permute-start | bytes 1769480 | tf_op jit(solution)/shard_map/ppermute | solution.py:61
  524.4 24.8 %collective-permute-start.48 = (bf16[384,512]{1,0:T(8,128)(2,1)}, bf16[384,512]{1,0:T(8,128)(2,1)}, u32[]{:S(2)}, u32[]{:S(2)}) collective-permute-start(bf16[384,512]{1,0:T(8,128)(2,1)} %get-tuple-element.557), channel_id=1, source_target_pairs={{0,8},{8,0},{16,24},{24,16},{1,9},{9,1},{17,25},{25,17},{2,10},{10... | collective-permute-start | bytes 1179656 | tf_op jit(solution)/shard_map/ppermute | solution.py:61
  524.7 24.5 %collective-permute-start.49 = (bf16[384,512]{1,0:T(8,128)(2,1)}, bf16[384,512]{1,0:T(8,128)(2,1)}, u32[]{:S(2)}, u32[]{:S(2)}) collective-permute-start(bf16[384,512]{1,0:T(8,128)(2,1)} %get-tuple-element.556), channel_id=1, source_target_pairs={{0,16},{8,24},{16,0},{24,8},{1,17},{9,25},{17,1},{25,9},{2,18},{10... | collective-permute-start | bytes 1179656 | tf_op jit(solution)/shard_map/ppermute | solution.py:61
  (151 other events, 1399.3 us)
Sparse Core Ops, SparseCore 0:
  51.6 86.2 all-gather.3
  139.7 49.2 all-gather.5
  192.3 50.1 all-gather.7
  306.2 48.5 reduce-scatter.3
  357.6 84.1 reduce-scatter.5
  444.6 36.2 reduce-scatter.7

commit v3 on v2

--- a/solution.py
+++ b/solution.py
@@ -127,18 +127,26 @@
     return jnp.concatenate([value, pad], 1)
 
 
-def qkv_kernel(count, where_ref, *refs):
+def qkv_kernel(count, n_jumps, where_ref, *refs):
     pieces, refs = refs[: 2 * count], refs[2 * count :]
+    jumps, refs = refs[:n_jumps], refs[n_jumps:]
     x0, x1, x_far, cos_ref, sin_ref, norm_ref, query_ref, kv_ref, weight_ref, gains_ref, x_ref = refs
     step = pl.program_id(0)
 
     @pl.when(step == 0)
     def _():
         half = pieces[0].shape[0] // 2
-        for n, piece in enumerate(pieces):
+
+        def place(block, n, value):
             for part in range(2):
-                at = pl.multiple_of(where_ref[2 * (n % count) + part], 64)
-                weight_ref[n // count, pl.ds(at, half), :] = piece[part * half : (part + 1) * half, :]
+                at = pl.multiple_of(where_ref[2 * n + part], 64)
+                weight_ref[block, pl.ds(at, half), :] = value[part * half : (part + 1) * half, :]
+
+        for block in range(2):
+            for n in range(count):
+                place(block, n, pieces[block * count + n])
+            for n in range(n_jumps):
+                place(block, count + n, jumps[n][2 * half * block : 2 * half * (block + 1), :])
         row = lax.broadcasted_iota(jnp.int32, (8, LANES), 0)
         lane = lax.broadcasted_iota(jnp.int32, (8, LANES), 1)
         pick = jnp.where(row == lane, 1.0, 0.0).astype(BF)
@@ -166,16 +174,16 @@
     kv_ref[...] = jnp.concatenate(packs, 1).astype(BF)
 
 
-def project_qkv(where, pieces, x_rows, x_far, cos_table, sin_table):
+def project_qkv(where, pieces, jumps, x_rows, x_far, cos_table, sin_table):
     rows, width = x_rows[0].shape
     n_cols = pieces[0].shape[1]
     table = pl.BlockSpec((1, rows, LANES), lambda i, *_: (i, 0, 0))
     return pl.pallas_call(
-        functools.partial(qkv_kernel, len(pieces) // 2),
+        functools.partial(qkv_kernel, len(pieces) // 2, len(jumps)),
         grid_spec=pltpu.PrefetchScalarGridSpec(
             num_scalar_prefetch=1,
             grid=(4,),
-            in_specs=[pl.BlockSpec(v.shape, lambda i, *_: (0, 0)) for v in (*pieces, *x_rows, x_far)] + [table, table],
+            in_specs=[pl.BlockSpec(v.shape, lambda i, *_: (0, 0)) for v in (*pieces, *jumps, *x_rows, x_far)] + [table, table],
             out_specs=[
                 pl.BlockSpec((1, rows, width), lambda i, *_: (i, 0, 0)),
                 pl.BlockSpec((2, 1, 2 * rows, LANES), lambda i, *_: (0, i, 0, 0)),
@@ -192,10 +200,10 @@
             jax.ShapeDtypeStruct((2, width, n_cols), BF),
             jax.ShapeDtypeStruct((8, width), F32),
         ],
-        compiler_params=params(48),
+        compiler_params=params(58),
         cost_estimate=cost(8),
         name="project_qkv",
-    )(where, *pieces, *x_rows, x_far, cos_table, sin_table)
+    )(where, *pieces, *jumps, *x_rows, x_far, cos_table, sin_table)
 
 
 def query_back_kernel(core_ref, dq_ref, weight_ref, cos_ref, sin_ref, grad_ref, share_ref):
@@ -252,7 +260,7 @@
             jax.ShapeDtypeStruct((2, count, rows, 2 * HEAD), BF),
             jax.ShapeDtypeStruct((count, rows, width), BF),
         ],
-        compiler_params=params(40),
+        compiler_params=params(58),
         cost_estimate=cost(4),
         name=name,
     )(core, *args, weights, cos_table, sin_table)
@@ -459,7 +467,7 @@
         out_specs=[per_piece, per_piece],
         out_shape=[jax.ShapeDtypeStruct(query.shape, BF)] * 2,
         scratch_shapes=[pltpu.VMEM((rows, width), BF)],
-        compiler_params=params(40),
+        compiler_params=params(58),
         cost_estimate=cost(6),
         name="prepare_back",
     )(*mid, *weights, kept, query)
@@ -802,7 +810,7 @@
         + [pl.BlockSpec((width, 256), lambda s: (0, tile))] * 2,
         out_specs=[whole, whole],
         out_shape=[jax.ShapeDtypeStruct((2 * rows, width), BF), jax.ShapeDtypeStruct((2 * rows, width), F32)],
-        compiler_params=params(40),
+        compiler_params=params(58),
         cost_estimate=cost(4),
         name="output_projection",
     )(mixed, *weights)
@@ -966,7 +974,9 @@
     inputs, out_cotangent, qkv_pair, ffn_keep, ffn_got = sync(inputs, out_cotangent, qkv_pair, ffn_keep, ffn_got)
 
     qkv_other = flip(qkv_pair, "zh")
-    qkv_near = from_groups(qkv_pair)
+    hops = [k for k in range(1, groups) if k & -k == k]
+    jumps = [k for k in range(1, groups) if k & -k != k]
+    qkv_near = [flip(qkv_pair, "g", k) for k in (*hops, *jumps)]
     x_beside = flip(inputs, "zl")
     ffn_pair = in_order(ffn_keep, ffn_got)
     up_at = half + 2 * HEAD + 64
@@ -982,24 +992,26 @@
     x_near = jnp.concatenate([inputs, x_beside], 0)
 
     ffn_own = all_groups(ffn_pair)
-    qkv_far = from_groups(qkv_other)
+    qkv_far = [flip(qkv_other, "g", k) for k in (*hops, *jumps)]
     x_far = flip(x_near, "c")
     first_other = flip(first_pair, "zh")
-    qkv_far, x_far, first_other, up_pair = sync(qkv_far, x_far, first_other, up_pair)
+    qkv_far, x_far, first_other, up_pair, out_cotangent = sync(qkv_far, x_far, first_other, up_pair, out_cotangent)
 
     up_other = flip(up_pair, "zh")
-    k_order = jnp.arange(groups)[:, None]
+    g_beside = flip(out_cotangent, "zl")
+    k_order = jnp.array([0, *hops, *jumps])[:, None]
     piece_rows = (g ^ k_order) * shard_pair + (c ^ jnp.arange(2)[None, :]) * shard_rows
     norm_one, query, kv, qkv_w, gain_rows = project_qkv(
         piece_rows.reshape(-1).astype(jnp.int32),
-        [*qkv_near, *qkv_far],
+        [qkv_pair, *qkv_near, qkv_other, *qkv_far],
+        [],
         [inputs, x_beside],
         x_far,
         cos_table,
         sin_table,
     )
     first_piece = lax.dynamic_slice_in_dim(kv, (2 * c + zl) * rows, rows, 0)
-    norm_one, query, kv, qkv_w, gain_rows, kv_chunks, first_piece, out_cotangent, up_other, down_pair, first_other = sync(
+    norm_one, query, kv, qkv_w, gain_rows, kv_chunks, first_piece, out_cotangent, g_beside, up_other, down_pair, first_other = sync(
         norm_one,
         query,
         kv,
@@ -1008,6 +1020,7 @@
         [kv[n * CHUNK : (n + 1) * CHUNK] for n in range(2)],
         first_piece,
         out_cotangent,
+        g_beside,
         up_other,
         down_pair,
         first_other,
@@ -1044,9 +1057,9 @@
 
     other = [flip(kv_chunks[0], "zh")]
     same = [lax.ppermute(kv, "g", shift_pairs(d)) for d in shifts]
-    g_beside, g_across = flip(out_cotangent, "zl"), flip(out_cotangent, "c")
+    g_across = flip(out_cotangent, "c")
     state = step([kv], own_bases, 0, None)
-    other, same, g_beside, g_across, state, kv_late = sync(other, same, g_beside, g_across, state, kv_chunks[1])
+    other, same, g_across, state, kv_late = sync(other, same, g_across, state, kv_chunks[1])
 
     other.append(flip(kv_late, "zh"))
     far_blocks = [[lax.ppermute(other[0], "g", shift_pairs(d))] for d in shifts]
@@ -1092,21 +1105,21 @@
     beside = flip(beside_sum, "zl")
     across = flip(early[3], "c")
     out_across = [flip(late[1], "c"), flip(early[1], "c")]
-    gate_part = weight_grad([(early[7], late[7], early[5], late[5])], 4)
-    beside, across, out_across, gate_part, early, late = sync(beside, across, out_across, gate_part, early, late)
-    gate_sum = over_groups(gate_part)
+    gate_up_part = weight_grad(
+        [(early[7], late[7], early[5], late[5]), (early[7], late[7], early[6], late[6])], 8
+    )
+    beside, across, out_across, gate_up_part, early, late = sync(beside, across, out_across, gate_up_part, early, late)
+    gate_up_sum = over_groups(gate_up_part)
     grad_mid, mid_low = backward_norm(1, early[2], across, beside, after_attn, out_cotangent, gain_rows, [F32, BF])
     grad_mid, mid_low, early, late = sync(grad_mid, mid_low, early, late)
 
     mid_beside, mid_across = flip(mid_low, "zl"), flip(mid_low, "c")
-    up_down_part = weight_grad(
-        [(early[7], late[7], early[6], late[6]), (early[8], late[8], early[4], late[4])], 8
-    )
+    down_part = weight_grad([(early[8], late[8], early[4], late[4])], 4)
+    second_column = gain_columns([early[2], late[2], early[3], late[3]], [norm_own, norm_beside, norm_across, norm_both], 1)
     out_sum = add_rows(late[0], 0, out_across[0], 0)
-    mid_beside, mid_across, up_down_part, out_sum, early, late = sync(
-        mid_beside, mid_across, up_down_part, out_sum, early, late
-    )
-    up_down_sum = over_groups(up_down_part)
+    mid_beside, mid_across, down_part, second_column, out_sum = sync(
+        mid_beside, mid_across, down_part, second_column, out_sum
+    )
     mid_rows = [mid_low, mid_beside, mid_across, flip(mid_beside, "c")]
     q_aug, o_aug = prepare_back(mid_rows, (ffn_own, first_far), o_tile, kept, query)
     q_aug, o_aug, mid_rows, out_sum, mixed, early, late = sync(q_aug, o_aug, mid_rows, out_sum, mixed, early, late)
@@ -1122,37 +1135,45 @@
     out_beside = flip(out_sum, "zl")
     d_query, d_far = step_back(far_blocks, far_bases, 1, None, [BF] * len(far_blocks))
     o_part = head_grad(mid_rows, mixed)
-    second_column = gain_columns([early[2], late[2], early[3], late[3]], [norm_own, norm_beside, norm_across, norm_both], 1)
-    out_beside, d_query, d_far, o_part, gate_sum, second_column = sync(
-        out_beside, d_query, d_far, o_part, gate_sum, second_column
-    )
-    o_sum = over_groups(o_part)
+    down_o_part = jnp.concatenate([down_part[:, :half], o_part[:, :256], down_part[:, half:], o_part[:, 256:]], 1)
+    out_beside, d_query, d_far, gate_up_sum, down_o_part, early, late = sync(
+        out_beside, d_query, d_far, gate_up_sum, down_o_part, early, late
+    )
+    down_o_sum = over_groups(down_o_part)
 
     back = [lax.ppermute(d_far[2 * n + m], "g", reverse(shift_pairs(d))) for n, d in enumerate(shifts) for m in range(2)]
-    gate_far = other_half(gate_sum)
+    gate_up_far = other_half(gate_up_sum)
     d_query, d_other = step_back(other, other_bases, 1, d_query, [BF] * 2)
+    d_query, d_same = step_back(same, same_bases, 0, d_query, [BF] * len(same))
+    d_query, d_other, d_same, d_far, back, gate_up_far = sync(d_query, d_other, d_same, d_far, back, gate_up_far)
+
     other_sum = [d_other[m].astype(F32) for m in range(2)]
     for n in range(len(shifts)):
         for m in range(2):
             other_sum[m] = other_sum[m] + back[2 * n + m].astype(F32)
     other_sum = [o.astype(BF) for o in other_sum]
-    d_query, other_sum, gate_far = sync(d_query, other_sum, gate_far)
-
     other_back = [flip(other_sum[0], "zh")]
-    d_query, d_same = step_back(same, same_bases, 0, d_query, [BF] * len(same))
-    d_query, d_same, other_back, d_far, other_late = sync(d_query, d_same, other_back, d_far, other_sum[1])
-
-    other_back.append(flip(other_late, "zh"))
     same_back = [lax.ppermute(d_same[n], "g", reverse(shift_pairs(d))) for n, d in enumerate(shifts)]
-    d_query, d_own = step_back([kv], own_bases, 0, d_query, [F32])
-    d_q, shares = query_back(core, d_query, qkv_w, cos_table, sin_table)
-    q_part = head_grad([norm_one[k] for k in range(4)], d_q)
     above_back = []
     if above_groups:
         above = lax.dynamic_slice_in_dim(d_far[-1], zl * rows, rows, 0)
         above_back.append(lax.ppermute(above, ("g", "zh"), reverse(above_pairs)))
-    other_back, same_back, above_back, d_own, d_q, shares, q_part, up_down_sum = sync(
-        other_back, same_back, above_back, d_own, d_q, shares, q_part, up_down_sum
+    d_query, d_own = step_back([kv], own_bases, 0, d_query, [F32])
+    core = jnp.reshape(2 * c + zl, (1,)).astype(jnp.int32)
+    d_q, shares = query_back(core, d_query, qkv_w, cos_table, sin_table)
+    q_part = head_grad([norm_one[k] for k in range(4)], d_q)
+    other_back, same_back, above_back, d_own, shares, q_part, other_late, early, late = sync(
+        other_back, same_back, above_back, d_own, shares, q_part, other_sum[1], early, late
+    )
+
+    def group_slice(part, k):
+        return lax.dynamic_slice_in_dim(part, (g ^ k) * shard_pair, shard_pair, 0)
+
+    other_back.append(flip(other_late, "zh"))
+    q_got = [flip(group_slice(q_part, k), "g", k) for k in range(1, groups)]
+    layer_out = (after_attn + (early[0].astype(F32) + out_across[1].astype(F32) + out_beside.astype(F32))).astype(BF)
+    other_back, same_back, above_back, d_own, shares, q_part, q_got, down_o_sum, layer_out = sync(
+        other_back, same_back, above_back, d_own, shares, q_part, q_got, down_o_sum, layer_out
     )
 
     d_kvs, shares = kv_back(core, d_own[0], other_back, same_back, above_back, shares, qkv_w, cos_table, sin_table)
@@ -1160,45 +1181,29 @@
     across = flip(share_rows[2 * rows :], "c")
     kv_part = kv_grad(norm_one, shares, d_kvs, second_column)
     beside_sum = add_rows(share_rows, 1, across, 1)
-    def group_slice(part, k):
-        return lax.dynamic_slice_in_dim(part, (g ^ k) * shard_pair, shard_pair, 0)
-
-    def one_hop(k):
-        return k & -k == k
-
-    q_got = {k: flip(group_slice(q_part, k), "g", k) for k in range(1, groups) if one_hop(k)}
-    up_far = flip(up_down_sum[:, 2 * half : 3 * half], "zh")
-    beside_sum, kv_part, across, share_rows, up_far, o_sum, q_got, q_part, gate_far, gate_sum, up_down_sum = sync(
-        beside_sum, kv_part, across, share_rows, up_far, o_sum, q_got, q_part, gate_far, gate_sum, up_down_sum
-    )
-
-    kv_got = [flip(group_slice(kv_part, k), "g", k) for k in range(1, groups) if one_hop(k)]
-    diagonal = [
-        flip(jnp.concatenate([group_slice(kv_part, k), group_slice(q_part, k)], 1), "g", k)
-        for k in range(1, groups)
-        if not one_hop(k)
-    ]
+    down_at = half + 256
+    down_far = flip(down_o_sum[:, down_at : down_at + half], "zh")
+    beside_sum, kv_part, across, share_rows, down_far, down_o_sum, gate_up_far, gate_up_sum = sync(
+        beside_sum, kv_part, across, share_rows, down_far, down_o_sum, gate_up_far, gate_up_sum
+    )
+
+    kv_got = [flip(group_slice(kv_part, k), "g", k) for k in range(1, groups)]
+    q_sum = group_slice(q_part, 0).astype(F32) + sum(v.astype(F32) for v in q_got)
     beside = flip(beside_sum, "zl")
-    do_far = flip(jnp.concatenate([up_down_sum[:, 3 * half :], o_sum[:, 256:]], 1), "zh")
-    kv_got, diagonal, beside, do_far, up_far, gate_far = sync(kv_got, diagonal, beside, do_far, up_far, gate_far)
+    o_far = flip(down_o_sum[:, down_at + half :], "zh")
+    middle = 2 * half
+    gu_own, gu_got = to_owner(gate_up_sum[:, :middle].astype(F32) + gate_up_far.astype(F32))
+    kv_got, q_sum, beside, gu_own, gu_got, o_far, down_far = sync(kv_got, q_sum, beside, gu_own, gu_got, o_far, down_far)
 
     kv_sum = group_slice(kv_part, 0).astype(F32) + sum(v.astype(F32) for v in kv_got)
-    q_sum = group_slice(q_part, 0).astype(F32) + sum(v.astype(F32) for v in q_got.values())
-    for value in diagonal:
-        kv_sum, q_sum = kv_sum + value[:, :512].astype(F32), q_sum + value[:, 512:].astype(F32)
     kvq_own = jnp.concatenate([kv_sum[:, :256], q_sum[:, :256]], 1)
     kvq_give = jnp.concatenate([kv_sum[:, 256:], q_sum[:, 256:]], 1).astype(BF)
-    kvq_own, kvq_give, do_far, beside, gate_far = sync(kvq_own, kvq_give, do_far, beside, gate_far)
+    kvq_own, kvq_give, o_far, down_far, beside = sync(kvq_own, kvq_give, o_far, down_far, beside)
+    down_o_far = jnp.concatenate([down_far, o_far], 1)
     kvq_far = flip(kvq_give, "zh")
     [input_grad] = backward_norm(0, share_rows, across, beside, inputs, grad_mid, gain_rows, [BF])
-    gate_up = jnp.concatenate([gate_sum[:, :half], up_down_sum[:, :half]], 1).astype(F32)
-    gu_own, gu_got = to_owner(gate_up + jnp.concatenate([gate_far, up_far], 1).astype(F32))
-    do_own = jnp.concatenate([up_down_sum[:, half : 2 * half], o_sum[:, :256]], 1)
-    do_own, do_got = to_owner(do_own.astype(F32) + do_far.astype(F32))
-    layer_out = (after_attn + (early[0].astype(F32) + out_across[1].astype(F32) + out_beside.astype(F32))).astype(BF)
-    kvq_far, do_own, do_got, gu_own, gu_got, input_grad, layer_out = sync(
-        kvq_far, do_own, do_got, gu_own, gu_got, input_grad, layer_out
-    )
+    do_own, do_got = to_owner(down_o_sum[:, : half + 256].astype(F32) + down_o_far.astype(F32))
+    kvq_far, do_own, do_got, input_grad = sync(kvq_far, do_own, do_got, input_grad)
 
     kvq_own, kvq_got = to_owner(kvq_own + kvq_far.astype(F32))
     gain_sums = (kvq_own + kvq_got)[:, 2 * HEAD : 2 * HEAD + 2]

time: 610 us -> 583 us (0.956)
  local copies, waits for them, and re-layouts: 89.9 us -> 59.4 us
  Pallas kernels: 175 us -> 186 us
    unnamed x217 -> x227, local copies, waits for them, and re-layouts: 58.2 us -> 28.3 us
    reduce_scatter x3 -> x2, waiting for transfers between devices: 0.02 us -> 16.4 us  [over_groups(): return lax.psum_scatter(value, 'g', scatter_dimension=0, tiled=True)]
    ppermute x50 -> x51, waiting for transfers between devices: 172 us -> 159 us  [flip(): return lax.ppermute(value, axis, [(s, s ^ bit) for s in range(count)])]
    ppermute x2, waiting for transfers between devices: 28.7 us -> 17.5 us  [body(): lax.ppermute(d_far[2 * n + m], 'g', reverse(shift_pairs(d)))]
    pallas_call x2, Pallas kernels: 8.78 us -> 15.5 us  [project_back(): pl.pallas_call(kernel, grid_spec=pltpu.PrefetchScalarGridSpec(num_scalar_...]
    ppermute x50 -> x51, starting transfers between devices: 48.9 us -> 51.6 us  [flip(): return lax.ppermute(value, axis, [(s, s ^ bit) for s in range(count)])]
  transfers between devices with their start and end apart: 64 -> 64, of which waited for: 30 -> 36; matrix products, arithmetic and copies ran while one was open for 8% -> 8% of each run, Pallas kernels for 26% -> 28%
where the time goes in v3:
time: 583 us; the launch traced here: 572 us
  waiting for transfers between devices  209 us (36%)
  Pallas kernels  186 us (32%)
  starting transfers between devices  72.5 us (12%)
  local copies, waits for them, and re-layouts  59.4 us (10%)
  other arithmetic  29.6 us (5%)
  between operations  15.7 us (3%)
    ppermute x51, waiting for transfers between devices, flip(): return lax.ppermute(value, axis, [(s, s ^ bit) for s in range(count)])  159 us
    ppermute x51, starting transfers between devices, flip(): return lax.ppermute(value, axis, [(s, s ^ bit) for s in range(count)])  51.6 us
    pallas_call x4, Pallas kernels, attend_back(): pl.pallas_call(functools.partial(backward_kernel, swaps, d_query is not N...  39.3 us
    pallas_call x2, Pallas kernels, feed_forward(): pl.pallas_call(functools.partial(ffn_kernel, tiles), grid=(2 * tiles,), i...  35.8 us
    unnamed x227, local copies, waits for them, and re-layouts  28.3 us
    pallas_call x4, Pallas kernels, attend(): pl.pallas_call(functools.partial(forward_kernel, swaps, state is None, la...  24.8 us
    ppermute x2, waiting for transfers between devices, body(): lax.ppermute(d_far[2 * n + m], 'g', reverse(shift_pairs(d)))  17.5 us
    reduce_scatter x2, waiting for transfers between devices, over_groups(): return lax.psum_scatter(value, 'g', scatter_dimension=0, tiled=True)  16.4 us
  transfers between devices with their start and end apart: 64, of which 36 were waited for; matrix products, arithmetic and copies ran while one was open for 8% of the time, Pallas kernels for 28%

profile of v3, /device:TPU:0, one launch (start us, length us, event | category | flops | bytes accessed | tf_op | source)
XLA Modules:
  0.0 572.2 jit_solution(12994028740723935086)
XLA Ops:
  37.9 8.4 %collective-permute-done.3.refs_2_ = bf16[384,512]{1,0:T(8,128)(2,1)} collective-permute-done((bf16[384,512]{1,0:T(8,128)(2,1)}, bf16[384,512]{1,0:T(8,128)(2,1)}, u32[]{:S(2)}, u32[]{:S(2)}) %collective-permute-start.3) | collective-permute-done | bytes 393248 | tf_op jit(solution)/shard_map/ppermute | solution.py:61
  60.4 12.7 %collective-permute-done.7.refs_5_ = bf16[384,512]{1,0:T(8,128)(2,1)S(1)} collective-permute-done((bf16[384,512]{1,0:T(8,128)(2,1)}, bf16[384,512]{1,0:T(8,128)(2,1)S(1)}, u32[]{:S(2)}, u32[]{:S(2)}) %collective-permute-start.7) | collective-permute-done | bytes 393248 | tf_op jit(solution)/shard_map/ppermute | solution.py:61
  77.9 12.0 %collective-permute-done.9.refs_7_ = bf16[384,512]{1,0:T(8,128)(2,1)S(1)} collective-permute-done((bf16[384,512]{1,0:T(8,128)(2,1)}, bf16[384,512]{1,0:T(8,128)(2,1)S(1)}, u32[]{:S(2)}, u32[]{:S(2)}) %collective-permute-start.9) | collective-permute-done | bytes 393248 | tf_op jit(solution)/shard_map/ppermute | solution.py:61
  93.6 12.8 %project_qkv.1 = (bf16[4,256,1536]{2,1,0:T(8,128)(2,1)}, bf16[2,4,512,128]{3,2,1,0:T(8,128)(2,1)}, bf16[1024,384]{1,0:T(8,128)(2,1)}, bf16[2,1536,512]{2,1,0:T(8,128)(2,1)}, f32[8,1536]{1,0:T(8,128)}) custom-call(s32[8]{0:T(128)} %add.259.where_ref, bf16[384,512]{1,0:T(8,128)(2,1)} %pad_maximum_fusion.4.refs_0_, ...), custom_call_target="tpu_custom_call" | custom-call | flops 92000000 | bytes 288000 | tf_op jit(solution)/shard_map/project_qkv/pallas_call | solution.py:181
  125.2 7.8 %attend.4.refs_4_ = f32[2,4,512,128]{3,2,1,0:T(8,128)S(1)} custom-call(s32[4,4]{1,0:T(4,128)S(1)} %pad_add_fusion.info_ref, s32[2]{0:T(128)S(1)} %pad_add_fusion.2.base_ref, s32[1]{0:T(128)} %bitcast.19.zl_ref, bf16[2,4,512,128]{3,2,1,0:T(8,128)(2,1)S(1)} %copy-done.1, s32[4,256,128]{2,1,0:T(8,128)S(1)} %broadcast_in_dim.114.refs_1_, ...), custom_call_target="tpu_custom_call" | custom-call | flops 117760000 | bytes 368640 | tf_op jit(solution)/shard_map/attend/pallas_call | solution.py:400
  134.3 8.9 %collective-permute-done.14.refs_3_.refs_4_ = bf16[512,384]{1,0:T(8,128)(2,1)S(1)} collective-permute-done((bf16[512,384]{1,0:T(8,128)(2,1)}, bf16[512,384]{1,0:T(8,128)(2,1)S(1)}, u32[]{:S(2)}, u32[]{:S(2)}) %collective-permute-start.14) | collective-permute-done | bytes 393248 | tf_op jit(solution)/shard_map/ppermute | solution.py:61
  157.0 6.9 %collective-permute-done.17.refs_4_.refs_5_ = bf16[512,384]{1,0:T(8,128)(2,1)S(1)} collective-permute-done((bf16[512,384]{1,0:T(8,128)(2,1)}, bf16[512,384]{1,0:T(8,128)(2,1)S(1)}, u32[]{:S(2)}, u32[]{:S(2)}) %collective-permute-start.17) | collective-permute-done | bytes 393248 | tf_op jit(solution)/shard_map/ppermute | solution.py:61
  209.3 19.6 %collective-permute-done.24.beside_ref = bf16[256,1536]{1,0:T(8,128)(2,1)S(1)} collective-permute-done((bf16[256,1536]{1,0:T(8,128)(2,1)S(1)}, bf16[256,1536]{1,0:T(8,128)(2,1)S(1)}, u32[]{:S(2)}, u32[]{:S(2)}) %collective-permute-start.24) | collective-permute-done | bytes 786464 | tf_op jit(solution)/shard_map/ppermute | solution.py:61
  232.0 8.2 %all-gather.8.cloned.1.call-done.refs_4_.refs_5_ = bf16[1536,1024]{1,0:T(8,128)(2,1)} async-done(((bf16[384,1024]{1,0:T(8,128)(2,1)}), bf16[1536,1024]{1,0:T(8,128)(2,1)}) %all-gather.8.cloned.1.call-update) | async-done | bytes 3145744 | tf_op jit(solution)/shard_map/all_gather | solution.py:56
  240.2 18.0 %feed_forward.2 = (bf16[256,1536]{1,0:T(8,128)(2,1)}, bf16[256,1536]{1,0:T(8,128)(2,1)}, bf16[256,1536]{1,0:T(8,128)(2,1)}, bf16[256,1536]{1,0:T(8,128)(2,1)}, b...) custom-call(bf16[256,1536]{1,0:T(8,128)(2,1)} %copy-done.19, ...), custom_call_target="tpu_custom_call" | custom-call | flops 207000000 | bytes 648000 | tf_op jit(solution)/shard_map/feed_forward/pallas_call | solution.py:649
  261.6 17.8 %feed_forward.3 = (bf16[256,1536]{1,0:T(8,128)(2,1)}, bf16[256,1536]{1,0:T(8,128)(2,1)}, bf16[256,1536]{1,0:T(8,128)(2,1)}, bf16[256,1536]{1,0:T(8,128)(2,1)}, b...) custom-call(bf16[256,1536]{1,0:T(8,128)(2,1)} %collective-permute-do, ...), custom_call_target="tpu_custom_call" | custom-call | flops 207000000 | bytes 648000 | tf_op jit(solution)/shard_map/feed_forward/pallas_call | solution.py:649
  288.7 10.9 %weight_grad.2 = bf16[1536,2048]{1,0:T(8,128)(2,1)} custom-call(bf16[1536,512]{1,0:T(8,128)(2,1)S(1)} %copy-done.13, bf16[1536,512]{1,0:T(8,128)(2,1)} %get-tuple-element.373.refs_1_.refs_5_, bf16[512,1024]{1,0:T(8,128)(2,1)S(1)} %copy-done.44, bf16[512,1024]{1,0:T(8,128)(2,1)S(1)} %copy-done.46, bf16[1536,512]{1,0:T(8,128)(2,1)S(1)} %copy-done.13, ...), custom_call_target="tpu_custom_call" | custom-call | flops 92000000 | bytes 288000 | tf_op jit(solution)/shard_map/weight_grad/pallas_call | solution.py:681
  331.5 10.3 %prepare_back.1 = (bf16[2,4,512,128]{3,2,1,0:T(8,128)(2,1)}, bf16[2,4,512,128]{3,2,1,0:T(8,128)(2,1)}) custom-call(bf16[256,1536]{1,0:T(8,128)(2,1)} %copy-done.30, bf16[256,1536]{1,0:T(8,128)(2,1)} %copy-done.32, bf16[256,1536]{1,0:T(8,128)(2,1)} %copy-done.34, bf16[256,1536]{1,0:T(8,128)(2,1)} %collective-permute-done.35.m3.l3, ...), custom_call_target="tpu_custom_call" | custom-call | flops 69000000 | bytes 216000 | tf_op jit(solution)/shard_map/prepare_back/pallas_call | solution.py:461
  347.1 6.8 %attend_back.4 = (f32[2,4,512,128]{3,2,1,0:T(8,128)}, bf16[512,384]{1,0:T(8,128)(2,1)}, bf16[512,384]{1,0:T(8,128)(2,1)}, bf16[512,384]{1,0:T(8,128)(2,1)}) custom-call(s32[4,4]{1,0:T(4,128)} %copy-done.59, s32[3]{0:T(128)} %copy-done.63, s32[1]{0:T(128)} %bitcast.19.zl_ref, bf16[2,4,512,128]{3,2,1,0:T(8,128)(2,1)} %get-tuple-element.422.refs_0_, ...), custom_call_target="tpu_custom_call" | custom-call | flops 276000000 | bytes 864000 | tf_op jit(solution)/shard_map/attend_back/pallas_call | solution.py:556
  361.4 16.4 %reduce-scatter.3.cloned.1.call-done = bf16[384,2048]{1,0:T(8,128)(2,1)} async-done(((bf16[1536,2048]{1,0:T(8,128)(2,1)}), bf16[384,2048]{1,0:T(8,128)(2,1)}) %reduce-scatter.3.cloned.1.call-update) | async-done | bytes 1572880 | tf_op jit(solution)/shard_map/reduce_scatter | solution.py:97
  385.2 10.1 %attend_back.5 = (f32[2,4,512,128]{3,2,1,0:T(8,128)}, bf16[512,384]{1,0:T(8,128)(2,1)}, bf16[512,384]{1,0:T(8,128)(2,1)}) custom-call(s32[4,4]{1,0:T(4,128)} %copy-done.59, s32[2]{0:T(128)} %copy-done.62, s32[1]{0:T(128)} %bitcast.19.zl_ref, bf16[2,4,512,128]{3,2,1,0:T(8,128)(2,1)} %get-tuple-element.422.refs_0_, ...), custom_call_target="tpu_custom_call" | custom-call | flops 184000000 | bytes 576000 | tf_op jit(solution)/shard_map/attend_back/pallas_call | solution.py:556
  395.3 6.8 %attend_back.6 = (f32[2,4,512,128]{3,2,1,0:T(8,128)}, bf16[1024,384]{1,0:T(8,128)(2,1)}) custom-call(s32[4,4]{1,0:T(4,128)} %copy-done.59, s32[2]{0:T(128)} %copy-done.60, s32[1]{0:T(128)} %bitcast.19.zl_ref, bf16[2,4,512,128]{3,2,1,0:T(8,128)(2,1)} %get-tuple-element.422.refs_0_, bf16[2,4,512,128]{3,2,1,0:T(8,128)(2,1)} %get-tuple-element.423.refs_1_, ...), custom_call_target="tpu_custom_call" | custom-call | flops 184000000 | bytes 576000 | tf_op jit(solution)/shard_map/attend_back/pallas_call | solution.py:556
  404.2 15.4 %collective-permute-done.38 = bf16[512,384]{1,0:T(8,128)(2,1)S(1)} collective-permute-done((bf16[512,384]{1,0:T(8,128)(2,1)}, bf16[512,384]{1,0:T(8,128)(2,1)S(1)}, u32[]{:S(2)}, u32[]{:S(2)}) %collective-permute-start.38) | collective-permute-done | bytes 393248 | tf_op jit(solution)/shard_map/ppermute | solution.py:1144
  424.0 15.5 %attend_back.7 = (f32[2,4,512,128]{3,2,1,0:T(8,128)}, f32[1024,384]{1,0:T(8,128)}) custom-call(s32[4,4]{1,0:T(4,128)} %copy-done.59, s32[2]{0:T(128)} %copy-done.61, s32[1]{0:T(128)} %bitcast.19.zl_ref, bf16[2,4,512,128]{3,2,1,0:T(8,128)(2,1)} %get-tuple-element.422.refs_0_, bf16[2,4,512,128]{3,2,1,0:T(8,128)(2,1)} %get-tuple-element.423.refs_1_, ...), custom_call_target="tpu_custom_call" | custom-call | flops 184000000 | bytes 576000 | tf_op jit(solution)/shard_map/attend_back/pallas_call | solution.py:556
  463.8 7.7 %collective-permute-done.43.refs_2_ = bf16[512,384]{1,0:T(8,128)(2,1)S(1)} collective-permute-done((bf16[512,384]{1,0:T(8,128)(2,1)S(1)}, bf16[512,384]{1,0:T(8,128)(2,1)S(1)}, u32[]{:S(2)}, u32[]{:S(2)}) %collective-permute-start.43) | collective-permute-done | bytes 393248 | tf_op jit(solution)/shard_map/ppermute | solution.py:61
  473.3 8.7 %kv_back.1 = (bf16[2,4,256,192]{3,2,1,0:T(8,128)(2,1)}, bf16[4,256,1536]{2,1,0:T(8,128)(2,1)}) custom-call(s32[1]{0:T(128)} %bitcast.27.core_ref, f32[1024,384]{1,0:T(8,128)} %get-tuple-element.475.refs_0_, bf16[512,384]{1,0:T(8,128)(2,1)} %collective-permute-done.40.refs_1_, bf16[512,384]{1,0:T(8,128)(2,1)} %copy-done.102, ...), custom_call_target="tpu_custom_call" | custom-call | flops 46000000 | bytes 144000 | tf_op jit(solution)/shard_map/kv_back/pallas_call | solution.py:251
  498.7 9.2 %collective-permute-done.48 = bf16[384,512]{1,0:T(8,128)(2,1)} collective-permute-done((bf16[384,512]{1,0:T(8,128)(2,1)}, bf16[384,512]{1,0:T(8,128)(2,1)}, u32[]{:S(2)}, u32[]{:S(2)}) %collective-permute-start.48) | collective-permute-done | bytes 393248 | tf_op jit(solution)/shard_map/ppermute | solution.py:61
  521.5 10.9 %collective-permute-done.54 = bf16[384,256]{1,0:T(8,128)(2,1)S(1)} collective-permute-done((bf16[384,256]{1,0:T(8,128)(2,1)S(1)}, bf16[384,256]{1,0:T(8,128)(2,1)S(1)}, u32[]{:S(2)}, u32[]{:S(2)}) %collective-permute-start.54) | collective-permute-done | bytes 196640 | tf_op jit(solution)/shard_map/ppermute | solution.py:61
  545.8 10.5 %collective-permute-done.55 = bf16[384,512]{1,0:T(8,128)(2,1)S(1)} collective-permute-done((bf16[384,512]{1,0:T(8,128)(2,1)S(1)}, bf16[384,512]{1,0:T(8,128)(2,1)S(1)}, u32[]{:S(2)}, u32[]{:S(2)}) %collective-permute-start.55) | collective-permute-done | bytes 393248 | tf_op jit(solution)/shard_map/ppermute | solution.py:61
  (486 shorter events, 284.4 us)
Async XLA Ops:
  7.2 156.8 %all-gather.4.cloned.1.call-start = ((), (), s32[]{:S(2)}) async-start(), calls=%async_computation.2 | async-start | bytes 6881280 | tf_op jit(solution)/shard_map/all_gather | solution.py:56
  21.0 29.2 %collective-permute-start.6 = (bf16[256,1536]{1,0:T(8,128)(2,1)S(1)}, bf16[256,1536]{1,0:T(8,128)(2,1)S(1)}, u32[]{:S(2)}, u32[]{:S(2)}) collective-permute-start(bf16[256,1536]{1,0:T(8,128)(2,1)S(1)} %copy-done.6), channel_id=1, source_target_pairs={{0,1},{1,0},{2,3},{3,2},{4,5},{5,4},{6,7},{7,6},{8,9},{9,8},{10,11... | collective-permute-start | bytes 2359304 | tf_op jit(solution)/shard_map/ppermute | solution.py:61
  52.8 144.6 %all-gather.6.cloned.1.call-start = ((), (), s32[]{:S(2)}) async-start(), calls=%async_computation.3 | async-start | bytes 2949120 | tf_op jit(solution)/shard_map/all_gather | solution.py:56
  54.1 36.5 %collective-permute-start.10 = (bf16[512,1536]{1,0:T(8,128)(2,1)}, bf16[512,1536]{1,0:T(8,128)(2,1)S(1)}, u32[]{:S(2)}, u32[]{:S(2)}) collective-permute-start(bf16[512,1536]{1,0:T(8,128)(2,1)} %pad_maximum_fusion.1), channel_id=1, source_target_pairs={{0,4},{4,0},{1,5},{5,1},{2,6},{6,2},{3,7},{7,3},{8,12},{12,8},{9,1... | collective-permute-start | bytes 4718600 | tf_op jit(solution)/shard_map/ppermute | solution.py:61
  54.1 36.5 %collective-permute-start.11 = (bf16[384,768]{1,0:T(8,128)(2,1)S(1)}, bf16[384,768]{1,0:T(8,128)(2,1)S(1)}, u32[]{:S(2)}, u32[]{:S(2)}) collective-permute-start(bf16[384,768]{1,0:T(8,128)(2,1)S(1)} %copy-done.85), channel_id=1, source_target_pairs={{0,2},{2,0},{1,3},{3,1},{4,6},{6,4},{5,7},{7,5},{8,10},{10,8},{9,1... | collective-permute-start | bytes 1769480 | tf_op jit(solution)/shard_map/ppermute | solution.py:61
  59.9 30.0 %collective-permute-start.9 = (bf16[384,512]{1,0:T(8,128)(2,1)}, bf16[384,512]{1,0:T(8,128)(2,1)S(1)}, u32[]{:S(2)}, u32[]{:S(2)}) collective-permute-start(bf16[384,512]{1,0:T(8,128)(2,1)} %collective-permute-done.5.refs_4_), channel_id=1, source_target_pairs={{0,24},{8,16},{16,8},{24,0},{1,25},{9,17},{17,9},{25,1},{2,26},{10... | collective-permute-start | bytes 1179656 | tf_op jit(solution)/shard_map/ppermute | solution.py:61
  90.7 26.3 %collective-permute-start.12 = (bf16[256,1536]{1,0:T(8,128)(2,1)}, bf16[256,1536]{1,0:T(8,128)(2,1)}, u32[]{:S(2)}, u32[]{:S(2)}) collective-permute-start(bf16[256,1536]{1,0:T(8,128)(2,1)} %base_ref), channel_id=1, source_target_pairs={{0,1},{1,0},{2,3},{3,2},{4,5},{5,4},{6,7},{7,6},{8,9},{9,8},{10,11... | collective-permute-start | bytes 2359304 | tf_op jit(solution)/shard_map/ppermute | solution.py:61
  92.4 23.7 %collective-permute-start.13 = (bf16[384,512]{1,0:T(8,128)(2,1)}, bf16[384,512]{1,0:T(8,128)(2,1)}, u32[]{:S(2)}, u32[]{:S(2)}) collective-permute-start(bf16[384,512]{1,0:T(8,128)(2,1)} %get-tuple-element.289), channel_id=1, source_target_pairs={{0,2},{2,0},{1,3},{3,1},{4,6},{6,4},{5,7},{7,5},{8,10},{10,8},{9,1... | collective-permute-start | bytes 1179656 | tf_op jit(solution)/shard_map/ppermute | solution.py:61
  117.0 123.2 %all-gather.8.cloned.1.call-start = ((), (), s32[]{:S(2)}) async-start(), calls=%async_computation.4 | async-start | bytes 3932160 | tf_op jit(solution)/shard_map/all_gather | solution.py:56
  117.0 26.7 %collective-permute-start.15 = (bf16[1024,384]{1,0:T(8,128)(2,1)S(1)}, bf16[1024,384]{1,0:T(8,128)(2,1)}, u32[]{:S(2)}, u32[]{:S(2)}) collective-permute-start(bf16[1024,384]{1,0:T(8,128)(2,1)S(1)} %copy-done.12), channel_id=1, source_target_pairs={{0,8},{1,9},{2,10},{3,11},{4,12},{5,13},{6,14},{7,15}} | collective-permute-start | bytes 2359304 | tf_op jit(solution)/shard_map/ppermute | solution.py:1059
  122.3 21.5 %collective-permute-start.16 = (bf16[256,1536]{1,0:T(8,128)(2,1)}, bf16[256,1536]{1,0:T(8,128)(2,1)}, u32[]{:S(2)}, u32[]{:S(2)}) collective-permute-start(bf16[256,1536]{1,0:T(8,128)(2,1)} %base_ref), channel_id=1, source_target_pairs={{0,4},{4,0},{1,5},{5,1},{2,6},{6,2},{3,7},{7,3},{8,12},{12,8},{9,1... | collective-permute-start | bytes 2359304 | tf_op jit(solution)/shard_map/ppermute | solution.py:61
  122.3 20.9 %collective-permute-start.14 = (bf16[512,384]{1,0:T(8,128)(2,1)}, bf16[512,384]{1,0:T(8,128)(2,1)S(1)}, u32[]{:S(2)}, u32[]{:S(2)}) collective-permute-start(bf16[512,384]{1,0:T(8,128)(2,1)} %get-tuple-element.295), channel_id=1, source_target_pairs={{0,2},{2,0},{1,3},{3,1},{4,6},{6,4},{5,7},{7,5},{8,10},{10,8},{9,1... | collective-permute-start | bytes 1179656 | tf_op jit(solution)/shard_map/ppermute | solution.py:61
  124.8 32.2 %collective-permute-start.19 = (bf16[256,1536]{1,0:T(8,128)(2,1)}, bf16[256,1536]{1,0:T(8,128)(2,1)}, u32[]{:S(2)}, u32[]{:S(2)}) collective-permute-start(bf16[256,1536]{1,0:T(8,128)(2,1)} %collective-permute-done.12.g0), channel_id=1, source_target_pairs={{0,4},{4,0},{1,5},{5,1},{2,6},{6,2},{3,7},{7,3},{8,12},{12,8},{9,1... | collective-permute-start | bytes 2359304 | tf_op jit(solution)/shard_map/ppermute | solution.py:61
  189.7 188.1 %reduce-scatter.3.cloned.1.call-start = ((), (), s32[]{:S(2)}) async-start(), calls=%async_computation.5 | async-start | bytes 7864320 | tf_op jit(solution)/shard_map/reduce_scatter | solution.py:97
  229.7 28.4 %collective-permute-start.25 = (bf16[256,1536]{1,0:T(8,128)(2,1)S(1)}, bf16[256,1536]{1,0:T(8,128)(2,1)}, u32[]{:S(2)}, u32[]{:S(2)}) collective-permute-start(bf16[256,1536]{1,0:T(8,128)(2,1)S(1)} %get-tuple-element.326.n0.refs_4_), channel_id=1, source_target_pairs={{0,1},{1,0},{2,3},{3,2},{4,5},{5,4},{6,7},{7,6},{8,9},{9,8},{10,11... | collective-permute-start | bytes 2359304 | tf_op jit(solution)/shard_map/ppermute | solution.py:61
  304.2 169.2 %reduce-scatter.5.cloned.1.call-start = ((), (), s32[]{:S(2)}) async-start(), calls=%async_computation.6 | async-start | bytes 5898240 | tf_op jit(solution)/shard_map/reduce_scatter | solution.py:97
  380.2 39.4 %collective-permute-start.39 = (bf16[384,1024]{1,0:T(8,128)(2,1)}, bf16[384,1024]{1,0:T(8,128)(2,1)S(1)}, u32[]{:S(2)}, u32[]{:S(2)}) collective-permute-start(bf16[384,1024]{1,0:T(8,128)(2,1)} %slice.134), channel_id=1, source_target_pairs={{0,2},{2,0},{1,3},{3,1},{4,6},{6,4},{5,7},{7,5},{8,10},{10,8},{9,1... | collective-permute-start | bytes 2359304 | tf_op jit(solution)/shard_map/ppermute | solution.py:61
  382.6 21.6 %collective-permute-start.37 = (bf16[512,384]{1,0:T(8,128)(2,1)}, bf16[512,384]{1,0:T(8,128)(2,1)S(1)}, u32[]{:S(2)}, u32[]{:S(2)}) collective-permute-start(bf16[512,384]{1,0:T(8,128)(2,1)} %get-tuple-element.445), channel_id=1, source_target_pairs={{8,0},{9,1},{10,2},{11,3},{12,4},{13,5},{14,6},{15,7}} | collective-permute-start | bytes 1179656 | tf_op jit(solution)/shard_map/ppermute | solution.py:1144
  383.9 35.7 %collective-permute-start.38 = (bf16[512,384]{1,0:T(8,128)(2,1)}, bf16[512,384]{1,0:T(8,128)(2,1)S(1)}, u32[]{:S(2)}, u32[]{:S(2)}) collective-permute-start(bf16[512,384]{1,0:T(8,128)(2,1)} %get-tuple-element.446), channel_id=1, source_target_pairs={{8,0},{9,1},{10,2},{11,3},{12,4},{13,5},{14,6},{15,7}} | collective-permute-start | bytes 1179656 | tf_op jit(solution)/shard_map/ppermute | solution.py:1144
  420.6 31.9 %collective-permute-start.41 = (bf16[1024,384]{1,0:T(8,128)(2,1)}, bf16[1024,384]{1,0:T(8,128)(2,1)}, u32[]{:S(2)}, u32[]{:S(2)}) collective-permute-start(bf16[1024,384]{1,0:T(8,128)(2,1)} %get-tuple-element.451), channel_id=1, source_target_pairs={{8,0},{9,1},{10,2},{11,3},{12,4},{13,5},{14,6},{15,7}} | collective-permute-start | bytes 2359304 | tf_op jit(solution)/shard_map/ppermute | solution.py:1156
  423.2 27.0 %collective-permute-start.40 = (bf16[512,384]{1,0:T(8,128)(2,1)S(1)}, bf16[512,384]{1,0:T(8,128)(2,1)}, u32[]{:S(2)}, u32[]{:S(2)}) collective-permute-start(bf16[512,384]{1,0:T(8,128)(2,1)S(1)} %add_convert_fusion.2), channel_id=1, source_target_pairs={{0,2},{2,0},{1,3},{3,1},{4,6},{6,4},{5,7},{7,5},{8,10},{10,8},{9,1... | collective-permute-start | bytes 1179656 | tf_op jit(solution)/shard_map/ppermute | solution.py:61
  423.3 26.9 %collective-permute-start.42 = (bf16[256,384]{1,0:T(8,128)(2,1)S(1)}, bf16[256,384]{1,0:T(8,128)(2,1)S(1)}, u32[]{:S(2)}, u32[]{:S(2)}) collective-permute-start(bf16[256,384]{1,0:T(8,128)(2,1)S(1)} %constant_dynamic-slice_fusion.8), channel_id=1, source_target_pairs={{2,8},{3,9},{6,12},{7,13}} | collective-permute-start | bytes 589832 | tf_op jit(solution)/shard_map/ppermute | solution.py:1160
  486.7 21.2 %collective-permute-start.48 = (bf16[384,512]{1,0:T(8,128)(2,1)}, bf16[384,512]{1,0:T(8,128)(2,1)}, u32[]{:S(2)}, u32[]{:S(2)}) collective-permute-start(bf16[384,512]{1,0:T(8,128)(2,1)} %slice.141), channel_id=1, source_target_pairs={{0,2},{2,0},{1,3},{3,1},{4,6},{6,4},{5,7},{7,5},{8,10},{10,8},{9,1... | collective-permute-start | bytes 1179656 | tf_op jit(solution)/shard_map/ppermute | solution.py:61
  510.1 24.5 %collective-permute-start.52 = (bf16[256,1536]{1,0:T(8,128)(2,1)}, bf16[256,1536]{1,0:T(8,128)(2,1)}, u32[]{:S(2)}, u32[]{:S(2)}) collective-permute-start(bf16[256,1536]{1,0:T(8,128)(2,1)} %add_rows.7), channel_id=1, source_target_pairs={{0,1},{1,0},{2,3},{3,2},{4,5},{5,4},{6,7},{7,6},{8,9},{9,8},{10,11... | collective-permute-start | bytes 2359304 | tf_op jit(solution)/shard_map/ppermute | solution.py:61
  (155 other events, 1543.4 us)
Sparse Core Ops, SparseCore 0:
  52.9 80.8 all-gather.3
  136.2 50.3 all-gather.5
  189.8 50.3 all-gather.7
  304.3 73.5 reduce-scatter.2
  380.7 80.4 reduce-scatter.4

commit v4 on v3

--- a/solution.py
+++ b/solution.py
@@ -243,7 +243,7 @@
     share_ref[0] = total.astype(BF)
 
 
-def project_back(kernel, core, args, specs, weights, cos_table, sin_table, name):
+def project_back(kernel, core, args, specs, weights, cos_table, sin_table, name, mib):
     count, rows, _ = cos_table.shape
     width = weights.shape[1]
     piece = pl.BlockSpec((1, rows, width), lambda i, *_: (i, 0, 0))
@@ -260,7 +260,7 @@
             jax.ShapeDtypeStruct((2, count, rows, 2 * HEAD), BF),
             jax.ShapeDtypeStruct((count, rows, width), BF),
         ],
-        compiler_params=params(58),
+        compiler_params=params(mib),
         cost_estimate=cost(4),
         name=name,
     )(core, *args, weights, cos_table, sin_table)
@@ -268,7 +268,7 @@
 
 def query_back(core, d_query, weights, cos_table, sin_table):
     spec = pl.BlockSpec((2, 1, 2 * PIECE, LANES), lambda i, *_: (0, i, 0, 0))
-    return project_back(query_back_kernel, core, [d_query], [spec], weights, cos_table, sin_table, "query_back")
+    return project_back(query_back_kernel, core, [d_query], [spec], weights, cos_table, sin_table, "query_back", 40)
 
 
 def kv_back(core, own, other, same, above, shares, weights, cos_table, sin_table):
@@ -279,7 +279,7 @@
     specs += [pl.BlockSpec((PIECE, 4 * HEAD), lambda i, *_: (0, 0))] * len(above)
     specs.append(pl.BlockSpec((1, *shares.shape[1:]), lambda i, *_: (i, 0, 0)))
     kernel = functools.partial(kv_back_kernel, len(same), bool(above))
-    return project_back(kernel, core, args, specs, weights, cos_table, sin_table, "kv_back")
+    return project_back(kernel, core, args, specs, weights, cos_table, sin_table, "kv_back", 58)
 
 
 CHUNK = 2 * PIECE
@@ -308,7 +308,7 @@
     return touched, full
 
 
-def forward_kernel(swaps, first, last, info_ref, base_ref, zl_ref, *refs):
+def forward_kernel(swaps, first, last, offset, stride, n_kept, info_ref, base_ref, zl_ref, *refs):
     refs = list(refs)
     n_blocks = len(swaps)
     query_ref, low_ref, high_ref = refs[:3]
@@ -316,13 +316,14 @@
     refs = refs[3 + n_blocks :]
     if not first:
         acc_in = refs.pop(0)
+    refs = refs[n_kept:]
     if last:
         mixed_ref = refs.pop(0)
     kept_ref = refs.pop(0)
     key_scratch, value_scratch, acc, top = refs
-    i = pl.program_id(0)
-
-    @pl.when(i == 0)
+    i = offset + stride * pl.program_id(0)
+
+    @pl.when(pl.program_id(0) == 0)
     def _():
         unpack_kv(swaps, block_refs, key_scratch, value_scratch)
 
@@ -379,29 +380,32 @@
             kept_ref[j, 0] = jnp.where(lane == HEAD + 1, top[j], acc[j])
 
 
-def attend(query, low, high, info, bases, zl, blocks, swaps, state, last):
+def attend(query, low, high, info, bases, zl, blocks, swaps, state, last, offset=0, stride=1, kept=()):
     count = query.shape[1]
     n_keys = sum(b.shape[0] for b in blocks)
-    per_piece = pl.BlockSpec((2, 1, CHUNK, LANES), lambda i, *_: (0, i, 0, 0))
-    bound = pl.BlockSpec((1, PIECE, LANES), lambda i, *_: (i, 0, 0))
+    per_piece = pl.BlockSpec((2, 1, CHUNK, LANES), lambda i, *_: (0, offset + stride * i, 0, 0))
+    bound = pl.BlockSpec((1, PIECE, LANES), lambda i, *_: (offset + stride * i, 0, 0))
     in_specs = [per_piece, bound, bound]
     in_specs += [pl.BlockSpec(b.shape, lambda i, *_: (0, 0)) for b in blocks]
     args = [query, low, high, *blocks]
     if state is not None:
         in_specs.append(per_piece)
         args.append(state)
+    aliases = {3 + len(args) + n: n for n in range(len(kept))}
+    in_specs += [pl.BlockSpec(memory_space=pl.ANY)] * len(kept)
+    args += list(kept)
     wide = jax.ShapeDtypeStruct((2, count, CHUNK, LANES), F32)
     if last:
         out_shape = [jax.ShapeDtypeStruct((2, count, PIECE, 2 * HEAD), BF), wide]
-        out_specs = [pl.BlockSpec((2, 1, PIECE, 2 * HEAD), lambda i, *_: (0, i, 0, 0)), per_piece]
+        out_specs = [pl.BlockSpec((2, 1, PIECE, 2 * HEAD), lambda i, *_: (0, offset + stride * i, 0, 0)), per_piece]
     else:
         out_shape = wide
         out_specs = per_piece
     return pl.pallas_call(
-        functools.partial(forward_kernel, swaps, state is None, last),
+        functools.partial(forward_kernel, swaps, state is None, last, offset, stride, len(kept)),
         grid_spec=pltpu.PrefetchScalarGridSpec(
             num_scalar_prefetch=3,
-            grid=(count,),
+            grid=(count // stride,),
             in_specs=in_specs,
             out_specs=out_specs,
             scratch_shapes=[
@@ -412,6 +416,7 @@
             ],
         ),
         out_shape=out_shape,
+        input_output_aliases=aliases,
         compiler_params=params(48),
         cost_estimate=cost(n_keys / 100),
         name="attend",
@@ -436,9 +441,10 @@
     return out.astype(BF)
 
 
-def prepare_kernel(m0, m1, m2, m3, w0, w1, kept_ref, query_ref, q_aug_ref, o_aug_ref, mid_ref):
+def prepare_kernel(n_kept, m0, m1, w0, w1, kept_ref, query_ref, *refs):
+    q_aug_ref, o_aug_ref, mid_ref = refs[n_kept:]
     step = pl.program_id(0)
-    for k, ref in enumerate((m0, m1, m2, m3)):
+    for k, ref in enumerate((m0, m1)):
 
         @pl.when(step == k)
         def _():
@@ -454,26 +460,27 @@
         o_aug_ref[j, 0] = augment(wide, -delta)
 
 
-def prepare_back(mid, weights, tile, kept, query):
-    count = len(mid)
+def prepare_back(mid, offset, weights, tile, kept, query, done=()):
     rows, width = mid[0].shape
-    per_piece = pl.BlockSpec((2, 1, CHUNK, LANES), lambda i: (0, i, 0, 0))
-    return pl.pallas_call(
-        prepare_kernel,
-        grid=(count,),
-        in_specs=[pl.BlockSpec((rows, width), lambda i: (0, 0))] * count
+    per_piece = pl.BlockSpec((2, 1, CHUNK, LANES), lambda i: (0, offset + 2 * i, 0, 0))
+    return pl.pallas_call(
+        functools.partial(prepare_kernel, len(done)),
+        grid=(2,),
+        in_specs=[pl.BlockSpec((rows, width), lambda i: (0, 0))] * 2
         + [pl.BlockSpec((width, 256), lambda i: (0, tile))] * 2
-        + [per_piece, per_piece],
+        + [per_piece, per_piece]
+        + [pl.BlockSpec(memory_space=pl.ANY)] * len(done),
         out_specs=[per_piece, per_piece],
         out_shape=[jax.ShapeDtypeStruct(query.shape, BF)] * 2,
         scratch_shapes=[pltpu.VMEM((rows, width), BF)],
+        input_output_aliases={6 + n: n for n in range(len(done))},
         compiler_params=params(58),
         cost_estimate=cost(6),
         name="prepare_back",
-    )(*mid, *weights, kept, query)
-
-
-def backward_kernel(swaps, has_dq, info_ref, base_ref, zl_ref, *refs):
+    )(*mid, *weights, kept, query, *done)
+
+
+def backward_kernel(swaps, has_dq, offset, stride, n_kept, info_ref, base_ref, zl_ref, *refs):
     refs = list(refs)
     n_blocks = len(swaps)
     q_aug, o_aug, low_ref, high_ref = refs[:4]
@@ -481,12 +488,13 @@
     refs = refs[4 + n_blocks :]
     if has_dq:
         dq_in = refs.pop(0)
+    refs = refs[n_kept:]
     dq_ref = refs.pop(0)
     out_refs = refs[:n_blocks]
     key_scratch, value_scratch, d_key, d_value = refs[n_blocks:]
-    i = pl.program_id(0)
-
-    @pl.when(i == 0)
+    i = offset + stride * pl.program_id(0)
+
+    @pl.when(pl.program_id(0) == 0)
     def _():
         unpack_kv(swaps, block_refs, key_scratch, value_scratch)
         d_key[...] = jnp.zeros(d_key.shape, F32)
@@ -529,7 +537,7 @@
         def _():
             visit(n, True)
 
-    @pl.when(i == pl.num_programs(0) - 1)
+    @pl.when(pl.program_id(0) == pl.num_programs(0) - 1)
     def _():
         at = 0
         for swap, ref in zip(swaps, out_refs):
@@ -542,22 +550,25 @@
                 at += CHUNK
 
 
-def attend_back(q_aug, o_aug, low, high, info, bases, zl, blocks, swaps, d_query, kinds):
+def attend_back(q_aug, o_aug, low, high, info, bases, zl, blocks, swaps, d_query, kinds, offset=0, stride=1, kept=()):
     count = q_aug.shape[1]
     n_keys = sum(b.shape[0] for b in blocks)
-    per_piece = pl.BlockSpec((2, 1, CHUNK, LANES), lambda i, *_: (0, i, 0, 0))
-    bound = pl.BlockSpec((1, 8, CHUNK), lambda i, *_: (i, 0, 0))
+    per_piece = pl.BlockSpec((2, 1, CHUNK, LANES), lambda i, *_: (0, offset + stride * i, 0, 0))
+    bound = pl.BlockSpec((1, 8, CHUNK), lambda i, *_: (offset + stride * i, 0, 0))
     whole = [pl.BlockSpec(b.shape, lambda i, *_: (0, 0)) for b in blocks]
     in_specs = [per_piece, per_piece, bound, bound, *whole]
     args = [q_aug, o_aug, low, high, *blocks]
     if d_query is not None:
         in_specs.append(per_piece)
         args.append(d_query)
-    return pl.pallas_call(
-        functools.partial(backward_kernel, swaps, d_query is not None),
+    aliases = {3 + len(args) + n: n for n in range(len(kept))}
+    in_specs += [pl.BlockSpec(memory_space=pl.ANY)] * len(kept)
+    args += list(kept)
+    return pl.pallas_call(
+        functools.partial(backward_kernel, swaps, d_query is not None, offset, stride, len(kept)),
         grid_spec=pltpu.PrefetchScalarGridSpec(
             num_scalar_prefetch=3,
-            grid=(count,),
+            grid=(count // stride,),
             in_specs=in_specs,
             out_specs=[per_piece, *whole],
             scratch_shapes=[
@@ -569,6 +580,7 @@
         ),
         out_shape=[jax.ShapeDtypeStruct((2, count, CHUNK, LANES), F32)]
         + [jax.ShapeDtypeStruct(b.shape, k) for b, k in zip(blocks, kinds)],
+        input_output_aliases=aliases,
         compiler_params=params(56),
         cost_estimate=cost(n_keys / 64),
         name="attend_back",
@@ -592,10 +604,10 @@
         gate = nn(norm_ref[...], gate_w)
         up = nn(norm_ref[...], up_w)
         d_hidden = nn(grad_ref[...], down_w)
-        sig = jax.nn.sigmoid(gate)
+        sig = 0.5 * jnp.tanh(0.5 * gate) + 0.5
         silu = gate * sig
         hidden = (silu * up).astype(BF)
-        d_gate = (d_hidden * up * sig * (1.0 + gate * (1.0 - sig))).astype(BF)
+        d_gate = (d_hidden * up * (sig + silu * (1.0 - sig))).astype(BF)
         d_up = (d_hidden * silu).astype(BF)
         hidden_ref[...] = hidden
         dg_ref[...] = d_gate
@@ -786,8 +798,7 @@
     step = pl.program_id(0)
     total = None
     for j, weight in enumerate((w0, w1)):
-        heads = jnp.concatenate([mixed_ref[j, 0], mixed_ref[j, 1]], 0)
-        term = nt(heads, weight[...][:, 0 : 2 * HEAD])
+        term = nt(mixed_ref[j, 0], weight[...][:, 0 : 2 * HEAD])
         total = term if total is None else total + term
 
     @pl.when(step == 0)
@@ -799,17 +810,17 @@
         near_ref[...] = total
 
 
-def output_projection(mixed, weights, tile):
+def output_projection(mixed, offset, weights, tile):
     _, count, rows, width_heads = mixed.shape
     width = weights[0].shape[0]
-    whole = pl.BlockSpec((2 * rows, width), lambda s: (0, 0))
+    whole = pl.BlockSpec((rows, width), lambda s: (0, 0))
     return pl.pallas_call(
         output_kernel,
         grid=(2,),
-        in_specs=[pl.BlockSpec((2, 2, rows, width_heads), lambda s: (0, 1 - s, 0, 0))]
+        in_specs=[pl.BlockSpec((2, 1, rows, width_heads), lambda s: (0, offset + 2 * (1 - s), 0, 0))]
         + [pl.BlockSpec((width, 256), lambda s: (0, tile))] * 2,
         out_specs=[whole, whole],
-        out_shape=[jax.ShapeDtypeStruct((2 * rows, width), BF), jax.ShapeDtypeStruct((2 * rows, width), F32)],
+        out_shape=[jax.ShapeDtypeStruct((rows, width), BF), jax.ShapeDtypeStruct((rows, width), F32)],
         compiler_params=params(58),
         cost_estimate=cost(4),
         name="output_projection",
@@ -983,10 +994,10 @@
     first_pair = ffn_pair[:, :up_at]
     up_pair, down_pair = ffn_pair[:, up_at : up_at + half], ffn_pair[:, up_at + half :]
     (
-        qkv_near, qkv_other, x_beside, ffn_pair, first_pair, up_pair, down_pair, cos_table, sin_table,
+        qkv_other, qkv_near, x_beside, ffn_pair, first_pair, up_pair, down_pair, cos_table, sin_table,
         info, low_wide, high_wide, low_rows, high_rows,
     ) = sync(
-        qkv_near, qkv_other, x_beside, ffn_pair, first_pair, up_pair, down_pair, cos_table, sin_table,
+        qkv_other, qkv_near, x_beside, ffn_pair, first_pair, up_pair, down_pair, cos_table, sin_table,
         info, low_wide, high_wide, low_rows, high_rows,
     )
     x_near = jnp.concatenate([inputs, x_beside], 0)
@@ -1051,9 +1062,9 @@
         far_bases.append(jnp.where(is_target, jnp.reshape(2 * (g + 1) * span, (1,)), far_away).astype(jnp.int32))
     same_bases, far_bases = jnp.concatenate(same_bases), jnp.concatenate(far_bases)
 
-    def step(blocks, bases, swap, state, last=False):
+    def step(blocks, bases, swap, state, *choice):
         swaps = [swap] * len(blocks)
-        return attend(query, low_wide, high_wide, info, bases, zl_info, blocks, swaps, state, last)
+        return attend(query, low_wide, high_wide, info, bases, zl_info, blocks, swaps, state, bool(choice), *choice)
 
     other = [flip(kv_chunks[0], "zh")]
     same = [lax.ppermute(kv, "g", shift_pairs(d)) for d in shifts]
@@ -1080,15 +1091,19 @@
     far_blocks, down_other, state = sync(far_blocks, down_other, state)
 
     second_far = all_groups(jnp.concatenate([up_other, down_other], 1))
-    mixed, kept = step(far_blocks, far_bases, 1, state, True)
+    o_tile = half // 256
+    mixed, kept = step(far_blocks, far_bases, 1, state, 1, 2)
     mixed, kept, first_far = sync(mixed, kept, first_far)
 
-    o_tile = half // 256
-    far_shares, near_shares = output_projection(mixed, (ffn_own, first_far), o_tile)
-    across = flip(far_shares, "c")
-    beside_sum = add_rows(near_shares, 1, across, 1)
+    far_share, near_share = output_projection(mixed, 1, (ffn_own, first_far), o_tile)
+    beside_sum = add_rows(near_share, 0, flip(far_share, "c"), 0)
+    beside_sum, state, mixed, kept = sync(beside_sum, state, mixed, kept)
     beside = flip(beside_sum, "zl")
-    after_attn, norm_own = sync(*forward_norm(inputs, near_shares, across, beside, gain_rows))
+    mixed, kept = step(far_blocks, far_bases, 1, state, 0, 2, (mixed, kept))
+    far_share, near_share = output_projection(mixed, 0, (ffn_own, first_far), o_tile)
+    across = flip(far_share, "c")
+    beside, near_share, across, mixed, kept = sync(beside, near_share, across, mixed, kept)
+    after_attn, norm_own = sync(*forward_norm(inputs, near_share, across, beside, gain_rows))
 
     norm_beside, norm_across = flip(norm_own, "zl"), flip(norm_own, "c")
     near_w = [(ffn_own, 0), (ffn_own, up_at), (ffn_own, up_at + half)]
@@ -1105,47 +1120,45 @@
     beside = flip(beside_sum, "zl")
     across = flip(early[3], "c")
     out_across = [flip(late[1], "c"), flip(early[1], "c")]
-    gate_up_part = weight_grad(
-        [(early[7], late[7], early[5], late[5]), (early[7], late[7], early[6], late[6])], 8
+    ffn_part = weight_grad(
+        [
+            (early[7], late[7], early[5], late[5]),
+            (early[7], late[7], early[6], late[6]),
+            (early[8], late[8], early[4], late[4]),
+        ],
+        12,
     )
-    beside, across, out_across, gate_up_part, early, late = sync(beside, across, out_across, gate_up_part, early, late)
-    gate_up_sum = over_groups(gate_up_part)
+    beside, across, out_across, ffn_part, early, late = sync(beside, across, out_across, ffn_part, early, late)
+    ffn_sum = over_groups(ffn_part)
     grad_mid, mid_low = backward_norm(1, early[2], across, beside, after_attn, out_cotangent, gain_rows, [F32, BF])
     grad_mid, mid_low, early, late = sync(grad_mid, mid_low, early, late)
 
     mid_beside, mid_across = flip(mid_low, "zl"), flip(mid_low, "c")
-    down_part = weight_grad([(early[8], late[8], early[4], late[4])], 4)
-    second_column = gain_columns([early[2], late[2], early[3], late[3]], [norm_own, norm_beside, norm_across, norm_both], 1)
-    out_sum = add_rows(late[0], 0, out_across[0], 0)
-    mid_beside, mid_across, down_part, second_column, out_sum = sync(
-        mid_beside, mid_across, down_part, second_column, out_sum
-    )
-    mid_rows = [mid_low, mid_beside, mid_across, flip(mid_beside, "c")]
-    q_aug, o_aug = prepare_back(mid_rows, (ffn_own, first_far), o_tile, kept, query)
-    q_aug, o_aug, mid_rows, out_sum, mixed, early, late = sync(q_aug, o_aug, mid_rows, out_sum, mixed, early, late)
-
-    def step_back(blocks, bases, swap, d_query, kinds):
+    out_w = (ffn_own, first_far)
+    aug = prepare_back([mid_low, mid_across], 0, out_w, o_tile, kept, query)
+
+    def step_back(blocks, bases, swap, d_query, kinds, *choice):
         swaps = [swap] * len(blocks)
-        out = attend_back(q_aug, o_aug, low_rows, high_rows, info, bases, zl_info, blocks, swaps, d_query, kinds)
+        out = attend_back(*aug, low_rows, high_rows, info, bases, zl_info, blocks, swaps, d_query, kinds, *choice)
         return out[0], list(out[1:])
 
     def other_half(summed):
         return flip(summed[:, summed.shape[1] // 2 :], "zh")
 
-    out_beside = flip(out_sum, "zl")
-    d_query, d_far = step_back(far_blocks, far_bases, 1, None, [BF] * len(far_blocks))
-    o_part = head_grad(mid_rows, mixed)
-    down_o_part = jnp.concatenate([down_part[:, :half], o_part[:, :256], down_part[:, half:], o_part[:, 256:]], 1)
-    out_beside, d_query, d_far, gate_up_sum, down_o_part, early, late = sync(
-        out_beside, d_query, d_far, gate_up_sum, down_o_part, early, late
-    )
-    down_o_sum = over_groups(down_o_part)
+    kinds = [BF] * len(far_blocks)
+    d_query, d_first = step_back(far_blocks, far_bases, 1, None, kinds, 0, 2)
+    mid_beside, mid_across, aug, d_query, d_first = sync(mid_beside, mid_across, aug, d_query, d_first)
+    mid_both = flip(mid_beside, "c")
+    aug = prepare_back([mid_beside, mid_both], 1, out_w, o_tile, kept, query, aug)
+    d_query, d_far = step_back(far_blocks, far_bases, 1, None, kinds, 1, 2, (d_query,))
+    d_far = [(a.astype(F32) + b.astype(F32)).astype(BF) for a, b in zip(d_first, d_far)]
+    mid_both, aug, d_query, d_far, early, late = sync(mid_both, aug, d_query, d_far, early, late)
 
     back = [lax.ppermute(d_far[2 * n + m], "g", reverse(shift_pairs(d))) for n, d in enumerate(shifts) for m in range(2)]
-    gate_up_far = other_half(gate_up_sum)
     d_query, d_other = step_back(other, other_bases, 1, d_query, [BF] * 2)
     d_query, d_same = step_back(same, same_bases, 0, d_query, [BF] * len(same))
-    d_query, d_other, d_same, d_far, back, gate_up_far = sync(d_query, d_other, d_same, d_far, back, gate_up_far)
+    out_sum = add_rows(late[0], 0, out_across[0], 0)
+    d_query, d_other, d_same, d_far, back, out_sum = sync(d_query, d_other, d_same, d_far, back, out_sum)
 
     other_sum = [d_other[m].astype(F32) for m in range(2)]
     for n in range(len(shifts)):
@@ -1158,52 +1171,64 @@
     if above_groups:
         above = lax.dynamic_slice_in_dim(d_far[-1], zl * rows, rows, 0)
         above_back.append(lax.ppermute(above, ("g", "zh"), reverse(above_pairs)))
+    out_beside = flip(out_sum, "zl")
     d_query, d_own = step_back([kv], own_bases, 0, d_query, [F32])
     core = jnp.reshape(2 * c + zl, (1,)).astype(jnp.int32)
     d_q, shares = query_back(core, d_query, qkv_w, cos_table, sin_table)
     q_part = head_grad([norm_one[k] for k in range(4)], d_q)
-    other_back, same_back, above_back, d_own, shares, q_part, other_late, early, late = sync(
-        other_back, same_back, above_back, d_own, shares, q_part, other_sum[1], early, late
-    )
 
     def group_slice(part, k):
         return lax.dynamic_slice_in_dim(part, (g ^ k) * shard_pair, shard_pair, 0)
 
+    q_slices = [group_slice(q_part, k) for k in range(groups)]
+    other_back, same_back, above_back, d_own, shares, q_slices, other_late, early, late, out_beside = sync(
+        other_back, same_back, above_back, d_own, shares, q_slices, other_sum[1], early, late, out_beside
+    )
+
     other_back.append(flip(other_late, "zh"))
-    q_got = [flip(group_slice(q_part, k), "g", k) for k in range(1, groups)]
-    layer_out = (after_attn + (early[0].astype(F32) + out_across[1].astype(F32) + out_beside.astype(F32))).astype(BF)
-    other_back, same_back, above_back, d_own, shares, q_part, q_got, down_o_sum, layer_out = sync(
-        other_back, same_back, above_back, d_own, shares, q_part, q_got, down_o_sum, layer_out
+    o_part = head_grad([mid_low, mid_beside, mid_across, mid_both], mixed)
+    second_column = gain_columns([early[2], late[2], early[3], late[3]], [norm_own, norm_beside, norm_across, norm_both], 1)
+    ffn_give = [ffn_sum[:, (3 + n) * half : (4 + n) * half] for n in range(3)]
+    q_got = [flip(q_slices[k], "g", k) for k in range(1, groups)]
+    other_back, same_back, above_back, d_own, shares, q_slices, q_got, o_part, second_column, ffn_sum, ffn_give = sync(
+        other_back, same_back, above_back, d_own, shares, q_slices, q_got, o_part, second_column, ffn_sum, ffn_give
     )
-
+    o_sum = over_groups(o_part)
+
+    gate_far = flip(ffn_give[0], "zh")
     d_kvs, shares = kv_back(core, d_own[0], other_back, same_back, above_back, shares, qkv_w, cos_table, sin_table)
     share_rows = shares.reshape(span, width)
-    across = flip(share_rows[2 * rows :], "c")
+    share_far = share_rows[2 * rows :]
+    gate_far, d_kvs, shares, share_rows, share_far, up_give = sync(gate_far, d_kvs, shares, share_rows, share_far, ffn_give[1])
+    up_far = flip(up_give, "zh")
+    across = flip(share_far, "c")
     kv_part = kv_grad(norm_one, shares, d_kvs, second_column)
+    kv_slices = [group_slice(kv_part, k) for k in range(groups)]
     beside_sum = add_rows(share_rows, 1, across, 1)
-    down_at = half + 256
-    down_far = flip(down_o_sum[:, down_at : down_at + half], "zh")
-    beside_sum, kv_part, across, share_rows, down_far, down_o_sum, gate_up_far, gate_up_sum = sync(
-        beside_sum, kv_part, across, share_rows, down_far, down_o_sum, gate_up_far, gate_up_sum
+    down_give = jnp.concatenate([ffn_give[2], o_sum[:, 256:]], 1)
+    down_give, beside_sum, kv_slices, across, share_rows, up_far, gate_far, ffn_sum = sync(
+        down_give, beside_sum, kv_slices, across, share_rows, up_far, gate_far, ffn_sum
     )
 
-    kv_got = [flip(group_slice(kv_part, k), "g", k) for k in range(1, groups)]
-    q_sum = group_slice(q_part, 0).astype(F32) + sum(v.astype(F32) for v in q_got)
+    kv_got = [flip(kv_slices[k], "g", k) for k in range(1, groups)]
+    q_sum = q_slices[0].astype(F32) + sum(v.astype(F32) for v in q_got)
     beside = flip(beside_sum, "zl")
-    o_far = flip(down_o_sum[:, down_at + half :], "zh")
-    middle = 2 * half
-    gu_own, gu_got = to_owner(gate_up_sum[:, :middle].astype(F32) + gate_up_far.astype(F32))
-    kv_got, q_sum, beside, gu_own, gu_got, o_far, down_far = sync(kv_got, q_sum, beside, gu_own, gu_got, o_far, down_far)
-
-    kv_sum = group_slice(kv_part, 0).astype(F32) + sum(v.astype(F32) for v in kv_got)
+    down_far = flip(down_give, "zh")
+    down_far, kv_got, q_sum, beside, o_sum, ffn_sum, gate_far, up_far = sync(
+        down_far, kv_got, q_sum, beside, o_sum, ffn_sum, gate_far, up_far
+    )
+
+    kv_sum = kv_slices[0].astype(F32) + sum(v.astype(F32) for v in kv_got)
     kvq_own = jnp.concatenate([kv_sum[:, :256], q_sum[:, :256]], 1)
     kvq_give = jnp.concatenate([kv_sum[:, 256:], q_sum[:, 256:]], 1).astype(BF)
-    kvq_own, kvq_give, o_far, down_far, beside = sync(kvq_own, kvq_give, o_far, down_far, beside)
-    down_o_far = jnp.concatenate([down_far, o_far], 1)
+    kvq_own, kvq_give, down_far, beside = sync(kvq_own, kvq_give, down_far, beside)
     kvq_far = flip(kvq_give, "zh")
     [input_grad] = backward_norm(0, share_rows, across, beside, inputs, grad_mid, gain_rows, [BF])
-    do_own, do_got = to_owner(down_o_sum[:, : half + 256].astype(F32) + down_o_far.astype(F32))
-    kvq_far, do_own, do_got, input_grad = sync(kvq_far, do_own, do_got, input_grad)
+    far_sum = jnp.concatenate([gate_far, up_far, down_far], 1).astype(F32)
+    near_sum = jnp.concatenate([ffn_sum[:, : 3 * half], o_sum[:, :256]], 1).astype(F32)
+    sum_own, sum_got = to_owner(near_sum + far_sum)
+    layer_out = (after_attn + (early[0].astype(F32) + out_across[1].astype(F32) + out_beside.astype(F32))).astype(BF)
+    kvq_far, sum_own, sum_got, input_grad, layer_out = sync(kvq_far, sum_own, sum_got, input_grad, layer_out)
 
     kvq_own, kvq_got = to_owner(kvq_own + kvq_far.astype(F32))
     gain_sums = (kvq_own + kvq_got)[:, 2 * HEAD : 2 * HEAD + 2]
@@ -1219,11 +1244,11 @@
         columns(kvq_own, kvq_got, 256, 2 * HEAD),
         columns(kvq_own, kvq_got, 0, HEAD),
         columns(kvq_own, kvq_got, HEAD, HEAD),
-        columns(do_own, do_got, half, 2 * HEAD).T,
+        columns(sum_own, sum_got, 3 * half, 2 * HEAD).T,
         gain_sums[:, 1] / second_gain.astype(F32),
-        columns(gu_own, gu_got, 0, half),
-        columns(gu_own, gu_got, half, half),
-        columns(do_own, do_got, 0, half).T,
+        columns(sum_own, sum_got, 0, half),
+        columns(sum_own, sum_got, half, half),
+        columns(sum_own, sum_got, 2 * half, half).T,
     )
 
 

time: 583 us -> 573 us (0.983)
  waiting for transfers between devices: 209 us -> 190 us
    reduce_scatter x2, waiting for transfers between devices: 16.4 us -> 0.01 us  [over_groups(): return lax.psum_scatter(value, 'g', scatter_dimension=0, tiled=True)]
    ppermute x51, waiting for transfers between devices: 159 us -> 148 us  [flip(): return lax.ppermute(value, axis, [(s, s ^ bit) for s in range(count)])]
    pallas_call x2 -> x4, Pallas kernels: 16.4 us -> 21.1 us  [the longest x2 12.3 us: prepare_back(): pl.pallas_call(functools.partial(prepare_kernel, len(done)), grid=(2,), i...]
    unnamed x227 -> x217, local copies, waits for them, and re-layouts: 28.3 us -> 31.4 us
    pallas_call x4 -> x5, Pallas kernels: 24.8 us -> 27.1 us  [attend(): pl.pallas_call(functools.partial(forward_kernel, swaps, state is None, la...]
    pallas_call x4 -> x5, Pallas kernels: 39.3 us -> 41.4 us  [attend_back(): pl.pallas_call(functools.partial(backward_kernel, swaps, d_query is not N...]
    pallas_call x2 -> x1, Pallas kernels: 15.9 us -> 16.8 us  [weight_grad(): pl.pallas_call(functools.partial(weight_grad_kernel, count), grid=(2, cou...]
  transfers between devices with their start and end apart: 64 -> 64, of which waited for: 36 -> 36; matrix products, arithmetic and copies ran while one was open for 8% -> 9% of each run, Pallas kernels for 28% -> 30%
where the time goes in v4:
time: 573 us; the launch traced here: 564 us
  waiting for transfers between devices  190 us (33%)
  Pallas kernels  190 us (33%)
  starting transfers between devices  75.3 us (13%)
  local copies, waits for them, and re-layouts  59.5 us (10%)
  other arithmetic  33.2 us (6%)
  between operations  15.7 us (3%)
    ppermute x51, waiting for transfers between devices, flip(): return lax.ppermute(value, axis, [(s, s ^ bit) for s in range(count)])  148 us
    ppermute x51, starting transfers between devices, flip(): return lax.ppermute(value, axis, [(s, s ^ bit) for s in range(count)])  53.7 us
    pallas_call x5, Pallas kernels, attend_back(): pl.pallas_call(functools.partial(backward_kernel, swaps, d_query is not N...  41.4 us
    pallas_call x2, Pallas kernels, feed_forward(): pl.pallas_call(functools.partial(ffn_kernel, tiles), grid=(2 * tiles,), i...  35 us
    unnamed x217, local copies, waits for them, and re-layouts  31.4 us
    pallas_call x5, Pallas kernels, attend(): pl.pallas_call(functools.partial(forward_kernel, swaps, state is None, la...  27.1 us
    pallas_call x1, Pallas kernels, weight_grad(): pl.pallas_call(functools.partial(weight_grad_kernel, count), grid=(2, cou...  16.8 us
    ppermute x2, waiting for transfers between devices, body(): lax.ppermute(d_far[2 * n + m], 'g', reverse(shift_pairs(d)))  14 us
  transfers between devices with their start and end apart: 64, of which 36 were waited for; matrix products, arithmetic and copies ran while one was open for 9% of the time, Pallas kernels for 30%

profile of v4, /device:TPU:0, one launch (start us, length us, event | category | flops | bytes accessed | tf_op | source)
XLA Modules:
  0.0 563.7 jit_solution(11217967920403998705)
XLA Ops:
  39.0 13.3 %collective-permute-done.2.refs_4_ = bf16[384,512]{1,0:T(8,128)(2,1)S(1)} collective-permute-done((bf16[384,512]{1,0:T(8,128)(2,1)}, bf16[384,512]{1,0:T(8,128)(2,1)S(1)}, u32[]{:S(2)}, u32[]{:S(2)}) %collective-permute-start.2) | collective-permute-done | bytes 393248 | tf_op jit(solution)/shard_map/ppermute | solution.py:61
  63.1 12.2 %collective-permute-done.7.refs_5_ = bf16[384,512]{1,0:T(8,128)(2,1)S(1)} collective-permute-done((bf16[384,512]{1,0:T(8,128)(2,1)S(1)}, bf16[384,512]{1,0:T(8,128)(2,1)S(1)}, u32[]{:S(2)}, u32[]{:S(2)}) %collective-permute-start.7) | collective-permute-done | bytes 393248 | tf_op jit(solution)/shard_map/ppermute | solution.py:61
  80.2 12.1 %collective-permute-done.9.refs_7_ = bf16[384,512]{1,0:T(8,128)(2,1)S(1)} collective-permute-done((bf16[384,512]{1,0:T(8,128)(2,1)S(1)}, bf16[384,512]{1,0:T(8,128)(2,1)S(1)}, u32[]{:S(2)}, u32[]{:S(2)}) %collective-permute-start.9) | collective-permute-done | bytes 393248 | tf_op jit(solution)/shard_map/ppermute | solution.py:61
  95.2 12.8 %project_qkv.1 = (bf16[4,256,1536]{2,1,0:T(8,128)(2,1)}, bf16[2,4,512,128]{3,2,1,0:T(8,128)(2,1)}, bf16[1024,384]{1,0:T(8,128)(2,1)}, bf16[2,1536,512]{2,1,0:T(8,128)(2,1)}, f32[8,1536]{1,0:T(8,128)}) custom-call(s32[8]{0:T(128)} %add.263.where_ref, bf16[384,512]{1,0:T(8,128)(2,1)} %pad_maximum_fusion.4.refs_0_, ...), custom_call_target="tpu_custom_call" | custom-call | flops 92000000 | bytes 288000 | tf_op jit(solution)/shard_map/project_qkv/pallas_call | solution.py:181
  111.2 6.5 %collective-permute-done.13 = bf16[384,512]{1,0:T(8,128)(2,1)} collective-permute-done((bf16[384,512]{1,0:T(8,128)(2,1)}, bf16[384,512]{1,0:T(8,128)(2,1)}, u32[]{:S(2)}, u32[]{:S(2)}) %collective-permute-start.13) | collective-permute-done | bytes 393248 | tf_op jit(solution)/shard_map/ppermute | solution.py:61
  126.8 7.8 %attend.5.refs_4_ = f32[2,4,512,128]{3,2,1,0:T(8,128)S(1)} custom-call(s32[4,4]{1,0:T(4,128)S(1)} %pad_add_fusion.info_ref, s32[2]{0:T(128)S(1)} %pad_add_fusion.2.base_ref, s32[1]{0:T(128)} %bitcast.19.zl_ref, bf16[2,4,512,128]{3,2,1,0:T(8,128)(2,1)S(1)} %copy-done, s32[4,256,128]{2,1,0:T(8,128)S(1)} %broadcast_in_dim.114.refs_1_, ...), custom_call_target="tpu_custom_call" | custom-call | flops 117760000 | bytes 368640 | tf_op jit(solution)/shard_map/attend/pallas_call | solution.py:404
  136.0 8.9 %collective-permute-done.14.refs_3_.refs_4_ = bf16[512,384]{1,0:T(8,128)(2,1)S(1)} collective-permute-done((bf16[512,384]{1,0:T(8,128)(2,1)}, bf16[512,384]{1,0:T(8,128)(2,1)S(1)}, u32[]{:S(2)}, u32[]{:S(2)}) %collective-permute-start.14) | collective-permute-done | bytes 393248 | tf_op jit(solution)/shard_map/ppermute | solution.py:61
  217.2 8.2 %collective-permute-done.24.beside_ref = bf16[256,1536]{1,0:T(8,128)(2,1)S(1)} collective-permute-done((bf16[256,1536]{1,0:T(8,128)(2,1)S(1)}, bf16[256,1536]{1,0:T(8,128)(2,1)S(1)}, u32[]{:S(2)}, u32[]{:S(2)}) %collective-permute-start.24) | collective-permute-done | bytes 786464 | tf_op jit(solution)/shard_map/ppermute | solution.py:61
  229.9 13.1 %all-gather.8.cloned.1.call-done.refs_4_.refs_5_ = bf16[1536,1024]{1,0:T(8,128)(2,1)} async-done(((bf16[384,1024]{1,0:T(8,128)(2,1)}), bf16[1536,1024]{1,0:T(8,128)(2,1)}) %all-gather.8.cloned.1.call-update) | async-done | bytes 3145744 | tf_op jit(solution)/shard_map/all_gather | solution.py:56
  242.9 17.5 %feed_forward.2 = (bf16[256,1536]{1,0:T(8,128)(2,1)}, bf16[256,1536]{1,0:T(8,128)(2,1)}, bf16[256,1536]{1,0:T(8,128)(2,1)}, bf16[256,1536]{1,0:T(8,128)(2,1)}, b...) custom-call(bf16[256,1536]{1,0:T(8,128)(2,1)} %copy-done.27, ...), custom_call_target="tpu_custom_call" | custom-call | flops 207000000 | bytes 648000 | tf_op jit(solution)/shard_map/feed_forward/pallas_call | solution.py:661
  263.9 17.6 %feed_forward.3 = (bf16[256,1536]{1,0:T(8,128)(2,1)}, bf16[256,1536]{1,0:T(8,128)(2,1)}, bf16[256,1536]{1,0:T(8,128)(2,1)}, bf16[256,1536]{1,0:T(8,128)(2,1)}, b...) custom-call(bf16[256,1536]{1,0:T(8,128)(2,1)} %collective-permute-do, ...), custom_call_target="tpu_custom_call" | custom-call | flops 207000000 | bytes 648000 | tf_op jit(solution)/shard_map/feed_forward/pallas_call | solution.py:661
  288.3 16.8 %weight_grad.1 = bf16[1536,3072]{1,0:T(8,128)(2,1)} custom-call(bf16[1536,512]{1,0:T(8,128)(2,1)} %get-tuple-element.416.refs_0_.refs_4_, bf16[1536,512]{1,0:T(8,128)(2,1)} %get-tuple-element.417.refs_1_.refs_5_, bf16[512,1024]{1,0:T(8,128)(2,1)S(1)} %copy-done.59, bf16[512,1024]{1,0:T(8,128)(2,1)S(1)} %copy-done.61, ...), custom_call_target="tpu_custom_call" | custom-call | flops 138000000 | bytes 432000 | tf_op jit(solution)/shard_map/weight_grad/pallas_call | solution.py:693
  354.8 9.2 %attend_back.7 = (f32[2,4,512,128]{3,2,1,0:T(8,128)}, bf16[512,384]{1,0:T(8,128)(2,1)}, bf16[512,384]{1,0:T(8,128)(2,1)}) custom-call(s32[4,4]{1,0:T(4,128)} %copy-done.69, s32[2]{0:T(128)} %copy-done.73, s32[1]{0:T(128)} %bitcast.19.zl_ref, bf16[2,4,512,128]{3,2,1,0:T(8,128)(2,1)} %get-tuple-element.471.refs_0_, ...), custom_call_target="tpu_custom_call" | custom-call | flops 184000000 | bytes 576000 | tf_op jit(solution)/shard_map/attend_back/pallas_call | solution.py:567
  374.0 10.4 %collective-permute-done.38 = bf16[512,384]{1,0:T(8,128)(2,1)S(1)} collective-permute-done((bf16[512,384]{1,0:T(8,128)(2,1)S(1)}, bf16[512,384]{1,0:T(8,128)(2,1)S(1)}, u32[]{:S(2)}, u32[]{:S(2)}) %collective-permute-start.38) | collective-permute-done | bytes 393248 | tf_op jit(solution)/shard_map/ppermute | solution.py:1157
  392.1 16.2 %attend_back.9 = (f32[2,4,512,128]{3,2,1,0:T(8,128)}, f32[1024,384]{1,0:T(8,128)}) custom-call(s32[4,4]{1,0:T(4,128)} %copy-done.69, s32[2]{0:T(128)} %copy-done.72, s32[1]{0:T(128)} %bitcast.19.zl_ref, bf16[2,4,512,128]{3,2,1,0:T(8,128)(2,1)} %get-tuple-element.471.refs_0_, bf16[2,4,512,128]{3,2,1,0:T(8,128)(2,1)} %get-tuple-element.472.refs_1_, ...), custom_call_target="tpu_custom_call" | custom-call | flops 184000000 | bytes 576000 | tf_op jit(solution)/shard_map/attend_back/pallas_call | solution.py:567
  417.1 7.4 %collective-permute-done.40.refs_3_ = bf16[1024,384]{1,0:T(8,128)(2,1)} collective-permute-done((bf16[1024,384]{1,0:T(8,128)(2,1)}, bf16[1024,384]{1,0:T(8,128)(2,1)}, u32[]{:S(2)}, u32[]{:S(2)}) %collective-permute-start.40) | collective-permute-done | bytes 786464 | tf_op jit(solution)/shard_map/ppermute | solution.py:1169
  424.5 8.5 %collective-permute-start.43 = (bf16[512,384]{1,0:T(8,128)(2,1)}, bf16[512,384]{1,0:T(8,128)(2,1)}, u32[]{:S(2)}, u32[]{:S(2)}) collective-permute-start(bf16[512,384]{1,0:T(8,128)(2,1)} %add_convert_fusion.1), channel_id=1, source_target_pairs={{0,2},{2,0},{1,3},{3,1},{4,6},{6,4},{5,7},{7,5},{8,10},{10,8},{9,1... | collective-permute-start | bytes 1179656 | tf_op jit(solution)/shard_map/ppermute | solution.py:61
  452.4 8.8 %kv_back.1 = (bf16[2,4,256,192]{3,2,1,0:T(8,128)(2,1)}, bf16[4,256,1536]{2,1,0:T(8,128)(2,1)}) custom-call(s32[1]{0:T(128)} %bitcast.27.core_ref, f32[1024,384]{1,0:T(8,128)} %get-tuple-element.526.refs_0_, bf16[512,384]{1,0:T(8,128)(2,1)} %collective-permute-done.39.refs_1_, bf16[512,384]{1,0:T(8,128)(2,1)} %collective-permute-done.43.refs_2_, ...), custom_call_target="tpu_custom_call" | custom-call | flops 46000000 | bytes 144000 | tf_op jit(solution)/shard_map/kv_back/pallas_call | solution.py:251
  462.9 8.5 %collective-permute-done.47 = bf16[384,512]{1,0:T(8,128)(2,1)} collective-permute-done((bf16[384,512]{1,0:T(8,128)(2,1)}, bf16[384,512]{1,0:T(8,128)(2,1)}, u32[]{:S(2)}, u32[]{:S(2)}) %collective-permute-start.47) | collective-permute-done | bytes 393248 | tf_op jit(solution)/shard_map/ppermute | solution.py:61
  484.6 6.7 %collective-permute-done.49 = bf16[384,512]{1,0:T(8,128)(2,1)} collective-permute-done((bf16[384,512]{1,0:T(8,128)(2,1)}, bf16[384,512]{1,0:T(8,128)(2,1)}, u32[]{:S(2)}, u32[]{:S(2)}) %collective-permute-start.49) | collective-permute-done | bytes 393248 | tf_op jit(solution)/shard_map/ppermute | solution.py:61
  499.4 7.3 %collective-permute-done.51 = bf16[384,512]{1,0:T(8,128)(2,1)} collective-permute-done((bf16[384,512]{1,0:T(8,128)(2,1)}, bf16[384,512]{1,0:T(8,128)(2,1)}, u32[]{:S(2)}, u32[]{:S(2)}) %collective-permute-start.51) | collective-permute-done | bytes 393248 | tf_op jit(solution)/shard_map/ppermute | solution.py:61
  506.7 7.6 %collective-permute-done.52 = bf16[384,512]{1,0:T(8,128)(2,1)} collective-permute-done((bf16[384,512]{1,0:T(8,128)(2,1)}, bf16[384,512]{1,0:T(8,128)(2,1)}, u32[]{:S(2)}, u32[]{:S(2)}) %collective-permute-start.52) | collective-permute-done | bytes 393248 | tf_op jit(solution)/shard_map/ppermute | solution.py:61
  514.3 7.3 %collective-permute-done.50 = bf16[384,768]{1,0:T(8,128)(2,1)} collective-permute-done((bf16[384,768]{1,0:T(8,128)(2,1)}, bf16[384,768]{1,0:T(8,128)(2,1)}, u32[]{:S(2)}, u32[]{:S(2)}) %collective-permute-start.50) | collective-permute-done | bytes 589856 | tf_op jit(solution)/shard_map/ppermute | solution.py:61
  535.5 9.6 %collective-permute-done.55 = bf16[384,512]{1,0:T(8,128)(2,1)S(1)} collective-permute-done((bf16[384,512]{1,0:T(8,128)(2,1)S(1)}, bf16[384,512]{1,0:T(8,128)(2,1)S(1)}, u32[]{:S(2)}, u32[]{:S(2)}) %collective-permute-start.55) | collective-permute-done | bytes 393248 | tf_op jit(solution)/shard_map/ppermute | solution.py:61
  (475 shorter events, 293.9 us)
Async XLA Ops:
  7.2 158.8 %all-gather.4.cloned.1.call-start = ((), (), s32[]{:S(2)}) async-start(), calls=%async_computation.2 | async-start | bytes 6881280 | tf_op jit(solution)/shard_map/all_gather | solution.py:56
  23.7 29.2 %collective-permute-start.6 = (bf16[256,1536]{1,0:T(8,128)(2,1)S(1)}, bf16[256,1536]{1,0:T(8,128)(2,1)S(1)}, u32[]{:S(2)}, u32[]{:S(2)}) collective-permute-start(bf16[256,1536]{1,0:T(8,128)(2,1)S(1)} %copy-done.10), channel_id=1, source_target_pairs={{0,1},{1,0},{2,3},{3,2},{4,5},{5,4},{6,7},{7,6},{8,9},{9,8},{10,11... | collective-permute-start | bytes 2359304 | tf_op jit(solution)/shard_map/ppermute | solution.py:61
  29.2 23.0 %collective-permute-start.2 = (bf16[384,512]{1,0:T(8,128)(2,1)}, bf16[384,512]{1,0:T(8,128)(2,1)S(1)}, u32[]{:S(2)}, u32[]{:S(2)}) collective-permute-start(bf16[384,512]{1,0:T(8,128)(2,1)} %pad_maximum_fusion.4.refs_0_), channel_id=1, source_target_pairs={{0,2},{2,0},{1,3},{3,1},{4,6},{6,4},{5,7},{7,5},{8,10},{10,8},{9,1... | collective-permute-start | bytes 1179656 | tf_op jit(solution)/shard_map/ppermute | solution.py:61
  55.5 141.8 %all-gather.6.cloned.1.call-start = ((), (), s32[]{:S(2)}) async-start(), calls=%async_computation.3 | async-start | bytes 2949120 | tf_op jit(solution)/shard_map/all_gather | solution.py:56
  56.9 35.4 %collective-permute-start.10 = (bf16[512,1536]{1,0:T(8,128)(2,1)}, bf16[512,1536]{1,0:T(8,128)(2,1)}, u32[]{:S(2)}, u32[]{:S(2)}) collective-permute-start(bf16[512,1536]{1,0:T(8,128)(2,1)} %pad_maximum_fusion), channel_id=1, source_target_pairs={{0,4},{4,0},{1,5},{5,1},{2,6},{6,2},{3,7},{7,3},{8,12},{12,8},{9,1... | collective-permute-start | bytes 4718600 | tf_op jit(solution)/shard_map/ppermute | solution.py:61
  56.9 35.4 %collective-permute-start.11 = (bf16[384,768]{1,0:T(8,128)(2,1)S(1)}, bf16[384,768]{1,0:T(8,128)(2,1)S(1)}, u32[]{:S(2)}, u32[]{:S(2)}) collective-permute-start(bf16[384,768]{1,0:T(8,128)(2,1)S(1)} %copy-done.84), channel_id=1, source_target_pairs={{0,2},{2,0},{1,3},{3,1},{4,6},{6,4},{5,7},{7,5},{8,10},{10,8},{9,1... | collective-permute-start | bytes 1769480 | tf_op jit(solution)/shard_map/ppermute | solution.py:61
  62.7 29.6 %collective-permute-start.9 = (bf16[384,512]{1,0:T(8,128)(2,1)S(1)}, bf16[384,512]{1,0:T(8,128)(2,1)S(1)}, u32[]{:S(2)}, u32[]{:S(2)}) collective-permute-start(bf16[384,512]{1,0:T(8,128)(2,1)S(1)} %copy-done.94), channel_id=1, source_target_pairs={{0,24},{8,16},{16,8},{24,0},{1,25},{9,17},{17,9},{25,1},{2,26},{10... | collective-permute-start | bytes 1179656 | tf_op jit(solution)/shard_map/ppermute | solution.py:61
  92.3 26.3 %collective-permute-start.12 = (bf16[256,1536]{1,0:T(8,128)(2,1)}, bf16[256,1536]{1,0:T(8,128)(2,1)}, u32[]{:S(2)}, u32[]{:S(2)}) collective-permute-start(bf16[256,1536]{1,0:T(8,128)(2,1)} %base_ref), channel_id=1, source_target_pairs={{0,1},{1,0},{2,3},{3,2},{4,5},{5,4},{6,7},{7,6},{8,9},{9,8},{10,11... | collective-permute-start | bytes 2359304 | tf_op jit(solution)/shard_map/ppermute | solution.py:61
  94.0 23.7 %collective-permute-start.13 = (bf16[384,512]{1,0:T(8,128)(2,1)}, bf16[384,512]{1,0:T(8,128)(2,1)}, u32[]{:S(2)}, u32[]{:S(2)}) collective-permute-start(bf16[384,512]{1,0:T(8,128)(2,1)} %get-tuple-element.321), channel_id=1, source_target_pairs={{0,2},{2,0},{1,3},{3,1},{4,6},{6,4},{5,7},{7,5},{8,10},{10,8},{9,1... | collective-permute-start | bytes 1179656 | tf_op jit(solution)/shard_map/ppermute | solution.py:61
  118.6 124.4 %all-gather.8.cloned.1.call-start = ((), (), s32[]{:S(2)}) async-start(), calls=%async_computation.4 | async-start | bytes 3932160 | tf_op jit(solution)/shard_map/all_gather | solution.py:56
  118.6 27.7 %collective-permute-start.15 = (bf16[1024,384]{1,0:T(8,128)(2,1)S(1)}, bf16[1024,384]{1,0:T(8,128)(2,1)}, u32[]{:S(2)}, u32[]{:S(2)}) collective-permute-start(bf16[1024,384]{1,0:T(8,128)(2,1)S(1)} %copy-done.18), channel_id=1, source_target_pairs={{0,8},{1,9},{2,10},{3,11},{4,12},{5,13},{6,14},{7,15}} | collective-permute-start | bytes 2359304 | tf_op jit(solution)/shard_map/ppermute | solution.py:1070
  126.4 33.5 %collective-permute-start.19 = (bf16[256,1536]{1,0:T(8,128)(2,1)}, bf16[256,1536]{1,0:T(8,128)(2,1)}, u32[]{:S(2)}, u32[]{:S(2)}) collective-permute-start(bf16[256,1536]{1,0:T(8,128)(2,1)} %collective-permute-done.12.g0), channel_id=1, source_target_pairs={{0,4},{4,0},{1,5},{5,1},{2,6},{6,2},{3,7},{7,3},{8,12},{12,8},{9,1... | collective-permute-start | bytes 2359304 | tf_op jit(solution)/shard_map/ppermute | solution.py:61
  191.7 255.7 %reduce-scatter.3.cloned.1.call-start = ((), (), s32[]{:S(2)}) async-start(), calls=%async_computation.5 | async-start | bytes 11796480 | tf_op jit(solution)/shard_map/reduce_scatter | solution.py:97
  227.6 32.8 %collective-permute-start.26 = (bf16[256,1536]{1,0:T(8,128)(2,1)S(1)}, bf16[256,1536]{1,0:T(8,128)(2,1)}, u32[]{:S(2)}, u32[]{:S(2)}) collective-permute-start(bf16[256,1536]{1,0:T(8,128)(2,1)S(1)} %get-tuple-element.370.n0.refs_4_), channel_id=1, source_target_pairs={{0,1},{1,0},{2,3},{3,2},{4,5},{5,4},{6,7},{7,6},{8,9},{9,8},{10,11... | collective-permute-start | bytes 2359304 | tf_op jit(solution)/shard_map/ppermute | solution.py:61
  306.2 175.6 %reduce-scatter.5.cloned.1.call-start = ((), (), s32[]{:S(2)}) async-start(), calls=%async_computation.6 | async-start | bytes 1966080 | tf_op jit(solution)/shard_map/reduce_scatter | solution.py:97
  348.1 25.9 %collective-permute-start.37 = (bf16[512,384]{1,0:T(8,128)(2,1)S(1)}, bf16[512,384]{1,0:T(8,128)(2,1)S(1)}, u32[]{:S(2)}, u32[]{:S(2)}) collective-permute-start(bf16[512,384]{1,0:T(8,128)(2,1)S(1)} %add_convert_fusion.5), channel_id=1, source_target_pairs={{8,0},{9,1},{10,2},{11,3},{12,4},{13,5},{14,6},{15,7}} | collective-permute-start | bytes 1179656 | tf_op jit(solution)/shard_map/ppermute | solution.py:1157
  349.6 34.9 %collective-permute-start.38 = (bf16[512,384]{1,0:T(8,128)(2,1)S(1)}, bf16[512,384]{1,0:T(8,128)(2,1)S(1)}, u32[]{:S(2)}, u32[]{:S(2)}) collective-permute-start(bf16[512,384]{1,0:T(8,128)(2,1)S(1)} %add_convert_fusion.4), channel_id=1, source_target_pairs={{8,0},{9,1},{10,2},{11,3},{12,4},{13,5},{14,6},{15,7}} | collective-permute-start | bytes 1179656 | tf_op jit(solution)/shard_map/ppermute | solution.py:1157
  384.4 40.1 %collective-permute-start.40 = (bf16[1024,384]{1,0:T(8,128)(2,1)}, bf16[1024,384]{1,0:T(8,128)(2,1)}, u32[]{:S(2)}, u32[]{:S(2)}) collective-permute-start(bf16[1024,384]{1,0:T(8,128)(2,1)} %get-tuple-element.486), channel_id=1, source_target_pairs={{8,0},{9,1},{10,2},{11,3},{12,4},{13,5},{14,6},{15,7}} | collective-permute-start | bytes 2359304 | tf_op jit(solution)/shard_map/ppermute | solution.py:1169
  385.7 38.8 %collective-permute-start.42 = (bf16[256,1536]{1,0:T(8,128)(2,1)}, bf16[256,1536]{1,0:T(8,128)(2,1)}, u32[]{:S(2)}, u32[]{:S(2)}) collective-permute-start(bf16[256,1536]{1,0:T(8,128)(2,1)} %add_rows.6), channel_id=1, source_target_pairs={{0,1},{1,0},{2,3},{3,2},{4,5},{5,4},{6,7},{7,6},{8,9},{9,8},{10,11... | collective-permute-start | bytes 2359304 | tf_op jit(solution)/shard_map/ppermute | solution.py:61
  387.4 29.7 %collective-permute-start.39 = (bf16[512,384]{1,0:T(8,128)(2,1)S(1)}, bf16[512,384]{1,0:T(8,128)(2,1)}, u32[]{:S(2)}, u32[]{:S(2)}) collective-permute-start(bf16[512,384]{1,0:T(8,128)(2,1)S(1)} %add_convert_fusion.2), channel_id=1, source_target_pairs={{0,2},{2,0},{1,3},{3,1},{4,6},{6,4},{5,7},{7,5},{8,10},{10,8},{9,1... | collective-permute-start | bytes 1179656 | tf_op jit(solution)/shard_map/ppermute | solution.py:61
  389.9 27.2 %collective-permute-start.41 = (bf16[256,384]{1,0:T(8,128)(2,1)S(1)}, bf16[256,384]{1,0:T(8,128)(2,1)}, u32[]{:S(2)}, u32[]{:S(2)}) collective-permute-start(bf16[256,384]{1,0:T(8,128)(2,1)S(1)} %constant_dynamic-slice_fusion.9), channel_id=1, source_target_pairs={{2,8},{3,9},{6,12},{7,13}} | collective-permute-start | bytes 589832 | tf_op jit(solution)/shard_map/ppermute | solution.py:1173
  424.5 25.9 %collective-permute-start.43 = (bf16[512,384]{1,0:T(8,128)(2,1)}, bf16[512,384]{1,0:T(8,128)(2,1)}, u32[]{:S(2)}, u32[]{:S(2)}) collective-permute-start(bf16[512,384]{1,0:T(8,128)(2,1)} %add_convert_fusion.1), channel_id=1, source_target_pairs={{0,2},{2,0},{1,3},{3,1},{4,6},{6,4},{5,7},{7,5},{8,10},{10,8},{9,1... | collective-permute-start | bytes 1179656 | tf_op jit(solution)/shard_map/ppermute | solution.py:61
  491.3 32.5 %collective-permute-start.54 = (bf16[256,1536]{1,0:T(8,128)(2,1)}, bf16[256,1536]{1,0:T(8,128)(2,1)}, u32[]{:S(2)}, u32[]{:S(2)}) collective-permute-start(bf16[256,1536]{1,0:T(8,128)(2,1)} %add_rows.7), channel_id=1, source_target_pairs={{0,1},{1,0},{2,3},{3,2},{4,5},{5,4},{6,7},{7,6},{8,9},{9,8},{10,11... | collective-permute-start | bytes 2359304 | tf_op jit(solution)/shard_map/ppermute | solution.py:61
  491.3 30.3 %collective-permute-start.50 = (bf16[384,768]{1,0:T(8,128)(2,1)}, bf16[384,768]{1,0:T(8,128)(2,1)}, u32[]{:S(2)}, u32[]{:S(2)}) collective-permute-start(bf16[384,768]{1,0:T(8,128)(2,1)} %pad_maximum_fusion.3), channel_id=1, source_target_pairs={{0,2},{2,0},{1,3},{3,1},{4,6},{6,4},{5,7},{7,5},{8,10},{10,8},{9,1... | collective-permute-start | bytes 1769480 | tf_op jit(solution)/shard_map/ppermute | solution.py:61
  (150 other events, 1703.9 us)
Sparse Core Ops, SparseCore 0:
  55.6 81.6 all-gather.3
  139.7 50.7 all-gather.5
  193.0 49.9 all-gather.7
  306.3 118.1 reduce-scatter.2
  452.0 28.5 reduce-scatter.4

commit v5 on v4

--- a/solution.py
+++ b/solution.py
@@ -480,7 +480,7 @@
     )(*mid, *weights, kept, query, *done)
 
 
-def backward_kernel(swaps, has_dq, offset, stride, n_kept, info_ref, base_ref, zl_ref, *refs):
+def backward_kernel(swaps, has_dq, offset, stride, n_kept, n_more, info_ref, base_ref, zl_ref, *refs):
     refs = list(refs)
     n_blocks = len(swaps)
     q_aug, o_aug, low_ref, high_ref = refs[:4]
@@ -488,7 +488,7 @@
     refs = refs[4 + n_blocks :]
     if has_dq:
         dq_in = refs.pop(0)
-    refs = refs[n_kept:]
+    more_refs, refs = refs[:n_more], refs[n_more + n_kept :]
     dq_ref = refs.pop(0)
     out_refs = refs[:n_blocks]
     key_scratch, value_scratch, d_key, d_value = refs[n_blocks:]
@@ -540,17 +540,20 @@
     @pl.when(pl.program_id(0) == pl.num_programs(0) - 1)
     def _():
         at = 0
-        for swap, ref in zip(swaps, out_refs):
+        for n, (swap, ref) in enumerate(zip(swaps, out_refs)):
             for start in range(0, ref.shape[0], CHUNK):
                 parts = []
                 for j in (swap, 1 - swap):
                     parts.append(d_key[j, at : at + CHUNK, :][:, 0:HEAD])
                     parts.append(d_value[j, at : at + CHUNK, :][:, 0:HEAD])
-                ref[start : start + CHUNK, :] = jnp.concatenate(parts, 1).astype(ref.dtype)
+                whole = jnp.concatenate(parts, 1)
+                if n_more:
+                    whole = whole + more_refs[n][start : start + CHUNK, :].astype(F32)
+                ref[start : start + CHUNK, :] = whole.astype(ref.dtype)
                 at += CHUNK
 
 
-def attend_back(q_aug, o_aug, low, high, info, bases, zl, blocks, swaps, d_query, kinds, offset=0, stride=1, kept=()):
+def attend_back(q_aug, o_aug, low, high, info, bases, zl, blocks, swaps, d_query, kinds, offset=0, stride=1, kept=(), more=()):
     count = q_aug.shape[1]
     n_keys = sum(b.shape[0] for b in blocks)
     per_piece = pl.BlockSpec((2, 1, CHUNK, LANES), lambda i, *_: (0, offset + stride * i, 0, 0))
@@ -561,11 +564,13 @@
     if d_query is not None:
         in_specs.append(per_piece)
         args.append(d_query)
+    in_specs += [pl.BlockSpec(m.shape, lambda i, *_: (0, 0)) for m in more]
+    args += list(more)
     aliases = {3 + len(args) + n: n for n in range(len(kept))}
     in_specs += [pl.BlockSpec(memory_space=pl.ANY)] * len(kept)
     args += list(kept)
     return pl.pallas_call(
-        functools.partial(backward_kernel, swaps, d_query is not None, offset, stride, len(kept)),
+        functools.partial(backward_kernel, swaps, d_query is not None, offset, stride, len(kept), len(more)),
         grid_spec=pltpu.PrefetchScalarGridSpec(
             num_scalar_prefetch=3,
             grid=(count // stride,),
@@ -1009,7 +1014,6 @@
     qkv_far, x_far, first_other, up_pair, out_cotangent = sync(qkv_far, x_far, first_other, up_pair, out_cotangent)
 
     up_other = flip(up_pair, "zh")
-    g_beside = flip(out_cotangent, "zl")
     k_order = jnp.array([0, *hops, *jumps])[:, None]
     piece_rows = (g ^ k_order) * shard_pair + (c ^ jnp.arange(2)[None, :]) * shard_rows
     norm_one, query, kv, qkv_w, gain_rows = project_qkv(
@@ -1022,7 +1026,7 @@
         sin_table,
     )
     first_piece = lax.dynamic_slice_in_dim(kv, (2 * c + zl) * rows, rows, 0)
-    norm_one, query, kv, qkv_w, gain_rows, kv_chunks, first_piece, out_cotangent, g_beside, up_other, down_pair, first_other = sync(
+    norm_one, query, kv, qkv_w, gain_rows, kv_chunks, first_piece, out_cotangent, up_other, down_pair, first_other = sync(
         norm_one,
         query,
         kv,
@@ -1031,7 +1035,6 @@
         [kv[n * CHUNK : (n + 1) * CHUNK] for n in range(2)],
         first_piece,
         out_cotangent,
-        g_beside,
         up_other,
         down_pair,
         first_other,
@@ -1068,14 +1071,14 @@
 
     other = [flip(kv_chunks[0], "zh")]
     same = [lax.ppermute(kv, "g", shift_pairs(d)) for d in shifts]
-    g_across = flip(out_cotangent, "c")
+    g_beside, g_across = flip(out_cotangent, "zl"), flip(out_cotangent, "c")
     state = step([kv], own_bases, 0, None)
-    other, same, g_across, state, kv_late = sync(other, same, g_across, state, kv_chunks[1])
+    other, same, g_beside, g_across, state, kv_late = sync(other, same, g_beside, g_across, state, kv_chunks[1])
 
     other.append(flip(kv_late, "zh"))
     far_blocks = [[lax.ppermute(other[0], "g", shift_pairs(d))] for d in shifts]
+    state = step(same, same_bases, 0, state)
     g_both = flip(g_beside, "c")
-    state = step(same, same_bases, 0, state)
     other, far_blocks, g_both, state, down_pair, first_piece, ffn_own = sync(
         other, far_blocks, g_both, state, down_pair, first_piece, ffn_own
     )
@@ -1150,8 +1153,7 @@
     mid_beside, mid_across, aug, d_query, d_first = sync(mid_beside, mid_across, aug, d_query, d_first)
     mid_both = flip(mid_beside, "c")
     aug = prepare_back([mid_beside, mid_both], 1, out_w, o_tile, kept, query, aug)
-    d_query, d_far = step_back(far_blocks, far_bases, 1, None, kinds, 1, 2, (d_query,))
-    d_far = [(a.astype(F32) + b.astype(F32)).astype(BF) for a, b in zip(d_first, d_far)]
+    d_query, d_far = step_back(far_blocks, far_bases, 1, None, kinds, 1, 2, (d_query,), d_first)
     mid_both, aug, d_query, d_far, early, late = sync(mid_both, aug, d_query, d_far, early, late)
 
     back = [lax.ppermute(d_far[2 * n + m], "g", reverse(shift_pairs(d))) for n, d in enumerate(shifts) for m in range(2)]

time: 573 us -> 569 us (level)
    unnamed x217 -> x205, local copies, waits for them, and re-layouts: 31.4 us -> 33.5 us
  transfers between devices with their start and end apart: 64 -> 64, of which waited for: 36 -> 35; matrix products, arithmetic and copies ran while one was open for 9% -> 8% of each run, Pallas kernels for 30% -> 31%
where the time goes in v5:
time: 569 us; the launch traced here: 558 us
  waiting for transfers between devices  191 us (34%)
  Pallas kernels  190 us (33%)
  starting transfers between devices  70.5 us (12%)
  local copies, waits for them, and re-layouts  60.7 us (11%)
  other arithmetic  30.4 us (5%)
  between operations  15.7 us (3%)
    ppermute x51, waiting for transfers between devices, flip(): return lax.ppermute(value, axis, [(s, s ^ bit) for s in range(count)])  149 us
    ppermute x51, starting transfers between devices, flip(): return lax.ppermute(value, axis, [(s, s ^ bit) for s in range(count)])  49.1 us
    pallas_call x5, Pallas kernels, attend_back(): pl.pallas_call(functools.partial(backward_kernel, swaps, d_query is not N...  42.7 us
    pallas_call x2, Pallas kernels, feed_forward(): pl.pallas_call(functools.partial(ffn_kernel, tiles), grid=(2 * tiles,), i...  35 us
    unnamed x205, local copies, waits for them, and re-layouts  33.5 us
    pallas_call x5, Pallas kernels, attend(): pl.pallas_call(functools.partial(forward_kernel, swaps, state is None, la...  27.2 us
    pallas_call x1, Pallas kernels, weight_grad(): pl.pallas_call(functools.partial(weight_grad_kernel, count), grid=(2, cou...  16.8 us
    ppermute x2, waiting for transfers between devices, body(): lax.ppermute(d_far[2 * n + m], 'g', reverse(shift_pairs(d)))  16.5 us
  transfers between devices with their start and end apart: 64, of which 35 were waited for; matrix products, arithmetic and copies ran while one was open for 8% of the time, Pallas kernels for 31%

profile of v5, /device:TPU:0, one launch (start us, length us, event | category | flops | bytes accessed | tf_op | source)
XLA Modules:
  0.0 558.2 jit_solution(10997072969989918959)
XLA Ops:
  35.4 14.2 %collective-permute-done.2.refs_4_ = bf16[384,512]{1,0:T(8,128)(2,1)} collective-permute-done((bf16[384,512]{1,0:T(8,128)(2,1)}, bf16[384,512]{1,0:T(8,128)(2,1)}, u32[]{:S(2)}, u32[]{:S(2)}) %collective-permute-start.2) | collective-permute-done | bytes 393248 | tf_op jit(solution)/shard_map/ppermute | solution.py:61
  60.4 12.6 %collective-permute-done.7.refs_5_ = bf16[384,512]{1,0:T(8,128)(2,1)S(1)} collective-permute-done((bf16[384,512]{1,0:T(8,128)(2,1)}, bf16[384,512]{1,0:T(8,128)(2,1)S(1)}, u32[]{:S(2)}, u32[]{:S(2)}) %collective-permute-start.7) | collective-permute-done | bytes 393248 | tf_op jit(solution)/shard_map/ppermute | solution.py:61
  77.9 12.0 %collective-permute-done.9.refs_7_ = bf16[384,512]{1,0:T(8,128)(2,1)S(1)} collective-permute-done((bf16[384,512]{1,0:T(8,128)(2,1)}, bf16[384,512]{1,0:T(8,128)(2,1)S(1)}, u32[]{:S(2)}, u32[]{:S(2)}) %collective-permute-start.9) | collective-permute-done | bytes 393248 | tf_op jit(solution)/shard_map/ppermute | solution.py:61
  92.0 12.7 %project_qkv.1 = (bf16[4,256,1536]{2,1,0:T(8,128)(2,1)}, bf16[2,4,512,128]{3,2,1,0:T(8,128)(2,1)}, bf16[1024,384]{1,0:T(8,128)(2,1)}, bf16[2,1536,512]{2,1,0:T(8,128)(2,1)}, f32[8,1536]{1,0:T(8,128)}) custom-call(s32[8]{0:T(128)} %add.254.where_ref, bf16[384,512]{1,0:T(8,128)(2,1)} %pad_maximum_fusion.4.refs_0_, ...), custom_call_target="tpu_custom_call" | custom-call | flops 92000000 | bytes 288000 | tf_op jit(solution)/shard_map/project_qkv/pallas_call | solution.py:181
  118.0 7.8 %attend.5.refs_4_ = f32[2,4,512,128]{3,2,1,0:T(8,128)S(1)} custom-call(s32[4,4]{1,0:T(4,128)S(1)} %pad_add_fusion.info_ref, s32[2]{0:T(128)S(1)} %pad_add_fusion.2.base_ref, s32[1]{0:T(128)} %bitcast.19.zl_ref, bf16[2,4,512,128]{3,2,1,0:T(8,128)(2,1)S(1)} %copy-done, s32[4,256,128]{2,1,0:T(8,128)S(1)} %broadcast_in_dim.114.refs_1_, ...), custom_call_target="tpu_custom_call" | custom-call | flops 117760000 | bytes 368640 | tf_op jit(solution)/shard_map/attend/pallas_call | solution.py:404
  127.2 12.1 %collective-permute-done.13.refs_3_.refs_4_ = bf16[512,384]{1,0:T(8,128)(2,1)S(1)} collective-permute-done((bf16[512,384]{1,0:T(8,128)(2,1)}, bf16[512,384]{1,0:T(8,128)(2,1)S(1)}, u32[]{:S(2)}, u32[]{:S(2)}) %collective-permute-start.13) | collective-permute-done | bytes 393248 | tf_op jit(solution)/shard_map/ppermute | solution.py:61
  157.5 7.4 %collective-permute-done.17.refs_4_.refs_5_ = bf16[512,384]{1,0:T(8,128)(2,1)} collective-permute-done((bf16[512,384]{1,0:T(8,128)(2,1)}, bf16[512,384]{1,0:T(8,128)(2,1)}, u32[]{:S(2)}, u32[]{:S(2)}) %collective-permute-start.17) | collective-permute-done | bytes 393248 | tf_op jit(solution)/shard_map/ppermute | solution.py:61
  217.2 8.3 %collective-permute-done.24.beside_ref = bf16[256,1536]{1,0:T(8,128)(2,1)S(1)} collective-permute-done((bf16[256,1536]{1,0:T(8,128)(2,1)S(1)}, bf16[256,1536]{1,0:T(8,128)(2,1)S(1)}, u32[]{:S(2)}, u32[]{:S(2)}) %collective-permute-start.24) | collective-permute-done | bytes 786464 | tf_op jit(solution)/shard_map/ppermute | solution.py:61
  232.1 9.6 %all-gather.8.cloned.1.call-done.refs_4_.refs_5_ = bf16[1536,1024]{1,0:T(8,128)(2,1)} async-done(((bf16[384,1024]{1,0:T(8,128)(2,1)}), bf16[1536,1024]{1,0:T(8,128)(2,1)}) %all-gather.8.cloned.1.call-update) | async-done | bytes 3145744 | tf_op jit(solution)/shard_map/all_gather | solution.py:56
  241.6 17.5 %feed_forward.2 = (bf16[256,1536]{1,0:T(8,128)(2,1)}, bf16[256,1536]{1,0:T(8,128)(2,1)}, bf16[256,1536]{1,0:T(8,128)(2,1)}, bf16[256,1536]{1,0:T(8,128)(2,1)}, b...) custom-call(bf16[256,1536]{1,0:T(8,128)(2,1)} %copy-done.28, ...), custom_call_target="tpu_custom_call" | custom-call | flops 207000000 | bytes 648000 | tf_op jit(solution)/shard_map/feed_forward/pallas_call | solution.py:666
  262.6 17.6 %feed_forward.3 = (bf16[256,1536]{1,0:T(8,128)(2,1)}, bf16[256,1536]{1,0:T(8,128)(2,1)}, bf16[256,1536]{1,0:T(8,128)(2,1)}, bf16[256,1536]{1,0:T(8,128)(2,1)}, b...) custom-call(bf16[256,1536]{1,0:T(8,128)(2,1)} %collective-permute-do, ...), custom_call_target="tpu_custom_call" | custom-call | flops 207000000 | bytes 648000 | tf_op jit(solution)/shard_map/feed_forward/pallas_call | solution.py:666
  287.0 16.8 %weight_grad.1 = bf16[1536,3072]{1,0:T(8,128)(2,1)} custom-call(bf16[1536,512]{1,0:T(8,128)(2,1)} %get-tuple-element.416.refs_0_.refs_4_, bf16[1536,512]{1,0:T(8,128)(2,1)} %get-tuple-element.417.refs_1_.refs_5_, bf16[512,1024]{1,0:T(8,128)(2,1)S(1)} %copy-done.56, bf16[512,1024]{1,0:T(8,128)(2,1)S(1)} %copy-done.58, ...), custom_call_target="tpu_custom_call" | custom-call | flops 138000000 | bytes 432000 | tf_op jit(solution)/shard_map/weight_grad/pallas_call | solution.py:698
  348.5 9.4 %attend_back.7 = (f32[2,4,512,128]{3,2,1,0:T(8,128)}, bf16[512,384]{1,0:T(8,128)(2,1)}, bf16[512,384]{1,0:T(8,128)(2,1)}) custom-call(s32[4,4]{1,0:T(4,128)} %copy-done.66, s32[2]{0:T(128)} %copy-done.70, s32[1]{0:T(128)} %bitcast.19.zl_ref, bf16[2,4,512,128]{3,2,1,0:T(8,128)(2,1)} %get-tuple-element.471.refs_0_, ...), custom_call_target="tpu_custom_call" | custom-call | flops 184000000 | bytes 576000 | tf_op jit(solution)/shard_map/attend_back/pallas_call | solution.py:572
  358.0 6.5 %attend_back.8 = (f32[2,4,512,128]{3,2,1,0:T(8,128)}, bf16[1024,384]{1,0:T(8,128)(2,1)}) custom-call(s32[4,4]{1,0:T(4,128)} %copy-done.66, s32[2]{0:T(128)} %copy-done.68, s32[1]{0:T(128)} %bitcast.19.zl_ref, bf16[2,4,512,128]{3,2,1,0:T(8,128)(2,1)} %get-tuple-element.471.refs_0_, bf16[2,4,512,128]{3,2,1,0:T(8,128)(2,1)} %get-tuple-element.472.refs_1_, ...), custom_call_target="tpu_custom_call" | custom-call | flops 184000000 | bytes 576000 | tf_op jit(solution)/shard_map/attend_back/pallas_call | solution.py:572
  364.5 8.0 %collective-permute-done.37 = bf16[512,384]{1,0:T(8,128)(2,1)S(1)} collective-permute-done((bf16[512,384]{1,0:T(8,128)(2,1)}, bf16[512,384]{1,0:T(8,128)(2,1)S(1)}, u32[]{:S(2)}, u32[]{:S(2)}) %collective-permute-start.37) | collective-permute-done | bytes 393248 | tf_op jit(solution)/shard_map/ppermute | solution.py:1159
  372.5 8.5 %collective-permute-done.38 = bf16[512,384]{1,0:T(8,128)(2,1)S(1)} collective-permute-done((bf16[512,384]{1,0:T(8,128)(2,1)}, bf16[512,384]{1,0:T(8,128)(2,1)S(1)}, u32[]{:S(2)}, u32[]{:S(2)}) %collective-permute-start.38) | collective-permute-done | bytes 393248 | tf_op jit(solution)/shard_map/ppermute | solution.py:1159
  389.9 16.2 %attend_back.9 = (f32[2,4,512,128]{3,2,1,0:T(8,128)}, f32[1024,384]{1,0:T(8,128)}) custom-call(s32[4,4]{1,0:T(4,128)} %copy-done.66, s32[2]{0:T(128)} %copy-done.69, s32[1]{0:T(128)} %bitcast.19.zl_ref, bf16[2,4,512,128]{3,2,1,0:T(8,128)(2,1)} %get-tuple-element.471.refs_0_, bf16[2,4,512,128]{3,2,1,0:T(8,128)(2,1)} %get-tuple-element.472.refs_1_, ...), custom_call_target="tpu_custom_call" | custom-call | flops 184000000 | bytes 576000 | tf_op jit(solution)/shard_map/attend_back/pallas_call | solution.py:572
  420.1 7.3 %collective-permute-start.43 = (bf16[512,384]{1,0:T(8,128)(2,1)}, bf16[512,384]{1,0:T(8,128)(2,1)}, u32[]{:S(2)}, u32[]{:S(2)}) collective-permute-start(bf16[512,384]{1,0:T(8,128)(2,1)} %add_convert_fusion.1), channel_id=1, source_target_pairs={{0,2},{2,0},{1,3},{3,1},{4,6},{6,4},{5,7},{7,5},{8,10},{10,8},{9,1... | collective-permute-start | bytes 1179656 | tf_op jit(solution)/shard_map/ppermute | solution.py:61
  446.9 8.8 %kv_back.1 = (bf16[2,4,256,192]{3,2,1,0:T(8,128)(2,1)}, bf16[4,256,1536]{2,1,0:T(8,128)(2,1)}) custom-call(s32[1]{0:T(128)} %bitcast.27.core_ref, f32[1024,384]{1,0:T(8,128)} %get-tuple-element.526.refs_0_, bf16[512,384]{1,0:T(8,128)(2,1)} %collective-permute-done.39.refs_1_, bf16[512,384]{1,0:T(8,128)(2,1)} %collective-permute-done.43.refs_2_, ...), custom_call_target="tpu_custom_call" | custom-call | flops 46000000 | bytes 144000 | tf_op jit(solution)/shard_map/kv_back/pallas_call | solution.py:251
  457.4 8.4 %collective-permute-done.47 = bf16[384,512]{1,0:T(8,128)(2,1)S(1)} collective-permute-done((bf16[384,512]{1,0:T(8,128)(2,1)}, bf16[384,512]{1,0:T(8,128)(2,1)S(1)}, u32[]{:S(2)}, u32[]{:S(2)}) %collective-permute-start.47) | collective-permute-done | bytes 393248 | tf_op jit(solution)/shard_map/ppermute | solution.py:61
  493.8 7.3 %collective-permute-done.51 = bf16[384,512]{1,0:T(8,128)(2,1)} collective-permute-done((bf16[384,512]{1,0:T(8,128)(2,1)}, bf16[384,512]{1,0:T(8,128)(2,1)}, u32[]{:S(2)}, u32[]{:S(2)}) %collective-permute-start.51) | collective-permute-done | bytes 393248 | tf_op jit(solution)/shard_map/ppermute | solution.py:61
  501.1 7.7 %collective-permute-done.52 = bf16[384,512]{1,0:T(8,128)(2,1)} collective-permute-done((bf16[384,512]{1,0:T(8,128)(2,1)}, bf16[384,512]{1,0:T(8,128)(2,1)}, u32[]{:S(2)}, u32[]{:S(2)}) %collective-permute-start.52) | collective-permute-done | bytes 393248 | tf_op jit(solution)/shard_map/ppermute | solution.py:61
  508.7 7.5 %collective-permute-done.50 = bf16[384,768]{1,0:T(8,128)(2,1)} collective-permute-done((bf16[384,768]{1,0:T(8,128)(2,1)}, bf16[384,768]{1,0:T(8,128)(2,1)}, u32[]{:S(2)}, u32[]{:S(2)}) %collective-permute-start.50) | collective-permute-done | bytes 589856 | tf_op jit(solution)/shard_map/ppermute | solution.py:61
  530.1 9.6 %collective-permute-done.55 = bf16[384,512]{1,0:T(8,128)(2,1)S(1)} collective-permute-done((bf16[384,512]{1,0:T(8,128)(2,1)S(1)}, bf16[384,512]{1,0:T(8,128)(2,1)S(1)}, u32[]{:S(2)}, u32[]{:S(2)}) %collective-permute-start.55) | collective-permute-done | bytes 393248 | tf_op jit(solution)/shard_map/ppermute | solution.py:61
  (460 shorter events, 289.0 us)
Async XLA Ops:
  7.2 158.8 %all-gather.4.cloned.1.call-start = ((), (), s32[]{:S(2)}) async-start(), calls=%async_computation.2 | async-start | bytes 6881280 | tf_op jit(solution)/shard_map/all_gather | solution.py:56
  21.0 29.2 %collective-permute-start.6 = (bf16[256,1536]{1,0:T(8,128)(2,1)S(1)}, bf16[256,1536]{1,0:T(8,128)(2,1)S(1)}, u32[]{:S(2)}, u32[]{:S(2)}) collective-permute-start(bf16[256,1536]{1,0:T(8,128)(2,1)S(1)} %copy-done.10), channel_id=1, source_target_pairs={{0,1},{1,0},{2,3},{3,2},{4,5},{5,4},{6,7},{7,6},{8,9},{9,8},{10,11... | collective-permute-start | bytes 2359304 | tf_op jit(solution)/shard_map/ppermute | solution.py:61
  25.6 24.0 %collective-permute-start.2 = (bf16[384,512]{1,0:T(8,128)(2,1)}, bf16[384,512]{1,0:T(8,128)(2,1)}, u32[]{:S(2)}, u32[]{:S(2)}) collective-permute-start(bf16[384,512]{1,0:T(8,128)(2,1)} %pad_maximum_fusion.4.refs_0_), channel_id=1, source_target_pairs={{0,2},{2,0},{1,3},{3,1},{4,6},{6,4},{5,7},{7,5},{8,10},{10,8},{9,1... | collective-permute-start | bytes 1179656 | tf_op jit(solution)/shard_map/ppermute | solution.py:61
  52.8 144.5 %all-gather.6.cloned.1.call-start = ((), (), s32[]{:S(2)}) async-start(), calls=%async_computation.3 | async-start | bytes 2949120 | tf_op jit(solution)/shard_map/all_gather | solution.py:56
  54.1 36.5 %collective-permute-start.10 = (bf16[512,1536]{1,0:T(8,128)(2,1)}, bf16[512,1536]{1,0:T(8,128)(2,1)S(1)}, u32[]{:S(2)}, u32[]{:S(2)}) collective-permute-start(bf16[512,1536]{1,0:T(8,128)(2,1)} %pad_maximum_fusion), channel_id=1, source_target_pairs={{0,4},{4,0},{1,5},{5,1},{2,6},{6,2},{3,7},{7,3},{8,12},{12,8},{9,1... | collective-permute-start | bytes 4718600 | tf_op jit(solution)/shard_map/ppermute | solution.py:61
  54.1 36.5 %collective-permute-start.11 = (bf16[384,768]{1,0:T(8,128)(2,1)S(1)}, bf16[384,768]{1,0:T(8,128)(2,1)S(1)}, u32[]{:S(2)}, u32[]{:S(2)}) collective-permute-start(bf16[384,768]{1,0:T(8,128)(2,1)S(1)} %copy-done.83), channel_id=1, source_target_pairs={{0,2},{2,0},{1,3},{3,1},{4,6},{6,4},{5,7},{7,5},{8,10},{10,8},{9,1... | collective-permute-start | bytes 1769480 | tf_op jit(solution)/shard_map/ppermute | solution.py:61
  59.9 30.0 %collective-permute-start.9 = (bf16[384,512]{1,0:T(8,128)(2,1)}, bf16[384,512]{1,0:T(8,128)(2,1)S(1)}, u32[]{:S(2)}, u32[]{:S(2)}) collective-permute-start(bf16[384,512]{1,0:T(8,128)(2,1)} %collective-permute-done.2.refs_4_), channel_id=1, source_target_pairs={{0,24},{8,16},{16,8},{24,0},{1,25},{9,17},{17,9},{25,1},{2,26},{10... | collective-permute-start | bytes 1179656 | tf_op jit(solution)/shard_map/ppermute | solution.py:61
  109.4 132.2 %all-gather.8.cloned.1.call-start = ((), (), s32[]{:S(2)}) async-start(), calls=%async_computation.4 | async-start | bytes 3932160 | tf_op jit(solution)/shard_map/all_gather | solution.py:56
  109.5 34.3 %collective-permute-start.14 = (bf16[1024,384]{1,0:T(8,128)(2,1)S(1)}, bf16[1024,384]{1,0:T(8,128)(2,1)}, u32[]{:S(2)}, u32[]{:S(2)}) collective-permute-start(bf16[1024,384]{1,0:T(8,128)(2,1)S(1)} %copy-done.18), channel_id=1, source_target_pairs={{0,8},{1,9},{2,10},{3,11},{4,12},{5,13},{6,14},{7,15}} | collective-permute-start | bytes 2359304 | tf_op jit(solution)/shard_map/ppermute | solution.py:1073
  114.7 29.1 %collective-permute-start.15 = (bf16[256,1536]{1,0:T(8,128)(2,1)}, bf16[256,1536]{1,0:T(8,128)(2,1)}, u32[]{:S(2)}, u32[]{:S(2)}) collective-permute-start(bf16[256,1536]{1,0:T(8,128)(2,1)} %base_ref), channel_id=1, source_target_pairs={{0,1},{1,0},{2,3},{3,2},{4,5},{5,4},{6,7},{7,6},{8,9},{9,8},{10,11... | collective-permute-start | bytes 2359304 | tf_op jit(solution)/shard_map/ppermute | solution.py:61
  115.5 28.2 %collective-permute-start.16 = (bf16[256,1536]{1,0:T(8,128)(2,1)}, bf16[256,1536]{1,0:T(8,128)(2,1)}, u32[]{:S(2)}, u32[]{:S(2)}) collective-permute-start(bf16[256,1536]{1,0:T(8,128)(2,1)} %base_ref), channel_id=1, source_target_pairs={{0,4},{4,0},{1,5},{5,1},{2,6},{6,2},{3,7},{7,3},{8,12},{12,8},{9,1... | collective-permute-start | bytes 2359304 | tf_op jit(solution)/shard_map/ppermute | solution.py:61
  115.5 23.8 %collective-permute-start.13 = (bf16[512,384]{1,0:T(8,128)(2,1)}, bf16[512,384]{1,0:T(8,128)(2,1)S(1)}, u32[]{:S(2)}, u32[]{:S(2)}) collective-permute-start(bf16[512,384]{1,0:T(8,128)(2,1)} %get-tuple-element.327), channel_id=1, source_target_pairs={{0,2},{2,0},{1,3},{3,1},{4,6},{6,4},{5,7},{7,5},{8,10},{10,8},{9,1... | collective-permute-start | bytes 1179656 | tf_op jit(solution)/shard_map/ppermute | solution.py:61
  191.7 249.0 %reduce-scatter.3.cloned.1.call-start = ((), (), s32[]{:S(2)}) async-start(), calls=%async_computation.5 | async-start | bytes 11796480 | tf_op jit(solution)/shard_map/reduce_scatter | solution.py:97
  229.8 29.3 %collective-permute-start.26 = (bf16[256,1536]{1,0:T(8,128)(2,1)S(1)}, bf16[256,1536]{1,0:T(8,128)(2,1)}, u32[]{:S(2)}, u32[]{:S(2)}) collective-permute-start(bf16[256,1536]{1,0:T(8,128)(2,1)S(1)} %get-tuple-element.370.n0.refs_4_), channel_id=1, source_target_pairs={{0,1},{1,0},{2,3},{3,2},{4,5},{5,4},{6,7},{7,6},{8,9},{9,8},{10,11... | collective-permute-start | bytes 2359304 | tf_op jit(solution)/shard_map/ppermute | solution.py:61
  304.9 172.3 %reduce-scatter.5.cloned.1.call-start = ((), (), s32[]{:S(2)}) async-start(), calls=%async_computation.6 | async-start | bytes 1966080 | tf_op jit(solution)/shard_map/reduce_scatter | solution.py:97
  344.2 28.3 %collective-permute-start.37 = (bf16[512,384]{1,0:T(8,128)(2,1)}, bf16[512,384]{1,0:T(8,128)(2,1)S(1)}, u32[]{:S(2)}, u32[]{:S(2)}) collective-permute-start(bf16[512,384]{1,0:T(8,128)(2,1)} %get-tuple-element.479), channel_id=1, source_target_pairs={{8,0},{9,1},{10,2},{11,3},{12,4},{13,5},{14,6},{15,7}} | collective-permute-start | bytes 1179656 | tf_op jit(solution)/shard_map/ppermute | solution.py:1159
  345.7 35.3 %collective-permute-start.38 = (bf16[512,384]{1,0:T(8,128)(2,1)}, bf16[512,384]{1,0:T(8,128)(2,1)S(1)}, u32[]{:S(2)}, u32[]{:S(2)}) collective-permute-start(bf16[512,384]{1,0:T(8,128)(2,1)} %get-tuple-element.480), channel_id=1, source_target_pairs={{8,0},{9,1},{10,2},{11,3},{12,4},{13,5},{14,6},{15,7}} | collective-permute-start | bytes 1179656 | tf_op jit(solution)/shard_map/ppermute | solution.py:1159
  381.0 39.1 %collective-permute-start.40 = (bf16[1024,384]{1,0:T(8,128)(2,1)}, bf16[1024,384]{1,0:T(8,128)(2,1)}, u32[]{:S(2)}, u32[]{:S(2)}) collective-permute-start(bf16[1024,384]{1,0:T(8,128)(2,1)} %get-tuple-element.486), channel_id=1, source_target_pairs={{8,0},{9,1},{10,2},{11,3},{12,4},{13,5},{14,6},{15,7}} | collective-permute-start | bytes 2359304 | tf_op jit(solution)/shard_map/ppermute | solution.py:1171
  382.3 37.9 %collective-permute-start.42 = (bf16[256,1536]{1,0:T(8,128)(2,1)S(1)}, bf16[256,1536]{1,0:T(8,128)(2,1)}, u32[]{:S(2)}, u32[]{:S(2)}) collective-permute-start(bf16[256,1536]{1,0:T(8,128)(2,1)S(1)} %add_rows.6), channel_id=1, source_target_pairs={{0,1},{1,0},{2,3},{3,2},{4,5},{5,4},{6,7},{7,6},{8,9},{9,8},{10,11... | collective-permute-start | bytes 2359304 | tf_op jit(solution)/shard_map/ppermute | solution.py:61
  384.6 31.8 %collective-permute-start.39 = (bf16[512,384]{1,0:T(8,128)(2,1)}, bf16[512,384]{1,0:T(8,128)(2,1)}, u32[]{:S(2)}, u32[]{:S(2)}) collective-permute-start(bf16[512,384]{1,0:T(8,128)(2,1)} %add_convert_fusion.2), channel_id=1, source_target_pairs={{0,2},{2,0},{1,3},{3,1},{4,6},{6,4},{5,7},{7,5},{8,10},{10,8},{9,1... | collective-permute-start | bytes 1179656 | tf_op jit(solution)/shard_map/ppermute | solution.py:61
  387.8 28.7 %collective-permute-start.41 = (bf16[256,384]{1,0:T(8,128)(2,1)}, bf16[256,384]{1,0:T(8,128)(2,1)}, u32[]{:S(2)}, u32[]{:S(2)}) collective-permute-start(bf16[256,384]{1,0:T(8,128)(2,1)} %constant_dynamic-slice_fusion.9), channel_id=1, source_target_pairs={{2,8},{3,9},{6,12},{7,13}} | collective-permute-start | bytes 589832 | tf_op jit(solution)/shard_map/ppermute | solution.py:1175
  420.1 24.8 %collective-permute-start.43 = (bf16[512,384]{1,0:T(8,128)(2,1)}, bf16[512,384]{1,0:T(8,128)(2,1)}, u32[]{:S(2)}, u32[]{:S(2)}) collective-permute-start(bf16[512,384]{1,0:T(8,128)(2,1)} %add_convert_fusion.1), channel_id=1, source_target_pairs={{0,2},{2,0},{1,3},{3,1},{4,6},{6,4},{5,7},{7,5},{8,10},{10,8},{9,1... | collective-permute-start | bytes 1179656 | tf_op jit(solution)/shard_map/ppermute | solution.py:61
  486.0 32.4 %collective-permute-start.54 = (bf16[256,1536]{1,0:T(8,128)(2,1)}, bf16[256,1536]{1,0:T(8,128)(2,1)}, u32[]{:S(2)}, u32[]{:S(2)}) collective-permute-start(bf16[256,1536]{1,0:T(8,128)(2,1)} %add_rows.7), channel_id=1, source_target_pairs={{0,1},{1,0},{2,3},{3,2},{4,5},{5,4},{6,7},{7,6},{8,9},{9,8},{10,11... | collective-permute-start | bytes 2359304 | tf_op jit(solution)/shard_map/ppermute | solution.py:61
  486.0 30.2 %collective-permute-start.50 = (bf16[384,768]{1,0:T(8,128)(2,1)}, bf16[384,768]{1,0:T(8,128)(2,1)}, u32[]{:S(2)}, u32[]{:S(2)}) collective-permute-start(bf16[384,768]{1,0:T(8,128)(2,1)} %pad_maximum_fusion.3), channel_id=1, source_target_pairs={{0,2},{2,0},{1,3},{3,1},{4,6},{6,4},{5,7},{7,5},{8,10},{10,8},{9,1... | collective-permute-start | bytes 1769480 | tf_op jit(solution)/shard_map/ppermute | solution.py:61
  (144 other events, 1590.8 us)
Sparse Core Ops, SparseCore 0:
  52.9 87.6 all-gather.3
  143.0 47.5 all-gather.5
  193.1 48.5 all-gather.7
  305.0 120.0 reduce-scatter.2
  446.5 28.7 reduce-scatter.4

commit v6 on v5

--- a/solution.py
+++ b/solution.py
@@ -417,7 +417,7 @@
         ),
         out_shape=out_shape,
         input_output_aliases=aliases,
-        compiler_params=params(48),
+        compiler_params=params(58),
         cost_estimate=cost(n_keys / 100),
         name="attend",
     )(info, bases, zl, *args)

time: 569 us -> 566 us (level)
  local copies, waits for them, and re-layouts: 60.7 us -> 48.7 us
  Pallas kernels: 190 us -> 199 us
    unnamed x205 -> x187, local copies, waits for them, and re-layouts: 33.5 us -> 20.9 us
    pallas_call x5, Pallas kernels: 27.2 us -> 34.6 us  [attend(): pl.pallas_call(functools.partial(forward_kernel, swaps, state is None, la...]
  transfers between devices with their start and end apart: 64 -> 64, of which waited for: 35 -> 36; matrix products, arithmetic and copies ran while one was open for 8% -> 8% of each run, Pallas kernels for 31% -> 32%
where the time goes in v6:
time: 566 us; the launch traced here: 556 us
  Pallas kernels  199 us (35%)
  waiting for transfers between devices  195 us (34%)
  starting transfers between devices  66.5 us (12%)
  local copies, waits for them, and re-layouts  48.7 us (9%)
  other arithmetic  31.4 us (6%)
  between operations  15.6 us (3%)
    ppermute x51, waiting for transfers between devices, flip(): return lax.ppermute(value, axis, [(s, s ^ bit) for s in range(count)])  149 us
    ppermute x51, starting transfers between devices, flip(): return lax.ppermute(value, axis, [(s, s ^ bit) for s in range(count)])  46.7 us
    pallas_call x5, Pallas kernels, attend_back(): pl.pallas_call(functools.partial(backward_kernel, swaps, d_query is not N...  42.6 us
    pallas_call x2, Pallas kernels, feed_forward(): pl.pallas_call(functools.partial(ffn_kernel, tiles), grid=(2 * tiles,), i...  35 us
    pallas_call x5, Pallas kernels, attend(): pl.pallas_call(functools.partial(forward_kernel, swaps, state is None, la...  34.6 us
    unnamed x187, local copies, waits for them, and re-layouts  20.9 us
    pallas_call x1, Pallas kernels, weight_grad(): pl.pallas_call(functools.partial(weight_grad_kernel, count), grid=(2, cou...  16.9 us
    ppermute x2, waiting for transfers between devices, body(): lax.ppermute(d_far[2 * n + m], 'g', reverse(shift_pairs(d)))  14.2 us
  transfers between devices with their start and end apart: 64, of which 36 were waited for; matrix products, arithmetic and copies ran while one was open for 8% of the time, Pallas kernels for 32%

profile of v6, /device:TPU:0, one launch (start us, length us, event | category | flops | bytes accessed | tf_op | source)
XLA Modules:
  0.0 555.5 jit_solution(12196253389868341592)
XLA Ops:
  35.7 13.8 %collective-permute-done.2.refs_4_ = bf16[384,512]{1,0:T(8,128)(2,1)} collective-permute-done((bf16[384,512]{1,0:T(8,128)(2,1)}, bf16[384,512]{1,0:T(8,128)(2,1)}, u32[]{:S(2)}, u32[]{:S(2)}) %collective-permute-start.2) | collective-permute-done | bytes 393248 | tf_op jit(solution)/shard_map/ppermute | solution.py:61
  61.1 12.6 %collective-permute-done.7.refs_5_ = bf16[384,512]{1,0:T(8,128)(2,1)S(1)} collective-permute-done((bf16[384,512]{1,0:T(8,128)(2,1)}, bf16[384,512]{1,0:T(8,128)(2,1)S(1)}, u32[]{:S(2)}, u32[]{:S(2)}) %collective-permute-start.7) | collective-permute-done | bytes 393248 | tf_op jit(solution)/shard_map/ppermute | solution.py:61
  78.6 12.1 %collective-permute-done.9.refs_7_ = bf16[384,512]{1,0:T(8,128)(2,1)} collective-permute-done((bf16[384,512]{1,0:T(8,128)(2,1)}, bf16[384,512]{1,0:T(8,128)(2,1)}, u32[]{:S(2)}, u32[]{:S(2)}) %collective-permute-start.9) | collective-permute-done | bytes 393248 | tf_op jit(solution)/shard_map/ppermute | solution.py:61
  91.9 12.8 %project_qkv.1 = (bf16[4,256,1536]{2,1,0:T(8,128)(2,1)}, bf16[2,4,512,128]{3,2,1,0:T(8,128)(2,1)}, bf16[1024,384]{1,0:T(8,128)(2,1)}, bf16[2,1536,512]{2,1,0:T(8,128)(2,1)}, f32[8,1536]{1,0:T(8,128)}) custom-call(s32[8]{0:T(128)} %add.254.where_ref, bf16[384,512]{1,0:T(8,128)(2,1)} %pad_maximum_fusion.4.refs_0_, ...), custom_call_target="tpu_custom_call" | custom-call | flops 92000000 | bytes 288000 | tf_op jit(solution)/shard_map/project_qkv/pallas_call | solution.py:181
  118.4 10.0 %attend.5.refs_4_ = f32[2,4,512,128]{3,2,1,0:T(8,128)} custom-call(s32[4,4]{1,0:T(4,128)} %pad_add_fusion.info_ref, s32[2]{0:T(128)} %pad_add_fusion.2.base_ref, s32[1]{0:T(128)} %bitcast.19.zl_ref, bf16[2,4,512,128]{3,2,1,0:T(8,128)(2,1)} %get-tuple-element.324.refs_0_.query_ref, s32[4,256,128]{2,1,0:T(8,128)} %broadcast_in_dim.114.refs_1_, ...), custom_call_target="tpu_custom_call" | custom-call | flops 117760000 | bytes 368640 | tf_op jit(solution)/shard_map/attend/pallas_call | solution.py:404
  128.4 10.5 %collective-permute-done.13.refs_3_.refs_4_ = bf16[512,384]{1,0:T(8,128)(2,1)S(1)} collective-permute-done((bf16[512,384]{1,0:T(8,128)(2,1)}, bf16[512,384]{1,0:T(8,128)(2,1)S(1)}, u32[]{:S(2)}, u32[]{:S(2)}) %collective-permute-start.13) | collective-permute-done | bytes 393248 | tf_op jit(solution)/shard_map/ppermute | solution.py:61
  159.1 6.5 %collective-permute-done.17.refs_4_.refs_5_ = bf16[512,384]{1,0:T(8,128)(2,1)S(1)} collective-permute-done((bf16[512,384]{1,0:T(8,128)(2,1)}, bf16[512,384]{1,0:T(8,128)(2,1)S(1)}, u32[]{:S(2)}, u32[]{:S(2)}) %collective-permute-start.17) | collective-permute-done | bytes 393248 | tf_op jit(solution)/shard_map/ppermute | solution.py:61
  172.4 8.1 %attend.7.refs_6_ = f32[2,4,512,128]{3,2,1,0:T(8,128)} custom-call(s32[4,4]{1,0:T(4,128)} %pad_add_fusion.info_ref, s32[2]{0:T(128)} %pad_add_fusion.3.base_ref, s32[1]{0:T(128)} %bitcast.19.zl_ref, bf16[2,4,512,128]{3,2,1,0:T(8,128)(2,1)} %get-tuple-element.324.refs_0_.query_ref, s32[4,256,128]{2,1,0:T(8,128)} %broadcast_in_dim.114.refs_1_, ...), custom_call_target="tpu_custom_call" | custom-call | flops 117760000 | bytes 368640 | tf_op jit(solution)/shard_map/attend/pallas_call | solution.py:404
  215.0 9.8 %collective-permute-done.24.beside_ref = bf16[256,1536]{1,0:T(8,128)(2,1)S(1)} collective-permute-done((bf16[256,1536]{1,0:T(8,128)(2,1)S(1)}, bf16[256,1536]{1,0:T(8,128)(2,1)S(1)}, u32[]{:S(2)}, u32[]{:S(2)}) %collective-permute-start.24) | collective-permute-done | bytes 786464 | tf_op jit(solution)/shard_map/ppermute | solution.py:61
  229.4 10.3 %all-gather.8.cloned.1.call-done.refs_4_.refs_5_ = bf16[1536,1024]{1,0:T(8,128)(2,1)} async-done(((bf16[384,1024]{1,0:T(8,128)(2,1)}), bf16[1536,1024]{1,0:T(8,128)(2,1)}) %all-gather.8.cloned.1.call-update) | async-done | bytes 3145744 | tf_op jit(solution)/shard_map/all_gather | solution.py:56
  239.7 17.4 %feed_forward.2 = (bf16[256,1536]{1,0:T(8,128)(2,1)}, bf16[256,1536]{1,0:T(8,128)(2,1)}, bf16[256,1536]{1,0:T(8,128)(2,1)}, bf16[256,1536]{1,0:T(8,128)(2,1)}, b...) custom-call(bf16[256,1536]{1,0:T(8,128)(2,1)} %copy-done.16, ...), custom_call_target="tpu_custom_call" | custom-call | flops 207000000 | bytes 648000 | tf_op jit(solution)/shard_map/feed_forward/pallas_call | solution.py:666
  260.6 17.6 %feed_forward.3 = (bf16[256,1536]{1,0:T(8,128)(2,1)}, bf16[256,1536]{1,0:T(8,128)(2,1)}, bf16[256,1536]{1,0:T(8,128)(2,1)}, bf16[256,1536]{1,0:T(8,128)(2,1)}, b...) custom-call(bf16[256,1536]{1,0:T(8,128)(2,1)} %collective-permute-do, ...), custom_call_target="tpu_custom_call" | custom-call | flops 207000000 | bytes 648000 | tf_op jit(solution)/shard_map/feed_forward/pallas_call | solution.py:666
  285.0 16.9 %weight_grad.1 = bf16[1536,3072]{1,0:T(8,128)(2,1)} custom-call(bf16[1536,512]{1,0:T(8,128)(2,1)} %get-tuple-element.416.refs_0_.refs_4_, bf16[1536,512]{1,0:T(8,128)(2,1)} %get-tuple-element.417.refs_1_.refs_5_, bf16[512,1024]{1,0:T(8,128)(2,1)S(1)} %copy-done.47, bf16[512,1024]{1,0:T(8,128)(2,1)S(1)} %copy-done.49, ...), custom_call_target="tpu_custom_call" | custom-call | flops 138000000 | bytes 432000 | tf_op jit(solution)/shard_map/weight_grad/pallas_call | solution.py:698
  348.9 9.2 %attend_back.7 = (f32[2,4,512,128]{3,2,1,0:T(8,128)}, bf16[512,384]{1,0:T(8,128)(2,1)}, bf16[512,384]{1,0:T(8,128)(2,1)}) custom-call(s32[4,4]{1,0:T(4,128)} %pad_add_fusion.info_ref, s32[2]{0:T(128)} %pad_add_fusion.3.base_ref, s32[1]{0:T(128)} %bitcast.19.zl_ref, bf16[2,4,512,128]{3,2,1,0:T(8,128)(2,1)} %get-tuple-element.471.refs_0_, ...), custom_call_target="tpu_custom_call" | custom-call | flops 184000000 | bytes 576000 | tf_op jit(solution)/shard_map/attend_back/pallas_call | solution.py:572
  358.1 6.6 %attend_back.8 = (f32[2,4,512,128]{3,2,1,0:T(8,128)}, bf16[1024,384]{1,0:T(8,128)(2,1)}) custom-call(s32[4,4]{1,0:T(4,128)} %pad_add_fusion.info_ref, s32[2]{0:T(128)} %broadcast_select_fusion.1.base_ref, s32[1]{0:T(128)} %bitcast.19.zl_ref, bf16[2,4,512,128]{3,2,1,0:T(8,128)(2,1)} %get-tuple-element.471.refs_0_, ...), custom_call_target="tpu_custom_call" | custom-call | flops 184000000 | bytes 576000 | tf_op jit(solution)/shard_map/attend_back/pallas_call | solution.py:572
  370.5 8.4 %collective-permute-done.38 = bf16[512,384]{1,0:T(8,128)(2,1)S(1)} collective-permute-done((bf16[512,384]{1,0:T(8,128)(2,1)}, bf16[512,384]{1,0:T(8,128)(2,1)S(1)}, u32[]{:S(2)}, u32[]{:S(2)}) %collective-permute-start.38) | collective-permute-done | bytes 393248 | tf_op jit(solution)/shard_map/ppermute | solution.py:1159
  386.6 16.2 %attend_back.9 = (f32[2,4,512,128]{3,2,1,0:T(8,128)}, f32[1024,384]{1,0:T(8,128)}) custom-call(s32[4,4]{1,0:T(4,128)} %pad_add_fusion.info_ref, s32[2]{0:T(128)} %pad_add_fusion.2.base_ref, s32[1]{0:T(128)} %bitcast.19.zl_ref, bf16[2,4,512,128]{3,2,1,0:T(8,128)(2,1)} %get-tuple-element.471.refs_0_, bf16[2,4,512,128]{3,2,1,0:T(8,128)(2,1)} %get-tuple-element.472.refs_1_, ...), custom_call_target="tpu_custom_call" | custom-call | flops 184000000 | bytes 576000 | tf_op jit(solution)/shard_map/attend_back/pallas_call | solution.py:572
  411.6 8.6 %collective-permute-done.40.refs_3_ = bf16[1024,384]{1,0:T(8,128)(2,1)} collective-permute-done((bf16[1024,384]{1,0:T(8,128)(2,1)}, bf16[1024,384]{1,0:T(8,128)(2,1)}, u32[]{:S(2)}, u32[]{:S(2)}) %collective-permute-start.40) | collective-permute-done | bytes 786464 | tf_op jit(solution)/shard_map/ppermute | solution.py:1171
  444.3 8.9 %kv_back.1 = (bf16[2,4,256,192]{3,2,1,0:T(8,128)(2,1)}, bf16[4,256,1536]{2,1,0:T(8,128)(2,1)}) custom-call(s32[1]{0:T(128)} %bitcast.27.core_ref, f32[1024,384]{1,0:T(8,128)} %get-tuple-element.526.refs_0_, bf16[512,384]{1,0:T(8,128)(2,1)} %collective-permute-done.39.refs_1_, bf16[512,384]{1,0:T(8,128)(2,1)} %collective-permute-done.43.refs_2_, ...), custom_call_target="tpu_custom_call" | custom-call | flops 46000000 | bytes 144000 | tf_op jit(solution)/shard_map/kv_back/pallas_call | solution.py:251
  454.8 8.4 %collective-permute-done.47 = bf16[384,512]{1,0:T(8,128)(2,1)} collective-permute-done((bf16[384,512]{1,0:T(8,128)(2,1)}, bf16[384,512]{1,0:T(8,128)(2,1)}, u32[]{:S(2)}, u32[]{:S(2)}) %collective-permute-start.47) | collective-permute-done | bytes 393248 | tf_op jit(solution)/shard_map/ppermute | solution.py:61
  476.5 6.7 %collective-permute-done.49 = bf16[384,512]{1,0:T(8,128)(2,1)} collective-permute-done((bf16[384,512]{1,0:T(8,128)(2,1)}, bf16[384,512]{1,0:T(8,128)(2,1)}, u32[]{:S(2)}, u32[]{:S(2)}) %collective-permute-start.49) | collective-permute-done | bytes 393248 | tf_op jit(solution)/shard_map/ppermute | solution.py:61
  491.3 7.3 %collective-permute-done.51 = bf16[384,512]{1,0:T(8,128)(2,1)} collective-permute-done((bf16[384,512]{1,0:T(8,128)(2,1)}, bf16[384,512]{1,0:T(8,128)(2,1)}, u32[]{:S(2)}, u32[]{:S(2)}) %collective-permute-start.51) | collective-permute-done | bytes 393248 | tf_op jit(solution)/shard_map/ppermute | solution.py:61
  498.5 8.5 %collective-permute-done.52 = bf16[384,512]{1,0:T(8,128)(2,1)} collective-permute-done((bf16[384,512]{1,0:T(8,128)(2,1)}, bf16[384,512]{1,0:T(8,128)(2,1)}, u32[]{:S(2)}, u32[]{:S(2)}) %collective-permute-start.52) | collective-permute-done | bytes 393248 | tf_op jit(solution)/shard_map/ppermute | solution.py:61
  527.4 9.6 %collective-permute-done.55 = bf16[384,512]{1,0:T(8,128)(2,1)S(1)} collective-permute-done((bf16[384,512]{1,0:T(8,128)(2,1)S(1)}, bf16[384,512]{1,0:T(8,128)(2,1)S(1)}, u32[]{:S(2)}, u32[]{:S(2)}) %collective-permute-start.55) | collective-permute-done | bytes 393248 | tf_op jit(solution)/shard_map/ppermute | solution.py:61
  (442 shorter events, 283.3 us)
Async XLA Ops:
  7.2 159.5 %all-gather.4.cloned.1.call-start = ((), (), s32[]{:S(2)}) async-start(), calls=%async_computation.2 | async-start | bytes 6881280 | tf_op jit(solution)/shard_map/all_gather | solution.py:56
  21.0 29.2 %collective-permute-start.6 = (bf16[256,1536]{1,0:T(8,128)(2,1)S(1)}, bf16[256,1536]{1,0:T(8,128)(2,1)S(1)}, u32[]{:S(2)}, u32[]{:S(2)}) collective-permute-start(bf16[256,1536]{1,0:T(8,128)(2,1)S(1)} %copy-done.5), channel_id=1, source_target_pairs={{0,1},{1,0},{2,3},{3,2},{4,5},{5,4},{6,7},{7,6},{8,9},{9,8},{10,11... | collective-permute-start | bytes 2359304 | tf_op jit(solution)/shard_map/ppermute | solution.py:61
  26.6 22.8 %collective-permute-start.2 = (bf16[384,512]{1,0:T(8,128)(2,1)}, bf16[384,512]{1,0:T(8,128)(2,1)}, u32[]{:S(2)}, u32[]{:S(2)}) collective-permute-start(bf16[384,512]{1,0:T(8,128)(2,1)} %pad_maximum_fusion.4.refs_0_), channel_id=1, source_target_pairs={{0,2},{2,0},{1,3},{3,1},{4,6},{6,4},{5,7},{7,5},{8,10},{10,8},{9,1... | collective-permute-start | bytes 1179656 | tf_op jit(solution)/shard_map/ppermute | solution.py:61
  53.5 143.3 %all-gather.6.cloned.1.call-start = ((), (), s32[]{:S(2)}) async-start(), calls=%async_computation.3 | async-start | bytes 2949120 | tf_op jit(solution)/shard_map/all_gather | solution.py:56
  54.8 35.9 %collective-permute-start.10 = (bf16[512,1536]{1,0:T(8,128)(2,1)}, bf16[512,1536]{1,0:T(8,128)(2,1)S(1)}, u32[]{:S(2)}, u32[]{:S(2)}) collective-permute-start(bf16[512,1536]{1,0:T(8,128)(2,1)} %pad_maximum_fusion), channel_id=1, source_target_pairs={{0,4},{4,0},{1,5},{5,1},{2,6},{6,2},{3,7},{7,3},{8,12},{12,8},{9,1... | collective-permute-start | bytes 4718600 | tf_op jit(solution)/shard_map/ppermute | solution.py:61
  54.8 35.9 %collective-permute-start.11 = (bf16[384,768]{1,0:T(8,128)(2,1)S(1)}, bf16[384,768]{1,0:T(8,128)(2,1)S(1)}, u32[]{:S(2)}, u32[]{:S(2)}) collective-permute-start(bf16[384,768]{1,0:T(8,128)(2,1)S(1)} %slice.154), channel_id=1, source_target_pairs={{0,2},{2,0},{1,3},{3,1},{4,6},{6,4},{5,7},{7,5},{8,10},{10,8},{9,1... | collective-permute-start | bytes 1769480 | tf_op jit(solution)/shard_map/ppermute | solution.py:61
  60.6 30.1 %collective-permute-start.9 = (bf16[384,512]{1,0:T(8,128)(2,1)}, bf16[384,512]{1,0:T(8,128)(2,1)}, u32[]{:S(2)}, u32[]{:S(2)}) collective-permute-start(bf16[384,512]{1,0:T(8,128)(2,1)} %collective-permute-done.2.refs_4_), channel_id=1, source_target_pairs={{0,24},{8,16},{16,8},{24,0},{1,25},{9,17},{17,9},{25,1},{2,26},{10... | collective-permute-start | bytes 1179656 | tf_op jit(solution)/shard_map/ppermute | solution.py:61
  109.3 130.4 %all-gather.8.cloned.1.call-start = ((), (), s32[]{:S(2)}) async-start(), calls=%async_computation.4 | async-start | bytes 3932160 | tf_op jit(solution)/shard_map/all_gather | solution.py:56
  110.0 34.4 %collective-permute-start.14 = (bf16[1024,384]{1,0:T(8,128)(2,1)S(1)}, bf16[1024,384]{1,0:T(8,128)(2,1)S(1)}, u32[]{:S(2)}, u32[]{:S(2)}) collective-permute-start(bf16[1024,384]{1,0:T(8,128)(2,1)S(1)} %copy-done.57), channel_id=1, source_target_pairs={{0,8},{1,9},{2,10},{3,11},{4,12},{5,13},{6,14},{7,15}} | collective-permute-start | bytes 2359304 | tf_op jit(solution)/shard_map/ppermute | solution.py:1073
  114.4 30.0 %collective-permute-start.15 = (bf16[256,1536]{1,0:T(8,128)(2,1)S(1)}, bf16[256,1536]{1,0:T(8,128)(2,1)S(1)}, u32[]{:S(2)}, u32[]{:S(2)}) collective-permute-start(bf16[256,1536]{1,0:T(8,128)(2,1)S(1)} %copy-done.14), channel_id=1, source_target_pairs={{0,1},{1,0},{2,3},{3,2},{4,5},{5,4},{6,7},{7,6},{8,9},{9,8},{10,11... | collective-permute-start | bytes 2359304 | tf_op jit(solution)/shard_map/ppermute | solution.py:61
  115.4 29.0 %collective-permute-start.16 = (bf16[256,1536]{1,0:T(8,128)(2,1)S(1)}, bf16[256,1536]{1,0:T(8,128)(2,1)}, u32[]{:S(2)}, u32[]{:S(2)}) collective-permute-start(bf16[256,1536]{1,0:T(8,128)(2,1)S(1)} %copy-done.14), channel_id=1, source_target_pairs={{0,4},{4,0},{1,5},{5,1},{2,6},{6,2},{3,7},{7,3},{8,12},{12,8},{9,1... | collective-permute-start | bytes 2359304 | tf_op jit(solution)/shard_map/ppermute | solution.py:61
  115.4 23.4 %collective-permute-start.13 = (bf16[512,384]{1,0:T(8,128)(2,1)}, bf16[512,384]{1,0:T(8,128)(2,1)S(1)}, u32[]{:S(2)}, u32[]{:S(2)}) collective-permute-start(bf16[512,384]{1,0:T(8,128)(2,1)} %get-tuple-element.327), channel_id=1, source_target_pairs={{0,2},{2,0},{1,3},{3,1},{4,6},{6,4},{5,7},{7,5},{8,10},{10,8},{9,1... | collective-permute-start | bytes 1179656 | tf_op jit(solution)/shard_map/ppermute | solution.py:61
  144.4 22.2 %collective-permute-start.19 = (bf16[256,1536]{1,0:T(8,128)(2,1)S(1)}, bf16[256,1536]{1,0:T(8,128)(2,1)}, u32[]{:S(2)}, u32[]{:S(2)}) collective-permute-start(bf16[256,1536]{1,0:T(8,128)(2,1)S(1)} %collective-permute-done.15.g0), channel_id=1, source_target_pairs={{0,4},{4,0},{1,5},{5,1},{2,6},{6,2},{3,7},{7,3},{8,12},{12,8},{9,1... | collective-permute-start | bytes 2359304 | tf_op jit(solution)/shard_map/ppermute | solution.py:61
  190.9 247.2 %reduce-scatter.3.cloned.1.call-start = ((), (), s32[]{:S(2)}) async-start(), calls=%async_computation.5 | async-start | bytes 11796480 | tf_op jit(solution)/shard_map/reduce_scatter | solution.py:97
  227.1 30.0 %collective-permute-start.26 = (bf16[256,1536]{1,0:T(8,128)(2,1)S(1)}, bf16[256,1536]{1,0:T(8,128)(2,1)}, u32[]{:S(2)}, u32[]{:S(2)}) collective-permute-start(bf16[256,1536]{1,0:T(8,128)(2,1)S(1)} %get-tuple-element.370.n0.refs_4_), channel_id=1, source_target_pairs={{0,1},{1,0},{2,3},{3,2},{4,5},{5,4},{6,7},{7,6},{8,9},{9,8},{10,11... | collective-permute-start | bytes 2359304 | tf_op jit(solution)/shard_map/ppermute | solution.py:61
  302.8 170.9 %reduce-scatter.5.cloned.1.call-start = ((), (), s32[]{:S(2)}) async-start(), calls=%async_computation.6 | async-start | bytes 1966080 | tf_op jit(solution)/shard_map/reduce_scatter | solution.py:97
  342.3 28.2 %collective-permute-start.37 = (bf16[512,384]{1,0:T(8,128)(2,1)}, bf16[512,384]{1,0:T(8,128)(2,1)S(1)}, u32[]{:S(2)}, u32[]{:S(2)}) collective-permute-start(bf16[512,384]{1,0:T(8,128)(2,1)} %get-tuple-element.479), channel_id=1, source_target_pairs={{8,0},{9,1},{10,2},{11,3},{12,4},{13,5},{14,6},{15,7}} | collective-permute-start | bytes 1179656 | tf_op jit(solution)/shard_map/ppermute | solution.py:1159
  343.7 35.2 %collective-permute-start.38 = (bf16[512,384]{1,0:T(8,128)(2,1)}, bf16[512,384]{1,0:T(8,128)(2,1)S(1)}, u32[]{:S(2)}, u32[]{:S(2)}) collective-permute-start(bf16[512,384]{1,0:T(8,128)(2,1)} %get-tuple-element.480), channel_id=1, source_target_pairs={{8,0},{9,1},{10,2},{11,3},{12,4},{13,5},{14,6},{15,7}} | collective-permute-start | bytes 1179656 | tf_op jit(solution)/shard_map/ppermute | solution.py:1159
  379.0 41.3 %collective-permute-start.40 = (bf16[1024,384]{1,0:T(8,128)(2,1)}, bf16[1024,384]{1,0:T(8,128)(2,1)}, u32[]{:S(2)}, u32[]{:S(2)}) collective-permute-start(bf16[1024,384]{1,0:T(8,128)(2,1)} %get-tuple-element.486), channel_id=1, source_target_pairs={{8,0},{9,1},{10,2},{11,3},{12,4},{13,5},{14,6},{15,7}} | collective-permute-start | bytes 2359304 | tf_op jit(solution)/shard_map/ppermute | solution.py:1171
  380.2 40.0 %collective-permute-start.42 = (bf16[256,1536]{1,0:T(8,128)(2,1)}, bf16[256,1536]{1,0:T(8,128)(2,1)}, u32[]{:S(2)}, u32[]{:S(2)}) collective-permute-start(bf16[256,1536]{1,0:T(8,128)(2,1)} %add_rows.6), channel_id=1, source_target_pairs={{0,1},{1,0},{2,3},{3,2},{4,5},{5,4},{6,7},{7,6},{8,9},{9,8},{10,11... | collective-permute-start | bytes 2359304 | tf_op jit(solution)/shard_map/ppermute | solution.py:61
  381.9 29.7 %collective-permute-start.39 = (bf16[512,384]{1,0:T(8,128)(2,1)S(1)}, bf16[512,384]{1,0:T(8,128)(2,1)}, u32[]{:S(2)}, u32[]{:S(2)}) collective-permute-start(bf16[512,384]{1,0:T(8,128)(2,1)S(1)} %add_convert_fusion.2), channel_id=1, source_target_pairs={{0,2},{2,0},{1,3},{3,1},{4,6},{6,4},{5,7},{7,5},{8,10},{10,8},{9,1... | collective-permute-start | bytes 1179656 | tf_op jit(solution)/shard_map/ppermute | solution.py:61
  384.4 27.2 %collective-permute-start.41 = (bf16[256,384]{1,0:T(8,128)(2,1)S(1)}, bf16[256,384]{1,0:T(8,128)(2,1)}, u32[]{:S(2)}, u32[]{:S(2)}) collective-permute-start(bf16[256,384]{1,0:T(8,128)(2,1)S(1)} %constant_dynamic-slice_fusion.9), channel_id=1, source_target_pairs={{2,8},{3,9},{6,12},{7,13}} | collective-permute-start | bytes 589832 | tf_op jit(solution)/shard_map/ppermute | solution.py:1175
  483.2 32.5 %collective-permute-start.54 = (bf16[256,1536]{1,0:T(8,128)(2,1)}, bf16[256,1536]{1,0:T(8,128)(2,1)}, u32[]{:S(2)}, u32[]{:S(2)}) collective-permute-start(bf16[256,1536]{1,0:T(8,128)(2,1)} %add_rows.7), channel_id=1, source_target_pairs={{0,1},{1,0},{2,3},{3,2},{4,5},{5,4},{6,7},{7,6},{8,9},{9,8},{10,11... | collective-permute-start | bytes 2359304 | tf_op jit(solution)/shard_map/ppermute | solution.py:61
  483.2 30.3 %collective-permute-start.50 = (bf16[384,768]{1,0:T(8,128)(2,1)}, bf16[384,768]{1,0:T(8,128)(2,1)}, u32[]{:S(2)}, u32[]{:S(2)}) collective-permute-start(bf16[384,768]{1,0:T(8,128)(2,1)} %pad_maximum_fusion.3), channel_id=1, source_target_pairs={{0,2},{2,0},{1,3},{3,1},{4,6},{6,4},{5,7},{7,5},{8,10},{10,8},{9,1... | collective-permute-start | bytes 1769480 | tf_op jit(solution)/shard_map/ppermute | solution.py:61
  (135 other events, 1465.0 us)
Sparse Core Ops, SparseCore 0:
  53.6 87.6 all-gather.3
  143.7 47.1 all-gather.5
  193.4 46.2 all-gather.7
  303.0 120.0 reduce-scatter.2
  443.9 29.2 reduce-scatter.4
